TPU v7x, 32 devices: a whole 2x2x4 slice. The times are simulated.
32 devices in a mesh: sec: 4 (over y, core), dom: 8 (over z, x).
Axes of the slice: x: 2, y: 2, z: 4, core: 2. Of those that a mesh axis runs over, the one named last changes fastest.
Arguments:
- flow_state: bfloat16 [270, 32768], P(None, ('sec', 'dom')), may hold values from -6 to 6
- base_geometry: float32 [4, 32768], P(None, ('sec', 'dom')), may hold values from 0.5 to 2
- anchor_weight: float32 [32768], P(('sec', 'dom')), may hold values from 0 to 1.5
- wall_anchor: int32 [32768], P(('sec', 'dom')), may hold values from 0 to 32767
- face_nbr: int32 [6, 32768], P(None, ('sec', 'dom')), may hold values from 0 to 1151, as said below
- volume_ops: bfloat16 [4, 270, 270], replicated, may hold values from -0.375 to 0.375
- lift_ops: bfloat16 [6, 270, 90], replicated, may hold values from -0.625 to 0.625
- face_jac: bfloat16 [6, 2, 5, 5], replicated, may hold values from -2.5 to 2.5
- wall_load: float32 [3, 256, 128], P(None, ('sec', 'dom')), may hold values from -6 to 6
- wall_stiff: float32 [3, 256, 128], P(None, ('sec', 'dom')), may hold values from 0.01 to 0.3
Outputs:
- flow_residual: bfloat16 [270, 32768], P(None, ('sec', 'dom'))
- wall_disp: float32 [3, 256, 128], P(None, ('sec', 'dom'))
Inputs may be any that keep to these rules, and one draw needn't show every extreme that they name: `face_nbr`: for faces 0 to 3 a value v >= 1024 names element v - 1024 (below 128) of the device one step lower (faces 0 and 2) or higher (faces 1 and 3), cyclically, along dom (faces 0 and 1) or sec (faces 2 and 3); a smaller value names an element of the element's own device. Faces 4 and 5 always name an element of the own device.
All inputs are finite; a program needn't handle non-finite values.
Results may differ from a plain program's by a relative error of at most 0.0046.
Values may be sent and summed in bfloat16 or wider, within the bound.
No kernel may reach another device: no remote copies, remote signals or barrier semaphores. Data moves between devices by JAX's collectives and lax.ppermute only.
A program may use at most 320 MiB of HBM per device.

v0:
```python
import jax
import jax.numpy as jnp
from jax import lax
from jax.sharding import PartitionSpec as P

NV = 5
ITERS = 8


def shifted(x, axis, by):
    peers = lax.axis_size(axis)
    return lax.ppermute(x, axis, [(i, (i + by) % peers) for i in range(peers)])


def whole_operator(field, stiffness):
    padded = jnp.pad(field, ((0, 0), (1, 1), (1, 1)))
    beside = padded[:, 2:, 1:-1] + padded[:, :-2, 1:-1] + padded[:, 1:-1, 2:] + padded[:, 1:-1, :-2]
    return (4.0 + stiffness) * field - beside


def face_trace(values, face):
    shaped = values.reshape(NV, 2, 3, 3, 3, values.shape[1])
    picked = lax.index_in_dim(shaped, 0 if face % 2 == 0 else 2, 2 + face // 2, keepdims=False)
    return picked.reshape(NV * 18, values.shape[1])


def shift_dom(values, offset):
    return shifted(values, "dom", offset)


def shift_sec(values, offset):
    return shifted(values, "sec", offset)


def on_device(
    flow_state,
    base_geometry,
    anchor_weight,
    wall_anchor,
    face_nbr,
    volume_ops,
    lift_ops,
    face_jac,
    wall_load,
    wall_stiff,
):
    whole_load, whole_stiff = (
        lax.all_gather(wall_load, ("sec", "dom"), axis=1, tiled=True),
        lax.all_gather(wall_stiff, ("sec", "dom"), axis=1, tiled=True),
    )

    def iterate_whole(position, carry):
        whole_disp, resid, search, norm_now = carry
        image = whole_operator(search, whole_stiff)
        step_size = norm_now / jnp.sum(search * image)
        whole_disp = whole_disp + step_size * search
        resid = resid - step_size * image
        norm_next = jnp.sum(resid * resid)
        search = resid + norm_next / norm_now * search
        return (whole_disp, resid, search, norm_next)

    start_whole = (
        jnp.zeros_like(whole_load),
        whole_load,
        whole_load,
        jnp.sum(whole_load * whole_load),
    )
    whole_disp = lax.fori_loop(0, ITERS, iterate_whole, start_whole)[0]
    own_rows = wall_load.shape[1]
    first_row = lax.axis_index(("sec", "dom")) * own_rows
    wall_disp = lax.dynamic_slice_in_dim(whole_disp, first_row, own_rows, 1)
    flattened = whole_disp.reshape(3, whole_disp.shape[1] * whole_disp.shape[2])
    disp_at = jnp.take(flattened, wall_anchor, axis=1)
    geometry = jnp.concatenate(
        [base_geometry[:3] * jnp.exp(anchor_weight[None, :] * disp_at), base_geometry[3:]], axis=0
    )
    head_count = flow_state.shape[1] // 8
    head_block = flow_state[:, :head_count]
    remotes = [
        shift_dom(face_trace(head_block, 1), 1),
        shift_dom(face_trace(head_block, 0), -1),
        shift_sec(face_trace(head_block, 3), 1),
        shift_sec(face_trace(head_block, 2), -1),
    ]
    summed = jnp.zeros(flow_state.shape, jnp.float32)
    for direction in range(4):
        summed = summed + geometry[direction][None, :] * jnp.dot(
            volume_ops[direction], flow_state, preferred_element_type=jnp.float32
        )
    identity = jnp.eye(18, dtype=jnp.bfloat16)
    for face in range(6):
        own_trace = face_trace(flow_state, face)
        opposite = face_trace(flow_state, face ^ 1)
        if face < 4:
            candidates = jnp.concatenate([opposite, remotes[face]], axis=1)
        else:
            candidates = opposite
        neighbour_trace = jnp.take(candidates, face_nbr[face], axis=1)
        own_jac = jnp.kron(face_jac[face, 0], identity)
        other_jac = jnp.kron(face_jac[face, 1], identity)
        face_flux = geometry[face // 2][None, :] * (
            jnp.dot(own_jac, own_trace, preferred_element_type=jnp.float32)
            + jnp.dot(other_jac, neighbour_trace, preferred_element_type=jnp.float32)
        )
        face_flux = face_flux.astype(jnp.bfloat16)
        summed = summed + jnp.dot(lift_ops[face], face_flux, preferred_element_type=jnp.float32)
    return (summed.astype(jnp.bfloat16), wall_disp)


def solution(mesh):
    return jax.shard_map(
        on_device,
        mesh=mesh,
        in_specs=(
            P(None, ("sec", "dom")),
            P(None, ("sec", "dom")),
            P(("sec", "dom")),
            P(("sec", "dom")),
            P(None, ("sec", "dom")),
            P(),
            P(),
            P(),
            P(None, ("sec", "dom"), None),
            P(None, ("sec", "dom"), None),
        ),
        out_specs=(P(None, ("sec", "dom")), P(None, ("sec", "dom"), None)),
        check_vma=False,
    )
```

profile of v0, /device:TPU:0, one launch (start us, length us, event | category | flops | bytes accessed | tf_op | source)
XLA Modules:
  0.0 287.6 jit_solution(1124023343656779763)
XLA Ops:
  3.7 5.5 %collective-permute-start.1 = (bf16[90,128]{0,1:T(8,128)(2,1)}, bf16[90,128]{0,1:T(8,128)(2,1)}, u32[]{:S(2)}, u32[]{:S(2)}) collective-permute-start(bf16[90,128]{0,1:T(8,128)(2,1)} %copy.48), channel_id=1, source_target_pairs={{0,7},{1,0},{2,1},{3,2},{4,3},{5,4},{6,5},{7,6},{8,15},{9,8},{10,9... | collective-permute-start | bytes 69128 | tf_op jit(solution)/shard_map/ppermute | solution.py:12
  12.5 70.0 %all_gather.6 = f32[3,256,128]{2,1,0:T(8,128)S(1)} all-gather(f32[3,8,128]{2,1,0:T(8,128)S(1)} %copy-done.43), channel_id=1, replica_groups=mesh['sec'=4,'dom'=8] {'sec','dom'}, dimensions={1}, use_global_device_ids=true | all-gather | bytes 405504 | tf_op jit(solution)/shard_map/all_gather | solution.py:48
  91.0 2.5 slice_reduce_fusion.4
  100.3 65.8 %all_gather.7 = f32[3,256,128]{2,1,0:T(8,128)S(1)} all-gather(f32[3,8,128]{2,1,0:T(8,128)S(1)} %copy-done.44), channel_id=1, replica_groups=mesh['sec'=4,'dom'=8] {'sec','dom'}, dimensions={1}, use_global_device_ids=true | all-gather | bytes 405504 | tf_op jit(solution)/shard_map/all_gather | solution.py:49
  166.2 29.0 %while.19 = (s32[]{:T(128)}, f32[3,256,128]{2,1,0:T(8,128)S(1)}, f32[3,256,128]{2,1,0:T(8,128)S(1)}, f32[3,256,128]{2,1,0:T(8,128)S(1)}, f32[]{:T(128)}, /*index=5*/f32[3,256,128]{2,1,0:T(8,128)S(1)}, s32[]{:T(128)}, s32[]{:T(128)}) while((s32[]{:T(128)}, f32[3,256,128]{2,1,0:T(8,128)S(1)}, f32[3,256,128]{2,1,0:T(8,128)S(1)}, ...), condition=%wide.region_4.5_spmd.clone, body=%wide.region_1.4_spmd.clone.sunk | while | flops 1671171 | bytes 4325523 | solution.py:68
  195.2 8.8 %copy.36 = f32[3,256,128]{0,2,1:T(8,128)} copy(f32[3,256,128]{2,1,0:T(8,128)S(1)} %get-tuple-element.81) | data formatting | bytes 786432 | tf_op jit(solution)/shard_map/while | solution.py:68
  204.2 8.6 %gather_fusion = f32[1024,3]{1,0:T(8,128)S(1)} fusion(f32[3,32768]{0,1:T(8,128)} %bitcast.117, s32[1024]{0:T(1024)S(1)} %copy-done.41), kind=kCustom, calls=%fused_computation.6 | custom fusion | bytes 28672 | tf_op jit(solution)/shard_map/jit(_take)/gather | solution.py:73
  216.9 2.3 fusion.113
  220.2 1.7 mul.494
  228.6 4.3 %gather_fusion.6 = bf16[1024,90]{1,0:T(8,128)(2,1)} fusion(bf16[90,1024]{0,1:T(8,128)(2,1)S(1)} %copy.63, s32[1024]{0:T(1024)S(1)} %copy-done.40), kind=kCustom, calls=%fused_computation.5.clone | custom fusion | bytes 372736 | tf_op jit(solution)/shard_map/jit(_take)/gather | solution.py:98
  235.4 2.6 convolution_bitcast_fusion
  242.2 1.7 mul.466
  245.6 1.7 mul.447
  247.6 4.3 %gather_fusion.5 = bf16[1024,90]{1,0:T(8,128)(2,1)} fusion(bf16[90,1024]{0,1:T(8,128)(2,1)S(1)} %copy.60, s32[1024]{0:T(1024)S(1)} %copy-done.39), kind=kCustom, calls=%fused_computation.1.clone | custom fusion | bytes 372736 | tf_op jit(solution)/shard_map/jit(_take)/gather | solution.py:98
  254.4 4.3 %gather_fusion.3 = bf16[1024,90]{1,0:T(8,128)(2,1)} fusion(bf16[90,1152]{0,1:T(8,128)(2,1)S(1)} %pad_maximum_fusion.2, s32[1024]{0:T(1024)S(1)} %copy-done.36), kind=kCustom, calls=%fused_computation.3.clone | custom fusion | bytes 372736 | tf_op jit(solution)/shard_map/jit(_take)/gather | solution.py:98
  258.8 4.3 %gather_fusion.2 = bf16[1024,90]{1,0:T(8,128)(2,1)} fusion(bf16[90,1152]{0,1:T(8,128)(2,1)S(1)} %pad_maximum_fusion.1, s32[1024]{0:T(1024)S(1)} %copy-done.37), kind=kCustom, calls=%fused_computation.2.clone | custom fusion | bytes 372736 | tf_op jit(solution)/shard_map/jit(_take)/gather | solution.py:98
  263.1 3.2 %gather_fusion.1 = bf16[1024,90]{1,0:T(8,128)(2,1)S(1)} fusion(bf16[90,1152]{0,1:T(8,128)(2,1)S(1)} %pad_maximum_fusion, s32[1024]{0:T(1024)S(1)} %copy-done.38), kind=kCustom, calls=%fused_computation.clone | custom fusion | bytes 372736 | tf_op jit(solution)/shard_map/jit(_take)/gather | solution.py:98
  267.1 4.3 %gather_fusion.4 = bf16[1024,90]{1,0:T(8,128)(2,1)} fusion(bf16[90,1152]{0,1:T(8,128)(2,1)S(1)} %pad_maximum_fusion.3, s32[1024]{0:T(1024)S(1)} %copy-done.35), kind=kCustom, calls=%fused_computation.4.clone | custom fusion | bytes 372736 | tf_op jit(solution)/shard_map/jit(_take)/gather | solution.py:98
  271.5 1.7 convolution_bitcast_fusion.3
  273.2 2.5 convolution_bitcast_fusion.4
  275.8 2.6 convolution_bitcast_fusion.5
  278.4 2.5 convolution_bitcast_fusion.2
  281.0 3.6 %fusion.8 = f32[270,1024]{1,0:T(8,128)} fusion(f32[270,1024]{1,0:T(8,128)} %convolution_bitcast_fusion.2, f32[270,1024]{1,0:T(8,128)S(1)} %convolution_bitcast_fusion.3, f32[270,1024]{1,0:T(8,128)} %convolution_bitcast_fusion.4, f32[270,1024]{1,0:T(8,128)} %convolution_bitcast_fusion.5, f32[270,1024]{1,0:T(8,128)S(1)} %fusion.9, ...), kind=kOutput, calls=%fused_computation.31 | convolution fusion | flops 150958080 | bytes 7338376 | tf_op jit(solution)/shard_map/dot_general | solution.py:87
  284.6 3.0 %fusion.13 = bf16[270,1024]{1,0:T(8,128)(2,1)} fusion(f32[270,1024]{1,0:T(8,128)} %convolution_bitcast_fusion, f32[270,1024]{1,0:T(8,128)} %fusion.8, f32[90,1024]{1,0:T(8,128)S(1)} %copy-done.5, bf16[90,90]{1,0:T(8,128)(2,1)S(1)} %mul.485, bf16[1024,90]{1,0:T(8,128)(2,1)S(1)} %copy-done.15, pred[1024]{0:T(1024)(128)(4,1)S(1)} %copy-done.51, ...), kind=kOutput, calls=%fused_computation.39 | convolution fusion | flops 67553280 | bytes 3425096 | tf_op jit(solution)/shard_map/dot_general | solution.py:106
  (222 shorter events, 60.4 us)
Async XLA Ops:
  0.6 11.5 %copy-start = (bf16[270,1024]{1,0:T(8,128)(2,1)S(1)}, bf16[270,1024]{1,0:T(8,128)(2,1)}, u32[]{:S(2)}) copy-start(bf16[270,1024]{1,0:T(8,128)(2,1)} %param.16) | copy-start | bytes 1658884
  1.6 10.9 %copy-start.43 = (f32[3,8,128]{2,1,0:T(8,128)S(1)}, f32[3,8,128]{2,1,0:T(8,128)}, u32[]{:S(2)}) copy-start(f32[3,8,128]{2,1,0:T(8,128)} %param.24) | copy-start | bytes 36868
  2.4 249.5 %collective-permute-start.2 = (bf16[90,128]{0,1:T(8,128)(2,1)}, bf16[90,128]{0,1:T(8,128)(2,1)}, u32[]{:S(2)}, u32[]{:S(2)}) collective-permute-start(bf16[90,128]{0,1:T(8,128)(2,1)} %copy.52), channel_id=1, source_target_pairs={{0,8},{8,16},{16,24},{24,0},{1,9},{9,17},{17,25},{25,1},{2,10},{10... | collective-permute-start | bytes 69128 | tf_op jit(solution)/shard_map/ppermute | solution.py:12
  3.7 249.1 %collective-permute-start.1 = (bf16[90,128]{0,1:T(8,128)(2,1)}, bf16[90,128]{0,1:T(8,128)(2,1)}, u32[]{:S(2)}, u32[]{:S(2)}) collective-permute-start(bf16[90,128]{0,1:T(8,128)(2,1)} %copy.48), channel_id=1, source_target_pairs={{0,7},{1,0},{2,1},{3,2},{4,3},{5,4},{6,5},{7,6},{8,15},{9,8},{10,9... | collective-permute-start | bytes 69128 | tf_op jit(solution)/shard_map/ppermute | solution.py:12
  9.9 243.7 %collective-permute-start = (bf16[90,128]{0,1:T(8,128)(2,1)}, bf16[90,128]{0,1:T(8,128)(2,1)}, u32[]{:S(2)}, u32[]{:S(2)}) collective-permute-start(bf16[90,128]{0,1:T(8,128)(2,1)} %copy.44), channel_id=1, source_target_pairs={{0,1},{1,2},{2,3},{3,4},{4,5},{5,6},{6,7},{7,0},{8,9},{9,10},{10,1... | collective-permute-start | bytes 69128 | tf_op jit(solution)/shard_map/ppermute | solution.py:12
  10.7 255.6 %collective-permute-start.3 = (bf16[90,128]{0,1:T(8,128)(2,1)}, bf16[90,128]{0,1:T(8,128)(2,1)}, u32[]{:S(2)}, u32[]{:S(2)}) collective-permute-start(bf16[90,128]{0,1:T(8,128)(2,1)} %copy.56), channel_id=1, source_target_pairs={{0,24},{8,0},{16,8},{24,16},{1,25},{9,1},{17,9},{25,17},{2,26},{10... | collective-permute-start | bytes 69128 | tf_op jit(solution)/shard_map/ppermute | solution.py:12
  12.5 70.7 %copy-start.42 = (s32[1024]{0:T(1024)S(1)}, s32[1024]{0:T(1024)}, u32[]{:S(2)}) copy-start(s32[1024]{0:T(1024)} %param.19) | copy-start | bytes 12292
  12.5 71.9 %copy-start.33 = (s32[6,1024]{1,0:T(8,128)S(1)}, s32[6,1024]{1,0:T(8,128)}, u32[]{:S(2)}) copy-start(s32[6,1024]{1,0:T(8,128)} %param.20) | copy-start | bytes 73732
  86.6 9.3 %copy-start.2 = (bf16[6,2,5,5]{0,1,3,2:T(2,128)(2,1)S(1)}, bf16[6,2,5,5]{0,1,3,2:T(2,128)(2,1)}, u32[]{:S(2)}) copy-start(bf16[6,2,5,5]{0,1,3,2:T(2,128)(2,1)} %param.23) | copy-start | bytes 1804
  195.1 8.8 %copy-start.32 = (f32[4,1024]{1,0:T(4,128)S(1)}, f32[4,1024]{1,0:T(4,128)}, u32[]{:S(2)}) copy-start(f32[4,1024]{1,0:T(4,128)} %param.17) | copy-start | bytes 49156
  195.2 9.0 %copy-start.41 = (s32[1024]{0:T(1024)S(1)}, s32[1024]{0:T(1024)}, u32[]{:S(2)}) copy-start(s32[1024]{0:T(1024)} %fusion.93) | copy-start | bytes 12292
  195.2 17.6 %copy-start.45 = (f32[1024]{0:T(1024)S(1)}, f32[1024]{0:T(1024)}, u32[]{:S(2)}) copy-start(f32[1024]{0:T(1024)} %param.18) | copy-start | bytes 12292
  195.2 17.6 %copy-start.50 = (pred[1024]{0:T(1024)(128)(4,1)S(1)}, pred[1024]{0:T(1024)(128)(4,1)}, u32[]{:S(2)}) copy-start(pred[1024]{0:T(1024)(128)(4,1)} %compare_and_fusion.6) | copy-start | bytes 3076
  227.6 5.3 %copy-start.29 = (f32[1024]{0:T(1024)S(1)}, f32[1024]{0:T(1024)}, u32[]{:S(2)}) copy-start(f32[1024]{0:T(1024)} %get-tuple-element.107) | copy-start | bytes 12292
  239.6 7.8 %copy-start.16 = (bf16[5,18,5,18]{3,2,1,0:T(8,128)(2,1)S(1)}, bf16[5,18,5,18]{3,2,1,0:T(8,128)(2,1)}, u32[]{:S(2)}) copy-start(bf16[5,18,5,18]{3,2,1,0:T(8,128)(2,1)} %get-tuple-element.156) | copy-start | bytes 48604
  239.7 7.9 %copy-start.39 = (s32[1024]{0:T(1024)S(1)}, s32[1024]{0:T(1024)}, u32[]{:S(2)}) copy-start(s32[1024]{0:T(1024)} %fusion.98) | copy-start | bytes 12292
  240.5 6.7 %copy-start.17 = (bf16[5,18,5,18]{3,2,1,0:T(8,128)(2,1)S(1)}, bf16[5,18,5,18]{3,2,1,0:T(8,128)(2,1)}, u32[]{:S(2)}) copy-start(bf16[5,18,5,18]{3,2,1,0:T(8,128)(2,1)} %get-tuple-element.163) | copy-start | bytes 48604
  247.6 5.2 %copy-start.7 = (bf16[90,1024]{0,1:T(8,128)(2,1)S(1)}, bf16[90,1024]{0,1:T(8,128)(2,1)}, u32[]{:S(2)}) copy-start(bf16[90,1024]{0,1:T(8,128)(2,1)} %copy.49) | copy-start | bytes 552964
  247.6 6.0 %copy-start.6 = (bf16[90,1024]{0,1:T(8,128)(2,1)S(1)}, bf16[90,1024]{0,1:T(8,128)(2,1)}, u32[]{:S(2)}) copy-start(bf16[90,1024]{0,1:T(8,128)(2,1)} %copy.45) | copy-start | bytes 552964
  253.6 5.2 %copy-start.37 = (s32[1024]{0:T(1024)S(1)}, s32[1024]{0:T(1024)}, u32[]{:S(2)}) copy-start(s32[1024]{0:T(1024)} %fusion.95) | copy-start | bytes 12292
  258.8 4.3 %copy-start.38 = (s32[1024]{0:T(1024)S(1)}, s32[1024]{0:T(1024)}, u32[]{:S(2)}) copy-start(s32[1024]{0:T(1024)} %fusion.94) | copy-start | bytes 12292
  263.1 4.1 %copy-start.35 = (s32[1024]{0:T(1024)S(1)}, s32[1024]{0:T(1024)}, u32[]{:S(2)}) copy-start(s32[1024]{0:T(1024)} %fusion.97) | copy-start | bytes 12292
  266.3 5.2 %copy-start.25 = (bf16[90,90]{1,0:T(8,128)(2,1)S(1)}, bf16[90,90]{1,0:T(8,128)(2,1)}, u32[]{:S(2)}) copy-start(bf16[90,90]{1,0:T(8,128)(2,1)} %mul.466) | copy-start | bytes 48604
  266.3 5.2 %copy-start.47 = (pred[1024]{0:T(1024)(128)(4,1)S(1)}, pred[1024]{0:T(1024)(128)(4,1)}, u32[]{:S(2)}) copy-start(pred[1024]{0:T(1024)(128)(4,1)} %compare_and_fusion.3) | copy-start | bytes 3076
  (32 other events, 77.3 us)
where the time goes:
time: 289 us; the launch traced here: 288 us
  blocking collectives  136 us (47%)
  local copies, waits for them, and re-layouts  73.4 us (25%)
  other arithmetic  29 us (10%)
  matrix products  26.8 us (9%)
  loops' own time  13.9 us (5%)
  starting transfers between devices  7.44 us (3%)
    all_gather x1, blocking collectives, on_device(): lax.all_gather(wall_load, ('sec', 'dom'), axis=1, tiled=True)  70 us
    all_gather x1, blocking collectives, on_device(): lax.all_gather(wall_stiff, ('sec', 'dom'), axis=1, tiled=True)  65.8 us
    gather x6, local copies, waits for them, and re-layouts, on_device(): neighbour_trace = jnp.take(candidates, face_nbr[face], axis=1)  24.8 us
    dot_general x6, matrix products, on_device(): jnp.dot(lift_ops[face], face_flux, preferred_element_type=jnp.float32)  15 us
    another operation x1, loops' own time, on_device(): whole_disp = lax.fori_loop(0, ITERS, iterate_whole, start_whole)[0]  13.9 us
    while x1, local copies, waits for them, and re-layouts, on_device(): whole_disp = lax.fori_loop(0, ITERS, iterate_whole, start_whole)[0]  8.76 us
    gather x1, local copies, waits for them, and re-layouts, on_device(): disp_at = jnp.take(flattened, wall_anchor, axis=1)  8.57 us
    ppermute x4, starting transfers between devices, shifted(): return lax.ppermute(x, axis, [(i, (i + by) % peers) for i in range(peers)])  7.44 us
  transfers between devices with their start and end apart: 4, of which 0 were waited for; matrix products, arithmetic and copies ran while one was open for 37% of the time, Pallas kernels for 0%

commit v1 on v0

v1 whole, which is shorter than its diff:
```python
import functools

import jax
import jax.numpy as jnp
import numpy as np
from jax import lax
from jax.experimental import pallas as pl
from jax.experimental.pallas import tpu as pltpu
from jax.sharding import PartitionSpec as P

NV = 5
ITERS = 8
NODES = 18
SLOT = 96
TILE = 8
WIDE = 256
BOTH = ("sec", "dom")


def face_rows(face):
    rows = np.arange(NV * 54).reshape(NV * 2, 3, 3, 3)
    return np.take(rows, 0 if face % 2 == 0 else 2, axis=1 + face // 2).reshape(-1)


def picker(faces, unknowns):
    picks = np.zeros((len(faces) * SLOT, unknowns), np.float32)
    for slot, face in enumerate(faces):
        rows = face_rows(face)
        picks[slot * SLOT + np.arange(rows.size), rows] = 1
    return jnp.asarray(picks, jnp.bfloat16)


def kron_parts(sides):
    row = np.arange(SLOT)
    valid = row < NV * NODES
    variable, node = row // NODES, row % NODES
    left = np.zeros((SLOT, NV), np.float32)
    left[row[valid], variable[valid]] = 1
    right = np.zeros((sides * NV, sides * SLOT), np.float32)
    for side in range(sides):
        right[side * NV + variable[valid], side * SLOT + row[valid]] = 1
    same = (node[:, None] == node[None, :]) & valid[:, None] & valid[None, :]
    return (
        jnp.asarray(left, jnp.bfloat16),
        jnp.asarray(right, jnp.bfloat16),
        jnp.asarray(np.concatenate([same, same], axis=1), jnp.float32),
    )


def dot(a, b):
    return jnp.dot(a, b, preferred_element_type=jnp.float32)


def head_kernel(state_ref, picks_ref, *out_refs):
    head = state_ref[...]
    for slot, out_ref in enumerate(out_refs):
        out_ref[...] = dot(picks_ref[slot * SLOT : (slot + 1) * SLOT, :], head).astype(jnp.bfloat16)


def head_traces(flow_state, head_count):
    unknowns = flow_state.shape[0]
    faces = (1, 0, 3, 2)
    return pl.pallas_call(
        head_kernel,
        grid=(1,),
        in_specs=[
            pl.BlockSpec((unknowns, head_count), lambda i: (0, 0)),
            pl.BlockSpec((len(faces) * SLOT, unknowns), lambda i: (0, 0)),
        ],
        out_specs=[pl.BlockSpec((SLOT, head_count), lambda i: (0, 0))] * len(faces),
        out_shape=[jax.ShapeDtypeStruct((SLOT, head_count), jnp.bfloat16)] * len(faces),
        name="head_traces",
    )(flow_state, picker(faces, unknowns))


def flow_kernel(
    state_ref, nbr_ref, from0, from1, from2, from3, weights_ref, jac_ref, picks_ref, left_ref, right_ref, same_ref,
    out_ref, trace_ref, flux_mat_ref, gathered_ref,
):
    step = pl.program_id(0)
    chunks = state_ref.shape[1] // WIDE
    remotes = (from0, from1, from2, from3)

    @pl.when(step == 0)
    def _():
        def traces(chunk, carry):
            cols = pl.ds(pl.multiple_of(chunk * WIDE, WIDE), WIDE)
            trace_ref[:, cols] = dot(picks_ref[...], state_ref[:, cols]).astype(jnp.bfloat16)
            return carry

        lax.fori_loop(0, chunks, traces, 0)
        spread = dot(left_ref[...], jac_ref[...]).astype(jnp.bfloat16)
        spread = dot(spread, right_ref[...])
        for face in range(6):
            both = spread[:, face * 2 * SLOT : (face + 1) * 2 * SLOT]
            flux_mat_ref[face] = (both * same_ref[...]).astype(jnp.bfloat16)

    here = pl.ds(pl.multiple_of(step * WIDE, WIDE), WIDE)
    lane = lax.broadcasted_iota(jnp.int32, (WIDE, WIDE), 0)
    fluxes = []
    for face in range(6):
        index = nbr_ref[face : face + 1, :]
        part = index // WIDE
        pick = jnp.where(lane == index - part * WIDE, 1.0, 0.0).astype(jnp.bfloat16)
        opposite = (face ^ 1) * SLOT
        found = jnp.zeros((SLOT, WIDE), jnp.float32)
        for chunk in range(chunks):
            source = trace_ref[opposite : opposite + SLOT, chunk * WIDE : (chunk + 1) * WIDE]
            found = jnp.where(part == chunk, dot(source, pick), found)
        if face < 4:
            source = remotes[face][...]
            found = jnp.where(part == chunks, dot(source, pick[: source.shape[1], :]), found)
        gathered_ref[:SLOT, :] = trace_ref[face * SLOT : (face + 1) * SLOT, here]
        gathered_ref[SLOT:, :] = found.astype(jnp.bfloat16)
        fluxes.append(dot(flux_mat_ref[face], gathered_ref[...]).astype(jnp.bfloat16))
    own = state_ref[:, here]
    for direction in range(4):
        if direction < 3:
            operand = jnp.concatenate([fluxes[2 * direction], fluxes[2 * direction + 1], own], axis=0)
            out_ref[direction] = dot(weights_ref[direction], operand)
        else:
            out_ref[direction] = dot(weights_ref[direction, :, 2 * SLOT :], own)


def flow_parts(flow_state, face_nbr, remotes, weights, jac):
    unknowns, count = flow_state.shape
    head_count = remotes[0].shape[1]
    picks = picker(range(6), unknowns)
    left, right, same = kron_parts(12)

    def whole(array):
        return pl.BlockSpec(array.shape, lambda i: (0,) * array.ndim)

    args = (flow_state, face_nbr, *remotes, weights, jac, picks, left, right, same)
    specs = [whole(a) for a in args]
    specs[1] = pl.BlockSpec((6, WIDE), lambda i: (0, i))
    return pl.pallas_call(
        flow_kernel,
        grid=(count // WIDE,),
        in_specs=specs,
        out_specs=pl.BlockSpec((4, unknowns, WIDE), lambda i: (0, 0, i)),
        out_shape=jax.ShapeDtypeStruct((4, unknowns, count), jnp.float32),
        scratch_shapes=[
            pltpu.VMEM((6 * SLOT, count), jnp.bfloat16),
            pltpu.VMEM((6, SLOT, 2 * SLOT), jnp.bfloat16),
            pltpu.VMEM((2 * SLOT, WIDE), jnp.bfloat16),
        ],
        compiler_params=pltpu.CompilerParams(vmem_limit_bytes=24 << 20),
        cost_estimate=pl.CostEstimate(flops=4 << 30, bytes_accessed=8 << 20, transcendentals=0),
        name="flow_parts",
    )(*args)


def total(tile):
    return jnp.sum(jnp.sum(tile, axis=0, keepdims=True), axis=1, keepdims=True)


def wall_kernel(
    masks, rows, own_rows,
    near_ref, far_ref, base_ref, follow_ref, anchor_ref, parts_hbm, residual_ref, disp_ref,
    disp, resid, search, image, diag, parts_ref, copy_sem,
):
    comps = 3
    tiles = rows // TILE
    me = lax.axis_index(BOTH)
    fetch = pltpu.make_async_copy(parts_hbm, parts_ref, copy_sem)
    fetch.start()

    def strided(block):
        first = block * TILE
        return pl.ds((first % tiles) * TILE + first // tiles, TILE, stride=TILE)

    half = near_ref.shape[0]
    for slot in range(2 * half):
        ref, at = (near_ref, slot) if slot < half else (far_ref, slot - half)
        device = jnp.bitwise_xor(me, masks[slot])
        for block in range(own_rows // TILE):
            to = strided(device * (own_rows // TILE) + block)
            for c in range(comps):
                first = c * own_rows + block * TILE
                resid[c, to, :] = ref[at, first : first + TILE, :]
                first += comps * own_rows
                diag[c, to, :] = 4.0 + ref[at, first : first + TILE, :]

    lane = lax.broadcasted_iota(jnp.int32, (TILE, 128), 1)
    sub = lax.broadcasted_iota(jnp.int32, (TILE, 128), 0)
    group = 32 if tiles % 32 == 0 else 8
    zero = jnp.zeros((TILE, 128), jnp.float32)

    def at(tile):
        return pl.ds(pl.multiple_of(tile * TILE, TILE), TILE)

    def each_tile(body, carry):
        for c in range(comps):
            def some(chunk, carry, c=c):
                for k in range(group):
                    carry = body(c, chunk * group + k, carry)
                return carry

            if tiles == group:
                carry = some(0, carry)
            else:
                carry = lax.fori_loop(0, tiles // group, some, carry)
        return carry

    def load(c, tile, acc):
        value = resid[c, at(tile), :]
        search[c, at(tile + 1), :] = value
        disp[c, at(tile), :] = zero
        return acc + value * value

    norm = total(each_tile(load, zero))

    def iterate(position, norm_now):
        for c in range(comps):
            last = search[c, at(tiles), :]
            search[c, at(0), :] = jnp.where(sub == 0, 0.0, pltpu.roll(last, 1, 0))
            first = search[c, at(1), :]
            search[c, at(tiles + 1), :] = jnp.where(sub == TILE - 1, 0.0, pltpu.roll(first, TILE - 1, 0))

        def apply(c, tile, acc):
            value = search[c, at(tile + 1), :]
            beside = search[c, at(tile), :] + search[c, at(tile + 2), :]
            beside += jnp.where(lane == 0, 0.0, pltpu.roll(value, 1, 1))
            beside += jnp.where(lane == 127, 0.0, pltpu.roll(value, 127, 1))
            result = diag[c, at(tile), :] * value - beside
            image[c, at(tile), :] = result
            return acc + value * result

        step_size = norm_now / total(each_tile(apply, zero))

        def move(c, tile, acc):
            disp[c, at(tile), :] += step_size * search[c, at(tile + 1), :]
            value = resid[c, at(tile), :] - step_size * image[c, at(tile), :]
            resid[c, at(tile), :] = value
            return acc + value * value

        norm_next = total(each_tile(move, zero))
        ratio = norm_next / norm_now

        def turn(c, tile, acc):
            search[c, at(tile + 1), :] = resid[c, at(tile), :] + ratio * search[c, at(tile + 1), :]
            return acc

        each_tile(turn, 0)
        return norm_next

    lax.fori_loop(0, ITERS, iterate, norm)

    for block in range(own_rows // TILE):
        for c in range(comps):
            disp_ref[c, block * TILE : (block + 1) * TILE, :] = disp[c, strided(me * (own_rows // TILE) + block), :]

    anchor = anchor_ref[...]
    count = anchor.shape[1]
    row = anchor // 128
    column = anchor - row * 128
    upper = row // tiles
    place = (row - upper * tiles) * TILE + upper
    pick = jnp.where(lax.broadcasted_iota(jnp.int32, (128, count), 0) == column, 1.0, 0.0).astype(jnp.bfloat16)
    pick = jnp.concatenate([pick, pick], axis=0)
    some_rows = 128
    row_of = lax.broadcasted_iota(jnp.int32, (some_rows, count), 0)

    def look(chunk, sums):
        first = pl.multiple_of(chunk * some_rows, some_rows)
        hit = row_of == place - first
        out = []
        for c in range(comps):
            value = disp[c, pl.ds(first, some_rows), :]
            coarse = value.astype(jnp.bfloat16)
            fine = (value - coarse.astype(jnp.float32)).astype(jnp.bfloat16)
            found = dot(jnp.concatenate([coarse, fine], axis=1), pick)
            found = jnp.where(hit, found, 0.0).reshape(some_rows // TILE, TILE, count)
            out.append(sums[c] + jnp.sum(found, axis=0))
        return tuple(out)

    sums = lax.fori_loop(0, rows // some_rows, look, (jnp.zeros((TILE, count), jnp.float32),) * comps)
    follow = follow_ref[...]
    geometry = [
        base_ref[c : c + 1, :] * jnp.exp(follow * jnp.sum(sums[c], axis=0, keepdims=True)) for c in range(comps)
    ]
    geometry.append(base_ref[comps : comps + 1, :])
    fetch.wait()
    unknowns = residual_ref.shape[0]
    for first in range(0, unknowns, 16):
        some = slice(first, min(first + 16, unknowns))
        value = geometry[0] * parts_ref[0, some, :]
        for direction in range(1, 4):
            value += geometry[direction] * parts_ref[direction, some, :]
        residual_ref[some, :] = value.astype(jnp.bfloat16)


def wall_and_residual(near, far, masks, base_geometry, anchor_weight, wall_anchor, parts, own_rows):
    rows = own_rows * 2 * near.shape[0]
    _, unknowns, count = parts.shape
    field = pltpu.VMEM((3, rows, 128), jnp.float32)
    vmem = pl.BlockSpec(memory_space=pltpu.VMEM)
    return pl.pallas_call(
        functools.partial(wall_kernel, masks, rows, own_rows),
        in_specs=[vmem, vmem, vmem, vmem, vmem, pl.BlockSpec(memory_space=pl.ANY)],
        out_specs=[vmem, vmem],
        out_shape=[
            jax.ShapeDtypeStruct((unknowns, count), jnp.bfloat16),
            jax.ShapeDtypeStruct((3, own_rows, 128), jnp.float32),
        ],
        scratch_shapes=[
            field,
            field,
            pltpu.VMEM((3, rows + 2 * TILE, 128), jnp.float32),
            field,
            field,
            pltpu.VMEM(parts.shape, jnp.float32),
            pltpu.SemaphoreType.DMA,
        ],
        compiler_params=pltpu.CompilerParams(vmem_limit_bytes=(16 << 20) + 16 * rows * 3 * 128 * 4),
        cost_estimate=pl.CostEstimate(flops=1 << 30, bytes_accessed=8 << 20, transcendentals=0),
        name="wall_and_residual",
    )(near, far, base_geometry, anchor_weight[None, :], wall_anchor[None, :], parts)


def shifted(x, axis, by):
    peers = lax.axis_size(axis)
    return lax.ppermute(x, axis, [(i, (i + by) % peers) for i in range(peers)])


def gather_stages(mesh):
    def bits(axis):
        assert mesh.shape[axis] & (mesh.shape[axis] - 1) == 0
        return [(axis, 1 << b) for b in reversed(range(mesh.shape[axis].bit_length() - 1))]

    return bits("dom") + bits("sec")


def on_device(
    stages, n_dom,
    flow_state, base_geometry, anchor_weight, wall_anchor, face_nbr, volume_ops, lift_ops, face_jac, wall_load, wall_stiff,
):
    own_rows, width = wall_load.shape[1:]
    wall = jnp.concatenate([wall_load, wall_stiff], axis=0).reshape(1, 6 * own_rows, width)
    masks = [0]
    far = wall
    for position, (axis, bit) in enumerate(stages):
        if position > 0:
            wall = jnp.concatenate([wall, far], axis=0)
        far = lax.ppermute(wall, axis, [(i, i ^ bit) for i in range(lax.axis_size(axis))])
        masks += [m ^ (bit * n_dom if axis == "sec" else bit) for m in masks]

    head_count = flow_state.shape[1] // 8
    heads = head_traces(flow_state, head_count)
    remotes = [
        shifted(heads[0], "dom", 1),
        shifted(heads[1], "dom", -1),
        shifted(heads[2], "sec", 1),
        shifted(heads[3], "sec", -1),
    ]
    lifts = jnp.pad(lift_ops, ((0, 2), (0, 0), (0, SLOT - lift_ops.shape[2])))
    weights = jnp.concatenate([lifts[0::2], lifts[1::2], volume_ops], axis=2)
    jac = face_jac.transpose(2, 0, 1, 3).reshape(NV, 12 * NV)
    parts = flow_parts(flow_state, face_nbr, remotes, weights, jac)
    return wall_and_residual(wall, far, masks, base_geometry, anchor_weight, wall_anchor, parts, own_rows)


def solution(mesh):
    return jax.shard_map(
        functools.partial(on_device, gather_stages(mesh), mesh.shape["dom"]),
        mesh=mesh,
        in_specs=(
            P(None, BOTH),
            P(None, BOTH),
            P(BOTH),
            P(BOTH),
            P(None, BOTH),
            P(),
            P(),
            P(),
            P(None, BOTH, None),
            P(None, BOTH, None),
        ),
        out_specs=(P(None, BOTH), P(None, BOTH, None)),
        check_vma=False,
    )
```

time: 289 us -> 47.7 us (0.17)
  blocking collectives: 136 us -> 0 us
  local copies, waits for them, and re-layouts: 73.4 us -> 1.61 us
  other arithmetic: 29 us -> 1.47 us
  matrix products: 26.8 us -> 0 us
  Pallas kernels: 0 us -> 18.6 us
  loops' own time: 13.9 us -> 0 us
  waiting for transfers between devices: 0.01 us -> 12.5 us
  starting transfers between devices: 7.44 us -> 12.3 us
    all_gather x2 -> x0, blocking collectives: 136 us -> none  [the longest x1 70 us: on_device(): lax.all_gather(wall_load, ('sec', 'dom'), axis=1, tiled=True)]
    gather x7 -> x0, local copies, waits for them, and re-layouts: 33.4 us -> none  [the longest x6 24.8 us: on_device(): neighbour_trace = jnp.take(candidates, face_nbr[face], axis=1)]
    dot_general x16 -> x0, matrix products: 26.8 us -> none  [the longest x6 15 us: on_device(): jnp.dot(lift_ops[face], face_flux, preferred_element_type=jnp.float32)]
    pallas_call x0 -> x3, Pallas kernels: none -> 18.6 us  [the longest x1 8.95 us: flow_parts(): pl.pallas_call(flow_kernel, grid=(count // WIDE,), in_specs=specs, out_sp...]
    another operation x1 -> x0, loops' own time: 13.9 us -> none  [on_device(): whole_disp = lax.fori_loop(0, ITERS, iterate_whole, start_whole)[0]]
    reduce_sum x17 -> x0, other arithmetic: 13.7 us -> none  [the longest x8 6.75 us: iterate_whole(): step_size = norm_now / jnp.sum(search * image)]
    ppermute x0 -> x5, waiting for transfers between devices: none -> 12.5 us  [on_device(): lax.ppermute(wall, axis, [(i, i ^ bit) for i in range(lax.axis_size(axis))])]
    mul x12 -> x0, local copies, waits for them, and re-layouts: 10.6 us -> none  [the longest x6 7.03 us: on_device(): other_jac = jnp.kron(face_jac[face, 1], identity)]
  transfers between devices with their start and end apart: 4 -> 9, of which waited for: 0 -> 3; matrix products, arithmetic and copies ran while one was open for 37% -> 5% of each run, Pallas kernels for 0% -> 23%
where the time goes in v1:
time: 47.7 us; the launch traced here: 47.4 us
  Pallas kernels  18.6 us (39%)
  waiting for transfers between devices  12.5 us (26%)
  starting transfers between devices  12.3 us (26%)
  local copies, waits for them, and re-layouts  1.61 us (3%)
  other arithmetic  1.47 us (3%)
  between operations  0.96 us (2%)
    ppermute x5, waiting for transfers between devices, on_device(): lax.ppermute(wall, axis, [(i, i ^ bit) for i in range(lax.axis_size(axis))])  12.5 us
    pallas_call x1, Pallas kernels, flow_parts(): pl.pallas_call(flow_kernel, grid=(count // WIDE,), in_specs=specs, out_sp...  8.95 us
    pallas_call x1, Pallas kernels, wall_and_residual(): pl.pallas_call(functools.partial(wall_kernel, masks, rows, own_rows), in_...  7.8 us
    ppermute x4, starting transfers between devices, shifted(): return lax.ppermute(x, axis, [(i, (i + by) % peers) for i in range(peers)])  6.47 us
    ppermute x5, starting transfers between devices, on_device(): lax.ppermute(wall, axis, [(i, i ^ bit) for i in range(lax.axis_size(axis))])  5.83 us
    pallas_call x1, Pallas kernels, head_traces(): pl.pallas_call(head_kernel, grid=(1,), in_specs=[pl.BlockSpec((unknowns,...  1.81 us
    slice x1, local copies, waits for them, and re-layouts, on_device(): weights = jnp.concatenate([lifts[0::2], lifts[1::2], volume_ops], axis=2)  1.13 us
  transfers between devices with their start and end apart: 9, of which 3 were waited for; matrix products, arithmetic and copies ran while one was open for 5% of the time, Pallas kernels for 23%

profile of v1, /device:TPU:0, one launch (start us, length us, event | category | flops | bytes accessed | tf_op | source)
XLA Modules:
  0.0 47.4 jit_solution(3272191391568852432)
XLA Ops:
  0.6 0.8 %maximum_bitcast_fusion = f32[1,48,128]{2,1,0:T(8,128)S(1)} fusion(f32[3,8,128]{2,1,0:T(8,128)} %param.24, f32[3,8,128]{2,1,0:T(8,128)} %param.23), kind=kLoop, calls=%fused_computation.6 | loop fusion | flops 6144 | bytes 49152 | tf_op jit(solution)/shard_map/reshape | solution.py:340
  1.4 4.0 %collective-permute-start = (f32[1,48,128]{2,1,0:T(8,128)S(1)}, f32[1,48,128]{2,1,0:T(8,128)S(1)}, u32[]{:S(2)}, u32[]{:S(2)}) collective-permute-start(f32[1,48,128]{2,1,0:T(8,128)S(1)} %maximum_bitcast_fusion), channel_id=1, source_target_pairs={{0,4},{1,5},{2,6},{3,7},{4,0},{5,1},{6,2},{7,3},{8,12},{9,13},{10,... | collective-permute-start | bytes 73736 | tf_op jit(solution)/shard_map/ppermute | solution.py:346
  5.5 1.8 %head_traces.1 = (bf16[96,128]{1,0:T(8,128)(2,1)}, bf16[96,128]{1,0:T(8,128)(2,1)}, bf16[96,128]{1,0:T(8,128)(2,1)}, bf16[96,128]{1,0:T(8,128)(2,1)}) custom-call(bf16[270,1024]{1,0:T(8,128)(2,1)} %state_ref.3, bf16[384,270]{1,0:T(8,128)(2,1)} %constant.13.clone.picks_ref), custom_call_target="tpu_custom_call" | custom-call | tf_op jit(solution)/shard_map/head_traces/pallas_call | solution.py:63
  7.3 1.5 %collective-permute-start.5 = (bf16[96,128]{1,0:T(8,128)(2,1)}, bf16[96,128]{1,0:T(8,128)(2,1)S(1)}, u32[]{:S(2)}, u32[]{:S(2)}) collective-permute-start(bf16[96,128]{1,0:T(8,128)(2,1)} %get-tuple-element.6), channel_id=1, source_target_pairs={{0,1},{1,2},{2,3},{3,4},{4,5},{5,6},{6,7},{7,0},{8,9},{9,10},{10,1... | collective-permute-start | bytes 73736 | tf_op jit(solution)/shard_map/ppermute | solution.py:324
  8.8 3.2 %collective-permute-start.6 = (bf16[96,128]{1,0:T(8,128)(2,1)}, bf16[96,128]{1,0:T(8,128)(2,1)S(1)}, u32[]{:S(2)}, u32[]{:S(2)}) collective-permute-start(bf16[96,128]{1,0:T(8,128)(2,1)} %get-tuple-element.7), channel_id=1, source_target_pairs={{0,7},{1,0},{2,1},{3,2},{4,3},{5,4},{6,5},{7,6},{8,15},{9,8},{10,9... | collective-permute-start | bytes 73736 | tf_op jit(solution)/shard_map/ppermute | solution.py:324
  12.0 1.7 %collective-permute-start.8 = (bf16[96,128]{1,0:T(8,128)(2,1)}, bf16[96,128]{1,0:T(8,128)(2,1)S(1)}, u32[]{:S(2)}, u32[]{:S(2)}) collective-permute-start(bf16[96,128]{1,0:T(8,128)(2,1)} %get-tuple-element.9), channel_id=1, source_target_pairs={{0,24},{8,0},{16,8},{24,16},{1,25},{9,1},{17,9},{25,17},{2,26},{10... | collective-permute-start | bytes 73736 | tf_op jit(solution)/shard_map/ppermute | solution.py:324
  13.8 1.1 %pad_slice_fusion.1 = (bf16[4,270,96]{2,1,0:T(8,128)(2,1)S(1)}, bf16[4,270,96]{2,1,0:T(8,128)(2,1)S(1)}) fusion(bf16[6,270,90]{2,1,0:T(8,128)(2,1)} %param.21), kind=kLoop, calls=%fused_computation.2 | loop fusion | bytes 706320 | tf_op jit(solution)/shard_map/slice | solution.py:358
  14.9 0.1 copy.19
  15.1 0.0 copy-start.5
  15.1 0.0 copy-start.6
  15.1 0.0 copy-start.7
  15.1 0.0 copy-start.8
  15.1 0.6 %pad_maximum_fusion.weights_ref = bf16[4,270,462]{2,1,0:T(8,128)(2,1)S(1)} fusion(bf16[4,270,270]{2,1,0:T(8,128)(2,1)S(1)} %copy.19, bf16[4,270,96]{2,1,0:T(8,128)(2,1)S(1)} %get-tuple-element.11, bf16[4,270,96]{2,1,0:T(8,128)(2,1)S(1)} %get-tuple-element.10), kind=kLoop, calls=%fused_computation | loop fusion | flops 2993760 | bytes 1995840 | tf_op jit(solution)/shard_map/concatenate | solution.py:358
  15.8 0.1 collective-permute-start.1
  15.9 0.2 copy.20
  16.1 0.1 reshape.11.jac_ref
  16.2 3.8 %collective-permute-done.1 = f32[2,48,128]{2,1,0:T(8,128)S(1)} collective-permute-done((f32[2,48,128]{2,1,0:T(8,128)S(1)}, f32[2,48,128]{2,1,0:T(8,128)S(1)}, u32[]{:S(2)}, u32[]{:S(2)}) %collective-permute-start.1) | collective-permute-done | bytes 49184 | tf_op jit(solution)/shard_map/ppermute | solution.py:346
  19.9 0.1 collective-permute-start.2
  20.0 4.6 %collective-permute-done.2 = f32[4,48,128]{2,1,0:T(8,128)S(1)} collective-permute-done((f32[4,48,128]{2,1,0:T(8,128)S(1)}, f32[4,48,128]{2,1,0:T(8,128)S(1)}, u32[]{:S(2)}, u32[]{:S(2)}) %collective-permute-start.2) | collective-permute-done | bytes 98336 | tf_op jit(solution)/shard_map/ppermute | solution.py:346
  24.6 1.6 %collective-permute-start.3 = (f32[8,48,128]{2,1,0:T(8,128)S(1)}, f32[8,48,128]{2,1,0:T(8,128)S(1)}, u32[]{:S(2)}, u32[]{:S(2)}) collective-permute-start(f32[8,48,128]{2,1,0:T(8,128)S(1)} %pad_maximum_fusion.1), channel_id=1, source_target_pairs={{0,16},{8,24},{16,0},{24,8},{1,17},{9,25},{17,1},{25,9},{2,18},{10... | collective-permute-start | bytes 589832 | tf_op jit(solution)/shard_map/ppermute | solution.py:346
  26.2 4.1 %collective-permute-done.3 = f32[8,48,128]{2,1,0:T(8,128)S(1)} collective-permute-done((f32[8,48,128]{2,1,0:T(8,128)S(1)}, f32[8,48,128]{2,1,0:T(8,128)S(1)}, u32[]{:S(2)}, u32[]{:S(2)}) %collective-permute-start.3) | collective-permute-done | bytes 196640 | tf_op jit(solution)/shard_map/ppermute | solution.py:346
  30.4 0.1 collective-permute-start.4
  30.6 9.0 %flow_parts.1.parts_hbm = f32[4,270,1024]{2,1,0:T(8,128)S(1)} custom-call(bf16[270,1024]{1,0:T(8,128)(2,1)S(1)} %copy-done, s32[6,1024]{1,0:T(8,128)S(1)} %copy-done.4, bf16[96,128]{1,0:T(8,128)(2,1)S(1)} %collective-permute-done.5.from0, bf16[96,128]{1,0:T(8,128)(2,1)S(1)} %collective-permute-done.6.from1, ...), custom_call_target="tpu_custom_call" | custom-call | flops 4294967296 | bytes 8388608 | tf_op jit(solution)/shard_map/flow_parts/pallas_call | solution.py:137
  39.6 7.8 %wall_and_residual.1 = (bf16[270,1024]{1,0:T(8,128)(2,1)}, f32[3,8,128]{2,1,0:T(8,128)}) custom-call(f32[16,48,128]{2,1,0:T(8,128)S(1)} %constant_dynamic-update-slice_fusion.near_ref, f32[16,48,128]{2,1,0:T(8,128)S(1)} %collective-permute-done.4.far_ref, f32[4,1024]{1,0:T(4,128)S(1)} %copy-done.1, f32[1,1024]{1,0:T(1,128)S(1)} %bitcast.7, ...), custom_call_target="tpu_custom_call" | custom-call | flops 1073741824 | bytes 8388608 | tf_op jit(solution)/shard_map/wall_and_residual/pallas_call | solution.py:299
  (37 shorter events, 0.2 us)
Async XLA Ops:
  0.6 14.3 %copy-start.9 = (bf16[4,270,270]{2,0,1:T(4,128)(2,1)S(1)}, bf16[4,270,270]{2,0,1:T(4,128)(2,1)}, u32[]{:S(2)}) copy-start(bf16[4,270,270]{2,0,1:T(4,128)(2,1)} %param.20) | copy-start | bytes 1749604
  1.4 14.3 %collective-permute-start = (f32[1,48,128]{2,1,0:T(8,128)S(1)}, f32[1,48,128]{2,1,0:T(8,128)S(1)}, u32[]{:S(2)}, u32[]{:S(2)}) collective-permute-start(f32[1,48,128]{2,1,0:T(8,128)S(1)} %maximum_bitcast_fusion), channel_id=1, source_target_pairs={{0,4},{1,5},{2,6},{3,7},{4,0},{5,1},{6,2},{7,3},{8,12},{9,13},{10,... | collective-permute-start | bytes 73736 | tf_op jit(solution)/shard_map/ppermute | solution.py:346
  7.3 23.2 %collective-permute-start.5 = (bf16[96,128]{1,0:T(8,128)(2,1)}, bf16[96,128]{1,0:T(8,128)(2,1)S(1)}, u32[]{:S(2)}, u32[]{:S(2)}) collective-permute-start(bf16[96,128]{1,0:T(8,128)(2,1)} %get-tuple-element.6), channel_id=1, source_target_pairs={{0,1},{1,2},{2,3},{3,4},{4,5},{5,6},{6,7},{7,0},{8,9},{9,10},{10,1... | collective-permute-start | bytes 73736 | tf_op jit(solution)/shard_map/ppermute | solution.py:324
  8.8 21.7 %collective-permute-start.6 = (bf16[96,128]{1,0:T(8,128)(2,1)}, bf16[96,128]{1,0:T(8,128)(2,1)S(1)}, u32[]{:S(2)}, u32[]{:S(2)}) collective-permute-start(bf16[96,128]{1,0:T(8,128)(2,1)} %get-tuple-element.7), channel_id=1, source_target_pairs={{0,7},{1,0},{2,1},{3,2},{4,3},{5,4},{6,5},{7,6},{8,15},{9,8},{10,9... | collective-permute-start | bytes 73736 | tf_op jit(solution)/shard_map/ppermute | solution.py:324
  12.0 18.5 %collective-permute-start.7 = (bf16[96,128]{1,0:T(8,128)(2,1)}, bf16[96,128]{1,0:T(8,128)(2,1)S(1)}, u32[]{:S(2)}, u32[]{:S(2)}) collective-permute-start(bf16[96,128]{1,0:T(8,128)(2,1)} %get-tuple-element.8), channel_id=1, source_target_pairs={{0,8},{8,16},{16,24},{24,0},{1,9},{9,17},{17,25},{25,1},{2,10},{10... | collective-permute-start | bytes 73736 | tf_op jit(solution)/shard_map/ppermute | solution.py:324
  12.0 18.5 %collective-permute-start.8 = (bf16[96,128]{1,0:T(8,128)(2,1)}, bf16[96,128]{1,0:T(8,128)(2,1)S(1)}, u32[]{:S(2)}, u32[]{:S(2)}) collective-permute-start(bf16[96,128]{1,0:T(8,128)(2,1)} %get-tuple-element.9), channel_id=1, source_target_pairs={{0,24},{8,0},{16,8},{24,16},{1,25},{9,1},{17,9},{25,17},{2,26},{10... | collective-permute-start | bytes 73736 | tf_op jit(solution)/shard_map/ppermute | solution.py:324
  14.9 1.0 %copy-start.10 = (f32[3,8,128]{2,1,0:T(8,128)S(1)}, f32[3,8,128]{2,1,0:T(8,128)}, u32[]{:S(2)}) copy-start(f32[3,8,128]{2,1,0:T(8,128)} %param.24) | copy-start | bytes 36868
  14.9 1.0 %copy-start.11 = (f32[3,8,128]{2,1,0:T(8,128)S(1)}, f32[3,8,128]{2,1,0:T(8,128)}, u32[]{:S(2)}) copy-start(f32[3,8,128]{2,1,0:T(8,128)} %param.23) | copy-start | bytes 36868
  14.9 1.0 %copy-start.12 = (bf16[6,2,5,5]{0,1,3,2:T(2,128)(2,1)S(1)}, bf16[6,2,5,5]{0,1,3,2:T(2,128)(2,1)}, u32[]{:S(2)}) copy-start(bf16[6,2,5,5]{0,1,3,2:T(2,128)(2,1)} %param.22) | copy-start | bytes 1804
  15.1 15.5 %copy-start = (bf16[270,1024]{1,0:T(8,128)(2,1)S(1)}, bf16[270,1024]{1,0:T(8,128)(2,1)}, u32[]{:S(2)}) copy-start(bf16[270,1024]{1,0:T(8,128)(2,1)} %state_ref.3) | copy-start | bytes 1658884
  15.1 15.5 %copy-start.4 = (s32[6,1024]{1,0:T(8,128)S(1)}, s32[6,1024]{1,0:T(8,128)}, u32[]{:S(2)}) copy-start(s32[6,1024]{1,0:T(8,128)} %nbr_ref.1) | copy-start | bytes 73732
  15.1 15.5 %copy-start.5 = (bf16[576,270]{1,0:T(8,128)(2,1)S(1)}, bf16[576,270]{1,0:T(8,128)(2,1)}, u32[]{:S(2)}) copy-start(bf16[576,270]{1,0:T(8,128)(2,1)} %constant.14.clone.picks_ref) | copy-start | bytes 933124
  15.1 15.5 %copy-start.6 = (bf16[60,1152]{1,0:T(8,128)(2,1)S(1)}, bf16[60,1152]{1,0:T(8,128)(2,1)}, u32[]{:S(2)}) copy-start(bf16[60,1152]{1,0:T(8,128)(2,1)} %constant.16.clone.right_ref) | copy-start | bytes 414724
  15.1 15.5 %copy-start.7 = (f32[96,192]{1,0:T(8,128)S(1)}, f32[96,192]{1,0:T(8,128)}, u32[]{:S(2)}) copy-start(f32[96,192]{1,0:T(8,128)} %constant.17.clone.same_ref) | copy-start | bytes 221188
  15.1 15.5 %copy-start.8 = (bf16[96,5]{1,0:T(8,128)(2,1)S(1)}, bf16[96,5]{1,0:T(8,128)(2,1)}, u32[]{:S(2)}) copy-start(bf16[96,5]{1,0:T(8,128)(2,1)} %constant.15.clone.left_ref) | copy-start | bytes 2884
  15.8 4.2 %collective-permute-start.1 = (f32[2,48,128]{2,1,0:T(8,128)S(1)}, f32[2,48,128]{2,1,0:T(8,128)S(1)}, u32[]{:S(2)}, u32[]{:S(2)}) collective-permute-start(f32[2,48,128]{2,1,0:T(8,128)S(1)} %pad_maximum_fusion.3), channel_id=1, source_target_pairs={{0,2},{1,3},{2,0},{3,1},{4,6},{5,7},{6,4},{7,5},{8,10},{9,11},{10,... | collective-permute-start | bytes 147464 | tf_op jit(solution)/shard_map/ppermute | solution.py:346
  19.9 4.7 %collective-permute-start.2 = (f32[4,48,128]{2,1,0:T(8,128)S(1)}, f32[4,48,128]{2,1,0:T(8,128)S(1)}, u32[]{:S(2)}, u32[]{:S(2)}) collective-permute-start(f32[4,48,128]{2,1,0:T(8,128)S(1)} %pad_maximum_fusion.2), channel_id=1, source_target_pairs={{0,1},{1,0},{2,3},{3,2},{4,5},{5,4},{6,7},{7,6},{8,9},{9,8},{10,11... | collective-permute-start | bytes 294920 | tf_op jit(solution)/shard_map/ppermute | solution.py:346
  24.6 5.7 %collective-permute-start.3 = (f32[8,48,128]{2,1,0:T(8,128)S(1)}, f32[8,48,128]{2,1,0:T(8,128)S(1)}, u32[]{:S(2)}, u32[]{:S(2)}) collective-permute-start(f32[8,48,128]{2,1,0:T(8,128)S(1)} %pad_maximum_fusion.1), channel_id=1, source_target_pairs={{0,16},{8,24},{16,0},{24,8},{1,17},{9,25},{17,1},{25,9},{2,18},{10... | collective-permute-start | bytes 589832 | tf_op jit(solution)/shard_map/ppermute | solution.py:346
  30.4 9.2 %copy-start.1 = (f32[4,1024]{1,0:T(4,128)S(1)}, f32[4,1024]{1,0:T(4,128)}, u32[]{:S(2)}) copy-start(f32[4,1024]{1,0:T(4,128)} %base_ref.1) | copy-start | bytes 49156
  30.4 9.2 %copy-start.2 = (f32[1024]{0:T(1024)S(1)}, f32[1024]{0:T(1024)}, u32[]{:S(2)}) copy-start(f32[1024]{0:T(1024)} %param.17) | copy-start | bytes 12292
  30.4 9.2 %copy-start.3 = (s32[1024]{0:T(1024)S(1)}, s32[1024]{0:T(1024)}, u32[]{:S(2)}) copy-start(s32[1024]{0:T(1024)} %param.18) | copy-start | bytes 12292
  30.4 9.1 %collective-permute-start.4 = (f32[16,48,128]{2,1,0:T(8,128)S(1)}, f32[16,48,128]{2,1,0:T(8,128)S(1)}, u32[]{:S(2)}, u32[]{:S(2)}) collective-permute-start(f32[16,48,128]{2,1,0:T(8,128)S(1)} %constant_dynamic-update-slice_fusion.near_ref), channel_id=1, source_target_pairs={{0,8},{8,0},{16,24},{24,16},{1,9},{9,1},{17,25},{25,17},{2,10},{10... | collective-permute-start | bytes 1179656 | tf_op jit(solution)/shard_map/ppermute | solution.py:346

commit v2 on v1

v2 whole, which is shorter than its diff:
```python
import functools

import jax
import jax.numpy as jnp
import numpy as np
from jax import lax
from jax.experimental import pallas as pl
from jax.experimental.pallas import tpu as pltpu
from jax.sharding import PartitionSpec as P

NV = 5
ITERS = 8
NODES = 18
SLOT = 96
TILE = 8
WIDE = 256
BOTH = ("sec", "dom")


def face_rows(face):
    rows = np.arange(NV * 54).reshape(NV * 2, 3, 3, 3)
    return np.take(rows, 0 if face % 2 == 0 else 2, axis=1 + face // 2).reshape(-1)


def picker(faces, unknowns):
    picks = np.zeros((len(faces) * SLOT, unknowns), np.float32)
    for slot, face in enumerate(faces):
        rows = face_rows(face)
        picks[slot * SLOT + np.arange(rows.size), rows] = 1
    return jnp.asarray(picks, jnp.bfloat16)


def kron_parts(sides):
    row = np.arange(SLOT)
    valid = row < NV * NODES
    variable, node = row // NODES, row % NODES
    left = np.zeros((SLOT, NV), np.float32)
    left[row[valid], variable[valid]] = 1
    right = np.zeros((sides * NV, sides * SLOT), np.float32)
    for side in range(sides):
        right[side * NV + variable[valid], side * SLOT + row[valid]] = 1
    same = (node[:, None] == node[None, :]) & valid[:, None] & valid[None, :]
    return (
        jnp.asarray(left, jnp.bfloat16),
        jnp.asarray(right, jnp.bfloat16),
        jnp.asarray(np.concatenate([same, same], axis=1), jnp.float32),
    )


def dot(a, b):
    return jnp.dot(a, b, preferred_element_type=jnp.float32)


VMEM = pl.BlockSpec(memory_space=pltpu.VMEM)


def odd(axis):
    return lax.rem(lax.axis_index(axis), 2) == 1


def trace_kernel(state_ref, picks_ref, late_ref, trace_ref, *head_refs):
    unknowns, count = state_ref.shape
    width = head_refs[0].shape[1]
    early = min(unknowns, WIDE)
    tail = SLOT - late_ref.shape[0] // 6
    for chunk in range(count // WIDE):
        cols = slice(chunk * WIDE, (chunk + 1) * WIDE)
        picked = dot(picks_ref[...], state_ref[:early, cols])
        late = dot(late_ref[...], state_ref[early:, cols])
        rest = SLOT - tail
        for face in range(6):
            first = face * SLOT
            low = picked[first : first + tail].astype(jnp.bfloat16)
            high = (picked[first + tail : first + SLOT] + late[face * rest : (face + 1) * rest]).astype(jnp.bfloat16)
            trace_ref[face, chunk, :tail, :] = low
            trace_ref[face, chunk, tail:, :] = high
    for axis, which in enumerate(BOTH[::-1]):
        flip = odd(which)
        low, high = (trace_ref[2 * axis + side, 0, :, :width] for side in range(2))
        head_refs[2 * axis][...] = jnp.where(flip, low, high)
        head_refs[2 * axis + 1][...] = jnp.where(flip, high, low)


def all_traces(flow_state, head_count):
    unknowns, count = flow_state.shape
    picks = picker(range(6), unknowns)
    early = min(unknowns, WIDE)
    rows = np.concatenate([face_rows(face) for face in range(6)]).reshape(6, -1)
    tail = int(np.nonzero((rows >= early).any(axis=0))[0][0]) // 16 * 16
    late = picks.reshape(6, SLOT, unknowns)[:, tail:, early:].reshape(-1, unknowns - early)
    return pl.pallas_call(
        trace_kernel,
        in_specs=[VMEM] * 3,
        out_specs=[VMEM] * 5,
        out_shape=[jax.ShapeDtypeStruct((6, count // WIDE, SLOT, WIDE), jnp.bfloat16)]
        + [jax.ShapeDtypeStruct((SLOT, head_count), jnp.bfloat16)] * 4,
        compiler_params=pltpu.CompilerParams(vmem_limit_bytes=24 << 20),
        cost_estimate=pl.CostEstimate(flops=1 << 30, bytes_accessed=4 << 20, transcendentals=0),
        name="all_traces",
    )(flow_state, picks[:, :early], late)


def chosen(index, rows):
    row = lax.broadcasted_iota(jnp.int32, (rows, index.shape[1]), 0)
    return jnp.where(row == index, 1.0, 0.0).astype(jnp.bfloat16)


def local_kernel(trace_ref, nbr_ref, volume_ref, lift_ref, jac_ref, left_ref, right_ref, same_ref, out_ref, weights_ref, flux_mat_ref):
    chunks = trace_ref.shape[1]
    spread = dot(left_ref[...], jac_ref[...]).astype(jnp.bfloat16)
    spread = dot(spread, right_ref[...])
    for face in range(6):
        both = spread[:, face * 2 * SLOT : (face + 1) * 2 * SLOT]
        flux_mat_ref[face] = (both * same_ref[...]).astype(jnp.bfloat16)
    unknowns = volume_ref.shape[1]
    values = lift_ref.shape[2]
    first, second, total_width = operand_places(unknowns)
    for direction in range(4):
        weights_ref[direction, :, :unknowns] = volume_ref[direction]
        weights_ref[direction, :, unknowns:] = jnp.zeros((unknowns, total_width - unknowns), jnp.bfloat16)
        if direction < 3:
            weights_ref[direction, :, first : first + values] = lift_ref[2 * direction]
            weights_ref[direction, :, second : second + values] = lift_ref[2 * direction + 1]
    for step in range(chunks):
        here = slice(step * WIDE, (step + 1) * WIDE)
        for face in range(6):
            index = nbr_ref[face : face + 1, here]
            part = lax.shift_right_logical(index, WIDE.bit_length() - 1)
            source = trace_ref[face ^ 1].reshape(chunks * SLOT, WIDE)
            each = dot(source, chosen(jnp.bitwise_and(index, WIDE - 1), WIDE))
            found = jnp.where(part == 0, each[:SLOT], 0.0)
            for chunk in range(1, chunks):
                found = jnp.where(part == chunk, each[chunk * SLOT : (chunk + 1) * SLOT], found)
            out_ref[face, :, here] = found.astype(jnp.bfloat16)


def operand_places(unknowns):
    first = -(-unknowns // 16) * 16
    second = -(-(first + SLOT) // 128) * 128
    return first, second, second + SLOT


def local_traces(traces, face_nbr, volume_ops, lift_ops, jac):
    faces, chunks, slot, wide = traces.shape
    unknowns = volume_ops.shape[1]
    args = (traces, face_nbr, volume_ops, lift_ops, jac, *kron_parts(12))
    return pl.pallas_call(
        local_kernel,
        in_specs=[VMEM] * len(args),
        out_specs=[VMEM] * 3,
        out_shape=[
            jax.ShapeDtypeStruct((faces, slot, chunks * wide), jnp.bfloat16),
            jax.ShapeDtypeStruct((4, unknowns, operand_places(unknowns)[2]), jnp.bfloat16),
            jax.ShapeDtypeStruct((6, SLOT, 2 * SLOT), jnp.bfloat16),
        ],
        compiler_params=pltpu.CompilerParams(vmem_limit_bytes=24 << 20),
        cost_estimate=pl.CostEstimate(flops=2 << 30, bytes_accessed=4 << 20, transcendentals=0),
        name="local_traces",
    )(*args)


def flow_kernel(
    state_ref, nbr_ref, trace_ref, local_ref, partner0, other0, partner1, other1, weights_ref, flux_mat_ref,
    out_ref, remote_ref,
):
    unknowns, count = state_ref.shape
    first, second, height = operand_places(unknowns)
    for axis, (partner, other, which) in enumerate(((partner0, other0, "dom"), (partner1, other1, "sec"))):
        flip = odd(which)
        remote_ref[2 * axis] = jnp.where(flip, partner[...], other[...])
        remote_ref[2 * axis + 1] = jnp.where(flip, other[...], partner[...])

    def some(step, carry):
        here = pl.ds(pl.multiple_of(step * WIDE, WIDE), WIDE)
        fluxes = []
        for face in range(6):
            found = local_ref[face, :, here]
            if face < 4:
                index = nbr_ref[face : face + 1, here] - count
                found += dot(remote_ref[face], chosen(index, remote_ref.shape[2])).astype(jnp.bfloat16)
            sides = jnp.concatenate([trace_ref[face, step], found], axis=0)
            fluxes.append(dot(flux_mat_ref[face], sides).astype(jnp.bfloat16))
        own = state_ref[:, here]
        own_padded = jnp.concatenate([own, jnp.zeros((first - unknowns, WIDE), jnp.bfloat16)], axis=0)
        gap = jnp.zeros((second - first - SLOT, WIDE), jnp.bfloat16)
        for direction in range(4):
            if direction < 3:
                operand = jnp.concatenate([own_padded, fluxes[2 * direction], gap, fluxes[2 * direction + 1]], axis=0)
                out_ref[direction, :, here] = dot(weights_ref[direction], operand)
            else:
                out_ref[direction, :, here] = dot(weights_ref[direction, :, :unknowns], own)
        return carry

    lax.fori_loop(0, count // WIDE, some, 0)


def flow_parts(flow_state, face_nbr, traces, local, remotes, weights, flux_mat):
    unknowns, count = flow_state.shape
    args = (flow_state, face_nbr, traces, local, *remotes, weights, flux_mat)
    return pl.pallas_call(
        flow_kernel,
        in_specs=[VMEM] * len(args),
        out_specs=VMEM,
        out_shape=jax.ShapeDtypeStruct((4, unknowns, count), jnp.float32),
        scratch_shapes=[pltpu.VMEM((4, *remotes[0].shape), jnp.bfloat16)],
        compiler_params=pltpu.CompilerParams(vmem_limit_bytes=32 << 20),
        cost_estimate=pl.CostEstimate(flops=3 << 30, bytes_accessed=4 << 20, transcendentals=0),
        name="flow_parts",
    )(*args)


def total(tiles):
    tile = functools.reduce(jnp.add, tiles)
    tile = jnp.sum(jnp.sum(tile, axis=0, keepdims=True), axis=1, keepdims=True)
    return jnp.broadcast_to(tile, (TILE, 128))


def wall_kernel(
    masks, rows, own_rows,
    near_ref, far_ref, base_ref, follow_ref, anchor_ref, parts_ref, residual_ref, disp_ref,
    disp, resid, applied, search, image, diag,
):
    comps = 3
    tiles = rows // TILE
    me = lax.axis_index(BOTH)

    def strided(block):
        first = block * TILE
        return pl.ds((first % tiles) * TILE + first // tiles, TILE, stride=TILE)

    each = 3 * comps * own_rows
    half = near_ref.shape[0] // each
    for pair in range(half):
        ref, at = (near_ref, pair) if pair < half // 2 else (far_ref, pair - half // 2)
        both = ref[2 * at * each : 2 * (at + 1) * each, :].astype(jnp.float32)
        for slot in range(2):
            device = jnp.bitwise_xor(me, masks[2 * pair + slot])
            upper, lower, stiff = (both[slot * each + k * comps * own_rows :][: comps * own_rows] for k in range(3))
            load = upper + lower
            for block in range(own_rows // TILE):
                to = strided(device * (own_rows // TILE) + block)
                for c in range(comps):
                    first = c * own_rows + block * TILE
                    resid[c, to, :] = load[first : first + TILE]
                    diag[c, to, :] = 4.0 + stiff[first : first + TILE]

    lane = lax.broadcasted_iota(jnp.int32, (TILE, 128), 1)
    sub = lax.broadcasted_iota(jnp.int32, (TILE, 128), 0)
    group = 32 if tiles % 32 == 0 else 8
    zero = jnp.zeros((TILE, 128), jnp.float32)

    def at(tile):
        return pl.ds(tile * TILE if isinstance(tile, int) else pl.multiple_of(tile * TILE, TILE), TILE)

    def sweep(renew):
        norms, energies = [], []
        for c in range(comps):
            above = jnp.where(sub == 0, 0.0, pltpu.roll(renew(c, tiles - 1, False), 1, 0))

            def operate(tile, above, value, below, c=c):
                beside = above + below
                beside += jnp.where(lane == 0, 0.0, pltpu.roll(value, 1, 1))
                beside += jnp.where(lane == 127, 0.0, pltpu.roll(value, 127, 1))
                result = diag[c, at(tile), :] * value - beside
                applied[c, at(tile), :] = result
                return value * value, value * result

            def some(chunk, carry, c=c):
                above, value, norm, energy = carry
                norm, energy = [norm, zero], [energy, zero]
                for k in range(group):
                    tile = chunk * group + k + 1
                    below = renew(c, tile, True)
                    terms = operate(tile - 1, above, value, below)
                    norm[k % 2] += terms[0]
                    energy[k % 2] += terms[1]
                    above, value = value, below
                return above, value, norm[0] + norm[1], energy[0] + energy[1]

            first = value = renew(c, 0, True)
            norm = energy = zero
            if tiles > group:
                above, value, norm, energy = lax.fori_loop(0, tiles // group - 1, some, (above, value, norm, energy))
            norm, energy = [norm, zero], [energy, zero]
            for tile in range(tiles - group + 1, tiles + 1):
                if tile < tiles:
                    below = renew(c, tile, True)
                else:
                    below = jnp.where(sub == TILE - 1, 0.0, pltpu.roll(first, TILE - 1, 0))
                terms = operate(tile - 1, above, value, below)
                norm[tile % 2] += terms[0]
                energy[tile % 2] += terms[1]
                above, value = value, below
            norms += norm
            energies += energy
        return total(norms), total(energies)

    def begin(c, tile, keep):
        return resid[c, at(tile), :]

    def advance(step_size, ratio, last_step=None, first=False):
        def renew(c, tile, keep):
            value = resid[c, at(tile), :]
            toward, moved = value, applied[c, at(tile), :]
            if not first:
                before = search[c, at(tile), :]
                toward += ratio * before
                moved += ratio * image[c, at(tile), :]
            value -= step_size * moved
            if keep:
                search[c, at(tile), :] = toward
                image[c, at(tile), :] = moved
                resid[c, at(tile), :] = value
                if last_step is not None:
                    disp[c, at(tile), :] += last_step * before + step_size * toward
            return value

        return renew

    def sizes(norm, energy, last_norm, last_curve):
        ratio = norm / last_norm
        curve = energy - ratio * ratio * last_curve
        return norm / curve, ratio, curve

    norm, curve = sweep(begin)
    step_size = norm / curve
    last_norm, last_curve, last_step = norm, curve, step_size
    norm, energy = sweep(advance(step_size, None, first=True))

    def clear(tile, carry):
        for c in range(comps):
            disp[c, at(tile), :] = zero
        return carry

    lax.fori_loop(0, tiles, clear, 0, unroll=8)

    def two(position, carry):
        norm, energy, last_norm, last_curve, last_step = carry
        step_size, ratio, curve = sizes(norm, energy, last_norm, last_curve)
        last_norm = norm
        norm, energy = sweep(advance(step_size, ratio, last_step))
        step_size, ratio, curve = sizes(norm, energy, last_norm, curve)
        last_norm = norm
        norm, energy = sweep(advance(step_size, ratio))
        return norm, energy, last_norm, curve, step_size

    assert ITERS % 2 == 0
    carry = lax.fori_loop(0, ITERS // 2 - 1, two, (norm, energy, last_norm, last_curve, last_step))
    norm, energy, last_norm, last_curve, last_step = carry
    step_size, ratio, curve = sizes(norm, energy, last_norm, last_curve)

    def finish(tile, carry):
        for c in range(comps):
            before = search[c, at(tile), :]
            toward = resid[c, at(tile), :] + ratio * before
            disp[c, at(tile), :] += last_step * before + step_size * toward
        return carry

    lax.fori_loop(0, tiles, finish, 0, unroll=8)

    for block in range(own_rows // TILE):
        for c in range(comps):
            disp_ref[c, block * TILE : (block + 1) * TILE, :] = disp[c, strided(me * (own_rows // TILE) + block), :]

    anchor = anchor_ref[...]
    count = anchor.shape[1]
    row = anchor // 128
    column = anchor - row * 128
    upper = row // tiles
    place = (row - upper * tiles) * TILE + upper
    pick = jnp.where(lax.broadcasted_iota(jnp.int32, (128, count), 0) == column, 1.0, 0.0).astype(jnp.bfloat16)
    pick = jnp.concatenate([pick, pick], axis=0)
    some_rows = 128
    row_of = lax.broadcasted_iota(jnp.int32, (some_rows, count), 0)

    def look(chunk, sums):
        first = pl.multiple_of(chunk * some_rows, some_rows)
        hit = row_of == place - first
        out = []
        for c in range(comps):
            value = disp[c, pl.ds(first, some_rows), :]
            coarse = value.astype(jnp.bfloat16)
            fine = (value - coarse.astype(jnp.float32)).astype(jnp.bfloat16)
            found = dot(jnp.concatenate([coarse, fine], axis=1), pick)
            found = jnp.where(hit, found, 0.0).reshape(some_rows // TILE, TILE, count)
            out.append(sums[c] + jnp.sum(found, axis=0))
        return tuple(out)

    sums = lax.fori_loop(0, rows // some_rows, look, (jnp.zeros((TILE, count), jnp.float32),) * comps)
    follow = follow_ref[...]
    geometry = [
        base_ref[c : c + 1, :] * jnp.exp(follow * jnp.sum(sums[c], axis=0, keepdims=True)) for c in range(comps)
    ]
    geometry.append(base_ref[comps : comps + 1, :])
    unknowns = residual_ref.shape[0]
    for first in range(0, unknowns, 16):
        some = slice(first, min(first + 16, unknowns))
        value = geometry[0] * parts_ref[0, some, :]
        for direction in range(1, 4):
            value += geometry[direction] * parts_ref[direction, some, :]
        residual_ref[some, :] = value.astype(jnp.bfloat16)


def wall_and_residual(near, far, masks, base_geometry, anchor_weight, wall_anchor, parts, own_rows):
    rows = own_rows * len(masks)
    _, unknowns, count = parts.shape
    field = pltpu.VMEM((3, rows, 128), jnp.float32)
    return pl.pallas_call(
        functools.partial(wall_kernel, masks, rows, own_rows),
        in_specs=[VMEM] * 6,
        out_specs=[VMEM] * 2,
        out_shape=[
            jax.ShapeDtypeStruct((unknowns, count), jnp.bfloat16),
            jax.ShapeDtypeStruct((3, own_rows, 128), jnp.float32),
        ],
        scratch_shapes=[
            field,
            field,
            field,
            field,
            field,
            field,
        ],
        compiler_params=pltpu.CompilerParams(vmem_limit_bytes=(16 << 20) + 16 * rows * 3 * 128 * 4),
        cost_estimate=pl.CostEstimate(flops=4 << 30, bytes_accessed=8 << 20, transcendentals=0),
        name="wall_and_residual",
    )(near, far, base_geometry, anchor_weight[None, :], wall_anchor[None, :], parts)


def paired(x, axis, offset):
    peers = lax.axis_size(axis)
    pairs = [((i + offset) % peers, (i + offset + 1) % peers) for i in range(0, peers, 2)]
    return lax.ppermute(x, axis, pairs + [pair[::-1] for pair in pairs])


def gather_stages(mesh):
    def bits(axis):
        assert mesh.shape[axis] & (mesh.shape[axis] - 1) == 0
        return [(axis, 1 << b) for b in reversed(range(mesh.shape[axis].bit_length() - 1))]

    return bits("dom") + bits("sec")


def on_device(
    stages, n_dom,
    flow_state, base_geometry, anchor_weight, wall_anchor, face_nbr, volume_ops, lift_ops, face_jac, wall_load, wall_stiff,
):
    own_rows, width = wall_load.shape[1:]
    upper = lax.reduce_precision(wall_load, 8, 7)
    wall = jnp.concatenate([upper, wall_load - upper, wall_stiff], axis=0).astype(jnp.bfloat16)
    wall = wall.reshape(9 * own_rows, width)
    masks = [0]
    for axis, bit in stages:
        masks += [m ^ (bit * n_dom if axis == "sec" else bit) for m in masks]

    def sent(wall, position):
        axis, bit = stages[position]
        return lax.ppermute(wall, axis, [(i, i ^ bit) for i in range(lax.axis_size(axis))])

    barrier = lax.optimization_barrier
    far = sent(wall, 0)
    head_count = flow_state.shape[1] // 8
    traces, *heads = all_traces(flow_state, head_count)
    far, traces, heads = barrier((far, traces, heads))
    wall = jnp.concatenate([wall, far], axis=0)
    far = sent(wall, 1)
    remotes = [None] * 4
    remotes[2] = paired(heads[2], "sec", 0)
    remotes[1] = paired(heads[1], "dom", 1)
    far, heads, remotes[2], volume_ops, lift_ops, face_jac = barrier((far, heads, remotes[2], volume_ops, lift_ops, face_jac))
    wall = jnp.concatenate([wall, far], axis=0)
    far = sent(wall, 2)
    remotes[0] = paired(heads[0], "dom", 0)
    remotes[3] = paired(heads[3], "sec", 1)
    jac = face_jac.transpose(2, 0, 1, 3).reshape(NV, 12 * NV)
    local, weights, flux_mat = local_traces(traces, face_nbr, volume_ops, lift_ops, jac)
    far, remotes, local = barrier((far, remotes, local))
    wall = jnp.concatenate([wall, far], axis=0)
    far = sent(wall, 3)
    parts = flow_parts(flow_state, face_nbr, traces, local, remotes, weights, flux_mat)
    far, parts = barrier((far, parts))
    for position in range(4, len(stages)):
        wall = jnp.concatenate([wall, far], axis=0)
        far = sent(wall, position)
    return wall_and_residual(wall, far, masks, base_geometry, anchor_weight, wall_anchor, parts, own_rows)


def solution(mesh):
    return jax.shard_map(
        functools.partial(on_device, gather_stages(mesh), mesh.shape["dom"]),
        mesh=mesh,
        in_specs=(
            P(None, BOTH),
            P(None, BOTH),
            P(BOTH),
            P(BOTH),
            P(None, BOTH),
            P(),
            P(),
            P(),
            P(None, BOTH, None),
            P(None, BOTH, None),
        ),
        out_specs=(P(None, BOTH), P(None, BOTH, None)),
        check_vma=False,
    )
```

time: 47.7 us -> 33.2 us (0.70)
  waiting for transfers between devices: 12.5 us -> 4.53 us
  Pallas kernels: 18.6 us -> 11.1 us
  local copies, waits for them, and re-layouts: 1.61 us -> 3.23 us
  starting transfers between devices: 12.3 us -> 11.7 us
    ppermute x9, waiting for transfers between devices: 12.5 us -> 4.53 us  [the longest x5 3.49 us: sent(): lax.ppermute(wall, axis, [(i, i ^ bit) for i in range(lax.axis_size(axis))])]
    pallas_call x2 -> x3, Pallas kernels: 10.8 us -> 5.46 us  [the longest x1 3 us: flow_parts(): pl.pallas_call(flow_kernel, in_specs=[VMEM] * len(args), out_specs=VMEM,...]
    unnamed x30 -> x31, local copies, waits for them, and re-layouts: 0.21 us -> 2.85 us
    pallas_call x1, Pallas kernels: 7.8 us -> 5.68 us  [wall_and_residual(): pl.pallas_call(functools.partial(wall_kernel, masks, rows, own_rows), in_...]
    another operation x0 -> x2, other arithmetic: none -> 1.42 us
    slice x1 -> x0, local copies, waits for them, and re-layouts: 1.13 us -> none  [on_device(): weights = jnp.concatenate([lifts[0::2], lifts[1::2], volume_ops], axis=2)]
    reshape x1 -> x0, other arithmetic: 0.8 us -> none  [on_device(): jnp.concatenate([wall_load, wall_stiff], axis=0)]
    concatenate x1 -> x0, other arithmetic: 0.63 us -> none  [on_device(): weights = jnp.concatenate([lifts[0::2], lifts[1::2], volume_ops], axis=2)]
  transfers between devices with their start and end apart: 9 -> 9, of which waited for: 3 -> 5; matrix products, arithmetic and copies ran while one was open for 5% -> 1% of each run, Pallas kernels for 23% -> 17%
where the time goes in v2:
time: 33.2 us; the launch traced here: 32.9 us
  starting transfers between devices  11.7 us (35%)
  Pallas kernels  11.1 us (33%)
  waiting for transfers between devices  4.53 us (14%)
  local copies, waits for them, and re-layouts  3.23 us (10%)
  other arithmetic  1.45 us (4%)
  between operations  0.81 us (2%)
    ppermute x5, starting transfers between devices, sent(): lax.ppermute(wall, axis, [(i, i ^ bit) for i in range(lax.axis_size(axis))])  8.72 us
    pallas_call x1, Pallas kernels, wall_and_residual(): pl.pallas_call(functools.partial(wall_kernel, masks, rows, own_rows), in_...  5.68 us
    ppermute x5, waiting for transfers between devices, sent(): lax.ppermute(wall, axis, [(i, i ^ bit) for i in range(lax.axis_size(axis))])  3.49 us
    pallas_call x1, Pallas kernels, flow_parts(): pl.pallas_call(flow_kernel, in_specs=[VMEM] * len(args), out_specs=VMEM,...  3 us
    ppermute x4, starting transfers between devices, paired(): return lax.ppermute(x, axis, pairs + [pair[::-1] for pair in pairs])  2.99 us
    unnamed x31, local copies, waits for them, and re-layouts  2.85 us
    pallas_call x1, Pallas kernels, local_traces(): pl.pallas_call(local_kernel, in_specs=[VMEM] * len(args), out_specs=[VMEM...  1.91 us
    another operation x2, other arithmetic  1.42 us
  transfers between devices with their start and end apart: 9, of which 5 were waited for; matrix products, arithmetic and copies ran while one was open for 1% of the time, Pallas kernels for 17%

profile of v2, /device:TPU:0, one launch (start us, length us, event | category | flops | bytes accessed | tf_op | source)
XLA Modules:
  0.0 32.9 jit_solution(10338583220688850126)
XLA Ops:
  0.6 0.7 %reduce-precision_convert_fusion = (bf16[3,8,128]{2,1,0:T(8,128)(2,1)S(1)}, bf16[3,8,128]{2,1,0:T(8,128)(2,1)S(1)}) fusion(f32[3,8,128]{2,1,0:T(8,128)} %param.22), kind=kLoop, calls=%fused_computation.5 | loop fusion | flops 12288 | bytes 24576 | tf_op jit(solution)/shard_map/convert
  1.3 0.7 %convert.11 = bf16[3,8,128]{2,1,0:T(8,128)(2,1)S(1)} convert(f32[3,8,128]{2,1,0:T(8,128)} %param.23) | non-fusion elementwise | flops 3072 | bytes 18432 | tf_op jit(solution)/shard_map/convert.2
  2.1 4.0 %collective-permute-start = (bf16[72,128]{1,0:T(8,128)(2,1)S(1)}, bf16[72,128]{1,0:T(8,128)(2,1)S(1)}, u32[]{:S(2)}, u32[]{:S(2)}) collective-permute-start(bf16[72,128]{1,0:T(8,128)(2,1)S(1)} %maximum_bitcast_fusion), channel_id=1, source_target_pairs={{0,4},{1,5},{2,6},{3,7},{4,0},{5,1},{6,2},{7,3},{8,12},{9,13},{10,... | collective-permute-start | bytes 55304 | tf_op jit(solution)/shard_map/ppermute | solution.py:458
  6.1 1.1 %copy-done = bf16[270,1024]{1,0:T(8,128)(2,1)S(1)} copy-done((bf16[270,1024]{1,0:T(8,128)(2,1)S(1)}, bf16[270,1024]{1,0:T(8,128)(2,1)}, u32[]{:S(2)}) %copy-start) | copy-done | bytes 552984
  7.2 1.0 %copy-done.7 = bf16[576,256]{1,0:T(8,128)(2,1)S(1)} copy-done((bf16[576,256]{1,0:T(8,128)(2,1)S(1)}, bf16[576,256]{1,0:T(8,128)(2,1)}, u32[]{:S(2)}) %copy-start.7) | copy-done | bytes 294936
  8.1 0.7 %copy-done.11 = bf16[96,14]{1,0:T(8,128)(2,1)S(1)} copy-done((bf16[96,14]{1,0:T(8,128)(2,1)S(1)}, bf16[96,14]{1,0:T(8,128)(2,1)}, u32[]{:S(2)}) %copy-start.11) | copy-done | bytes 2712
  8.9 0.6 %all_traces.1 = (bf16[6,4,96,256]{3,2,1,0:T(8,128)(2,1)S(1)}, bf16[96,128]{1,0:T(8,128)(2,1)S(1)}, bf16[96,128]{1,0:T(8,128)(2,1)S(1)}, bf16[96,128]{1,0:T(8,128)(2,1)S(1)}, bf16[96,128]{1,0:T(8,128)(2,1)S(1)}) custom-call(bf16[270,1024]{1,0:T(8,128)(2,1)S(1)} %copy-done, bf16[576,256]{1,0:T(8,128)(2,1)S(1)} %copy-done.7, bf16[96,14]{1,0:T(8,128)(2,1)S(1)} %copy-done.11), custom_call_target="tpu_custom_call" | custom-call | flops 1073741824 | bytes 4194304 | tf_op jit(solution)/shard_map/all_traces/pallas_call | solution.py:91
  9.5 1.6 %collective-permute-start.1 = (bf16[144,128]{1,0:T(8,128)(2,1)S(1)}, bf16[144,128]{1,0:T(8,128)(2,1)S(1)}, u32[]{:S(2)}, u32[]{:S(2)}) collective-permute-start(bf16[144,128]{1,0:T(8,128)(2,1)S(1)} %pad_maximum_fusion.2), channel_id=1, source_target_pairs={{0,2},{1,3},{2,0},{3,1},{4,6},{5,7},{6,4},{7,5},{8,10},{9,11},{10,... | collective-permute-start | bytes 110600 | tf_op jit(solution)/shard_map/ppermute | solution.py:458
  11.2 2.0 %collective-permute-start.5 = (bf16[96,128]{1,0:T(8,128)(2,1)S(1)}, bf16[96,128]{1,0:T(8,128)(2,1)S(1)}, u32[]{:S(2)}, u32[]{:S(2)}) collective-permute-start(bf16[96,128]{1,0:T(8,128)(2,1)S(1)} %get-tuple-element.38), channel_id=1, source_target_pairs={{1,2},{3,4},{5,6},{7,0},{2,1},{4,3},{6,5},{0,7},{9,10},{11,12},{13... | collective-permute-start | bytes 73736 | tf_op jit(solution)/shard_map/ppermute | solution.py:433
  13.2 0.4 %collective-permute-done.1 = bf16[144,128]{1,0:T(8,128)(2,1)S(1)} collective-permute-done((bf16[144,128]{1,0:T(8,128)(2,1)S(1)}, bf16[144,128]{1,0:T(8,128)(2,1)S(1)}, u32[]{:S(2)}, u32[]{:S(2)}) %collective-permute-start.1) | collective-permute-done | bytes 36896 | tf_op jit(solution)/shard_map/ppermute | solution.py:458
  13.5 0.1 copy.19.volume_ref
  13.7 0.2 copy.18
  13.8 0.1 reshape.18.jac_ref
  13.9 1.5 %collective-permute-start.3 = (bf16[288,128]{1,0:T(8,128)(2,1)S(1)}, bf16[288,128]{1,0:T(8,128)(2,1)S(1)}, u32[]{:S(2)}, u32[]{:S(2)}) collective-permute-start(bf16[288,128]{1,0:T(8,128)(2,1)S(1)} %pad_maximum_fusion.1), channel_id=1, source_target_pairs={{0,1},{1,0},{2,3},{3,2},{4,5},{5,4},{6,7},{7,6},{8,9},{9,8},{10,11... | collective-permute-start | bytes 221192 | tf_op jit(solution)/shard_map/ppermute | solution.py:458
  15.5 0.5 %collective-permute-start.4 = (bf16[96,128]{1,0:T(8,128)(2,1)S(1)}, bf16[96,128]{1,0:T(8,128)(2,1)S(1)}, u32[]{:S(2)}, u32[]{:S(2)}) collective-permute-start(bf16[96,128]{1,0:T(8,128)(2,1)S(1)} %get-tuple-element.42), channel_id=1, source_target_pairs={{0,1},{2,3},{4,5},{6,7},{1,0},{3,2},{5,4},{7,6},{8,9},{10,11},{12,... | collective-permute-start | bytes 73736 | tf_op jit(solution)/shard_map/ppermute | solution.py:433
  16.0 0.4 %collective-permute-start.6 = (bf16[96,128]{1,0:T(8,128)(2,1)S(1)}, bf16[96,128]{1,0:T(8,128)(2,1)S(1)}, u32[]{:S(2)}, u32[]{:S(2)}) collective-permute-start(bf16[96,128]{1,0:T(8,128)(2,1)S(1)} %get-tuple-element.44), channel_id=1, source_target_pairs={{8,16},{24,0},{16,8},{0,24},{9,17},{25,1},{17,9},{1,25},{10,18},{2... | collective-permute-start | bytes 73736 | tf_op jit(solution)/shard_map/ppermute | solution.py:433
  16.5 1.9 %local_traces.1 = (bf16[6,96,1024]{2,1,0:T(8,128)(2,1)S(1)}, bf16[4,270,480]{2,1,0:T(8,128)(2,1)S(1)}, bf16[6,96,192]{2,1,0:T(8,128)(2,1)S(1)}) custom-call(bf16[6,4,96,256]{3,2,1,0:T(8,128)(2,1)S(1)} %get-tuple-element.45.trace_ref, s32[6,1024]{1,0:T(8,128)S(1)} %copy-done.3, bf16[4,270,270]{2,1,0:T(8,128)(2,1)S(1)} %copy.19.volume_ref, ...), custom_call_target="tpu_custom_call" | custom-call | flops 2147483648 | bytes 4194304 | tf_op jit(solution)/shard_map/local_traces/pallas_call | solution.py:147
  18.4 0.9 %collective-permute-done.4.partner0 = bf16[96,128]{1,0:T(8,128)(2,1)S(1)} collective-permute-done((bf16[96,128]{1,0:T(8,128)(2,1)S(1)}, bf16[96,128]{1,0:T(8,128)(2,1)S(1)}, u32[]{:S(2)}, u32[]{:S(2)}) %collective-permute-start.4) | collective-permute-done | bytes 24608 | tf_op jit(solution)/shard_map/ppermute | solution.py:433
  19.3 0.2 collective-permute-done.6.other1
  19.5 1.4 %collective-permute-start.7 = (bf16[576,128]{1,0:T(8,128)(2,1)S(1)}, bf16[576,128]{1,0:T(8,128)(2,1)S(1)}, u32[]{:S(2)}, u32[]{:S(2)}) collective-permute-start(bf16[576,128]{1,0:T(8,128)(2,1)S(1)} %pad_maximum_fusion), channel_id=1, source_target_pairs={{0,16},{8,24},{16,0},{24,8},{1,17},{9,25},{17,1},{25,9},{2,18},{10... | collective-permute-start | bytes 442376 | tf_op jit(solution)/shard_map/ppermute | solution.py:458
  20.9 3.0 %flow_parts.1.parts_ref = f32[4,270,1024]{2,1,0:T(8,128)S(1)} custom-call(bf16[270,1024]{1,0:T(8,128)(2,1)S(1)} %copy-done.1, s32[6,1024]{1,0:T(8,128)S(1)} %copy-done.3, bf16[6,4,96,256]{3,2,1,0:T(8,128)(2,1)S(1)} %get-tuple-element.45.trace_ref, bf16[6,96,1024]{2,1,0:T(8,128)(2,1)S(1)} %get-tuple-element.51.local_ref, ...), custom_call_target="tpu_custom_call" | custom-call | flops 3221225472 | bytes 4194304 | tf_op jit(solution)/shard_map/flow_parts/pallas_call | solution.py:200
  24.0 1.5 %collective-permute-done.7 = bf16[576,128]{1,0:T(8,128)(2,1)S(1)} collective-permute-done((bf16[576,128]{1,0:T(8,128)(2,1)S(1)}, bf16[576,128]{1,0:T(8,128)(2,1)S(1)}, u32[]{:S(2)}, u32[]{:S(2)}) %collective-permute-start.7) | collective-permute-done | bytes 147488 | tf_op jit(solution)/shard_map/ppermute | solution.py:458
  25.6 1.6 %collective-permute-done.8.far_ref = bf16[1152,128]{1,0:T(8,128)(2,1)S(1)} collective-permute-done((bf16[1152,128]{1,0:T(8,128)(2,1)S(1)}, bf16[1152,128]{1,0:T(8,128)(2,1)S(1)}, u32[]{:S(2)}, u32[]{:S(2)}) %collective-permute-start.8) | collective-permute-done | bytes 294944 | tf_op jit(solution)/shard_map/ppermute | solution.py:458
  27.2 5.7 %wall_and_residual.1 = (bf16[270,1024]{1,0:T(8,128)(2,1)}, f32[3,8,128]{2,1,0:T(8,128)}) custom-call(bf16[1152,128]{1,0:T(8,128)(2,1)S(1)} %constant_dynamic-update-slice_fusion.near_ref, bf16[1152,128]{1,0:T(8,128)(2,1)S(1)} %collective-permute-done.8.far_ref, f32[4,1024]{1,0:T(4,128)S(1)} %copy-done.4, f32[1,1024]{1,0:T(1,128)S(1)} %bitcast.7, ...), custom_call_target="tpu_custom_call" | custom-call | flops 4294967296 | bytes 8388608 | tf_op jit(solution)/shard_map/wall_and_residual/pallas_call | solution.py:408
  (40 shorter events, 0.2 us)
Async XLA Ops:
  2.1 7.4 %collective-permute-start = (bf16[72,128]{1,0:T(8,128)(2,1)S(1)}, bf16[72,128]{1,0:T(8,128)(2,1)S(1)}, u32[]{:S(2)}, u32[]{:S(2)}) collective-permute-start(bf16[72,128]{1,0:T(8,128)(2,1)S(1)} %maximum_bitcast_fusion), channel_id=1, source_target_pairs={{0,4},{1,5},{2,6},{3,7},{4,0},{5,1},{6,2},{7,3},{8,12},{9,13},{10,... | collective-permute-start | bytes 55304 | tf_op jit(solution)/shard_map/ppermute | solution.py:458
  6.1 1.1 %copy-start = (bf16[270,1024]{1,0:T(8,128)(2,1)S(1)}, bf16[270,1024]{1,0:T(8,128)(2,1)}, u32[]{:S(2)}) copy-start(bf16[270,1024]{1,0:T(8,128)(2,1)} %state_ref.3) | copy-start | bytes 1658884
  7.2 1.0 %copy-start.7 = (bf16[576,256]{1,0:T(8,128)(2,1)S(1)}, bf16[576,256]{1,0:T(8,128)(2,1)}, u32[]{:S(2)}) copy-start(bf16[576,256]{1,0:T(8,128)(2,1)} %constant.14.picks_ref) | copy-start | bytes 884740
  8.1 0.7 %copy-start.11 = (bf16[96,14]{1,0:T(8,128)(2,1)S(1)}, bf16[96,14]{1,0:T(8,128)(2,1)}, u32[]{:S(2)}) copy-start(bf16[96,14]{1,0:T(8,128)(2,1)} %constant.17.late_ref) | copy-start | bytes 8068
  8.9 4.7 %copy-start.12 = (bf16[4,270,270]{2,0,1:T(4,128)(2,1)S(1)}, bf16[4,270,270]{2,0,1:T(4,128)(2,1)}, u32[]{:S(2)}) copy-start(bf16[4,270,270]{2,0,1:T(4,128)(2,1)} %param.19) | copy-start | bytes 1749604
  9.4 4.2 %copy-start.13 = (bf16[6,2,5,5]{0,1,3,2:T(2,128)(2,1)S(1)}, bf16[6,2,5,5]{0,1,3,2:T(2,128)(2,1)}, u32[]{:S(2)}) copy-start(bf16[6,2,5,5]{0,1,3,2:T(2,128)(2,1)} %param.21) | copy-start | bytes 1804
  9.4 7.1 %copy-start.2 = (bf16[6,270,90]{2,1,0:T(8,128)(2,1)S(1)}, bf16[6,270,90]{2,1,0:T(8,128)(2,1)}, u32[]{:S(2)}) copy-start(bf16[6,270,90]{2,1,0:T(8,128)(2,1)} %lift_ref) | copy-start | bytes 874804
  9.4 7.0 %copy-start.3 = (s32[6,1024]{1,0:T(8,128)S(1)}, s32[6,1024]{1,0:T(8,128)}, u32[]{:S(2)}) copy-start(s32[6,1024]{1,0:T(8,128)} %nbr_ref.3) | copy-start | bytes 73732
  9.4 7.0 %copy-start.8 = (bf16[60,1152]{1,0:T(8,128)(2,1)S(1)}, bf16[60,1152]{1,0:T(8,128)(2,1)}, u32[]{:S(2)}) copy-start(bf16[60,1152]{1,0:T(8,128)(2,1)} %constant.10.clone.right_ref) | copy-start | bytes 414724
  9.5 7.0 %copy-start.9 = (f32[96,192]{1,0:T(8,128)S(1)}, f32[96,192]{1,0:T(8,128)}, u32[]{:S(2)}) copy-start(f32[96,192]{1,0:T(8,128)} %constant.11.clone.same_ref) | copy-start | bytes 221188
  9.5 7.0 %copy-start.10 = (bf16[96,5]{1,0:T(8,128)(2,1)S(1)}, bf16[96,5]{1,0:T(8,128)(2,1)}, u32[]{:S(2)}) copy-start(bf16[96,5]{1,0:T(8,128)(2,1)} %constant.9.clone.left_ref) | copy-start | bytes 2884
  9.5 4.0 %collective-permute-start.1 = (bf16[144,128]{1,0:T(8,128)(2,1)S(1)}, bf16[144,128]{1,0:T(8,128)(2,1)S(1)}, u32[]{:S(2)}, u32[]{:S(2)}) collective-permute-start(bf16[144,128]{1,0:T(8,128)(2,1)S(1)} %pad_maximum_fusion.2), channel_id=1, source_target_pairs={{0,2},{1,3},{2,0},{3,1},{4,6},{5,7},{6,4},{7,5},{8,10},{9,11},{10,... | collective-permute-start | bytes 110600 | tf_op jit(solution)/shard_map/ppermute | solution.py:458
  11.2 2.0 %collective-permute-start.2 = (bf16[96,128]{1,0:T(8,128)(2,1)S(1)}, bf16[96,128]{1,0:T(8,128)(2,1)S(1)}, u32[]{:S(2)}, u32[]{:S(2)}) collective-permute-start(bf16[96,128]{1,0:T(8,128)(2,1)S(1)} %get-tuple-element.39), channel_id=1, source_target_pairs={{0,8},{16,24},{8,0},{24,16},{1,9},{17,25},{9,1},{25,17},{2,10},{18... | collective-permute-start | bytes 73736 | tf_op jit(solution)/shard_map/ppermute | solution.py:433
  11.2 7.3 %collective-permute-start.5 = (bf16[96,128]{1,0:T(8,128)(2,1)S(1)}, bf16[96,128]{1,0:T(8,128)(2,1)S(1)}, u32[]{:S(2)}, u32[]{:S(2)}) collective-permute-start(bf16[96,128]{1,0:T(8,128)(2,1)S(1)} %get-tuple-element.38), channel_id=1, source_target_pairs={{1,2},{3,4},{5,6},{7,0},{2,1},{4,3},{6,5},{0,7},{9,10},{11,12},{13... | collective-permute-start | bytes 73736 | tf_op jit(solution)/shard_map/ppermute | solution.py:433
  13.9 7.0 %copy-start.1 = (bf16[270,1024]{1,0:T(8,128)(2,1)S(1)}, bf16[270,1024]{1,0:T(8,128)(2,1)}, u32[]{:S(2)}) copy-start(bf16[270,1024]{1,0:T(8,128)(2,1)} %state_ref.3) | copy-start | bytes 1658884
  13.9 5.5 %collective-permute-start.3 = (bf16[288,128]{1,0:T(8,128)(2,1)S(1)}, bf16[288,128]{1,0:T(8,128)(2,1)S(1)}, u32[]{:S(2)}, u32[]{:S(2)}) collective-permute-start(bf16[288,128]{1,0:T(8,128)(2,1)S(1)} %pad_maximum_fusion.1), channel_id=1, source_target_pairs={{0,1},{1,0},{2,3},{3,2},{4,5},{5,4},{6,7},{7,6},{8,9},{9,8},{10,11... | collective-permute-start | bytes 221192 | tf_op jit(solution)/shard_map/ppermute | solution.py:458
  15.5 3.8 %collective-permute-start.4 = (bf16[96,128]{1,0:T(8,128)(2,1)S(1)}, bf16[96,128]{1,0:T(8,128)(2,1)S(1)}, u32[]{:S(2)}, u32[]{:S(2)}) collective-permute-start(bf16[96,128]{1,0:T(8,128)(2,1)S(1)} %get-tuple-element.42), channel_id=1, source_target_pairs={{0,1},{2,3},{4,5},{6,7},{1,0},{3,2},{5,4},{7,6},{8,9},{10,11},{12,... | collective-permute-start | bytes 73736 | tf_op jit(solution)/shard_map/ppermute | solution.py:433
  16.0 3.4 %collective-permute-start.6 = (bf16[96,128]{1,0:T(8,128)(2,1)S(1)}, bf16[96,128]{1,0:T(8,128)(2,1)S(1)}, u32[]{:S(2)}, u32[]{:S(2)}) collective-permute-start(bf16[96,128]{1,0:T(8,128)(2,1)S(1)} %get-tuple-element.44), channel_id=1, source_target_pairs={{8,16},{24,0},{16,8},{0,24},{9,17},{25,1},{17,9},{1,25},{10,18},{2... | collective-permute-start | bytes 73736 | tf_op jit(solution)/shard_map/ppermute | solution.py:433
  19.5 6.0 %collective-permute-start.7 = (bf16[576,128]{1,0:T(8,128)(2,1)S(1)}, bf16[576,128]{1,0:T(8,128)(2,1)S(1)}, u32[]{:S(2)}, u32[]{:S(2)}) collective-permute-start(bf16[576,128]{1,0:T(8,128)(2,1)S(1)} %pad_maximum_fusion), channel_id=1, source_target_pairs={{0,16},{8,24},{16,0},{24,8},{1,17},{9,25},{17,1},{25,9},{2,18},{10... | collective-permute-start | bytes 442376 | tf_op jit(solution)/shard_map/ppermute | solution.py:458
  20.9 6.3 %copy-start.4 = (f32[4,1024]{1,0:T(4,128)S(1)}, f32[4,1024]{1,0:T(4,128)}, u32[]{:S(2)}) copy-start(f32[4,1024]{1,0:T(4,128)} %base_ref.1) | copy-start | bytes 49156
  20.9 6.3 %copy-start.5 = (f32[1024]{0:T(1024)S(1)}, f32[1024]{0:T(1024)}, u32[]{:S(2)}) copy-start(f32[1024]{0:T(1024)} %param.16) | copy-start | bytes 12292
  20.9 6.3 %copy-start.6 = (s32[1024]{0:T(1024)S(1)}, s32[1024]{0:T(1024)}, u32[]{:S(2)}) copy-start(s32[1024]{0:T(1024)} %param.17) | copy-start | bytes 12292
  25.5 1.6 %collective-permute-start.8 = (bf16[1152,128]{1,0:T(8,128)(2,1)S(1)}, bf16[1152,128]{1,0:T(8,128)(2,1)S(1)}, u32[]{:S(2)}, u32[]{:S(2)}) collective-permute-start(bf16[1152,128]{1,0:T(8,128)(2,1)S(1)} %constant_dynamic-update-slice_fusion.near_ref), channel_id=1, source_target_pairs={{0,8},{8,0},{16,24},{24,16},{1,9},{9,1},{17,25},{25,17},{2,10},{10... | collective-permute-start | bytes 884744 | tf_op jit(solution)/shard_map/ppermute | solution.py:458

commit v3 on v2

--- a/solution.py
+++ b/solution.py
@@ -20,14 +20,6 @@
 def face_rows(face):
     rows = np.arange(NV * 54).reshape(NV * 2, 3, 3, 3)
     return np.take(rows, 0 if face % 2 == 0 else 2, axis=1 + face // 2).reshape(-1)
-
-
-def picker(faces, unknowns):
-    picks = np.zeros((len(faces) * SLOT, unknowns), np.float32)
-    for slot, face in enumerate(faces):
-        rows = face_rows(face)
-        picks[slot * SLOT + np.arange(rows.size), rows] = 1
-    return jnp.asarray(picks, jnp.bfloat16)
 
 
 def kron_parts(sides):
@@ -53,27 +45,51 @@
 
 VMEM = pl.BlockSpec(memory_space=pltpu.VMEM)
 
+HBM = pl.BlockSpec(memory_space=pltpu.HBM)
+
 
 def odd(axis):
     return lax.rem(lax.axis_index(axis), 2) == 1
 
 
-def trace_kernel(state_ref, picks_ref, late_ref, trace_ref, *head_refs):
+def picks(face, rows, columns):
+    shape = (rows.stop - rows.start, columns.stop - columns.start)
+    row = lax.broadcasted_iota(jnp.int32, shape, 0) + rows.start
+    column = lax.broadcasted_iota(jnp.int32, shape, 1) + columns.start
+    group = lax.shift_right_logical(row * 57, 9)
+    inner = row - 9 * group
+    upper = lax.shift_right_logical(inner * 11, 5)
+    side = 2 * (face % 2)
+    if face // 2 == 0:
+        within = 9 * side + inner
+    elif face // 2 == 1:
+        within = 9 * upper + 3 * side + inner - 3 * upper
+    else:
+        within = 3 * inner + side
+    hit = (column == 27 * group + within) & (row < NV * NODES)
+    return jnp.where(hit, 1.0, 0.0).astype(jnp.bfloat16)
+
+
+def trace_kernel(state_ref, trace_ref, *refs):
+    head_refs = refs[:4]
+    main_ref, late_ref = refs[4:]
     unknowns, count = state_ref.shape
     width = head_refs[0].shape[1]
     early = min(unknowns, WIDE)
-    tail = SLOT - late_ref.shape[0] // 6
+    tail = late_rows(unknowns)
+    rest = SLOT - tail
+    for face in range(6):
+        main_ref[face * SLOT : (face + 1) * SLOT, :] = picks(face, range(SLOT), range(early))
+        late_ref[face * rest : (face + 1) * rest, :] = picks(face, range(tail, SLOT), range(early, unknowns))
     for chunk in range(count // WIDE):
         cols = slice(chunk * WIDE, (chunk + 1) * WIDE)
-        picked = dot(picks_ref[...], state_ref[:early, cols])
+        main = dot(main_ref[...], state_ref[:early, cols])
         late = dot(late_ref[...], state_ref[early:, cols])
-        rest = SLOT - tail
         for face in range(6):
             first = face * SLOT
-            low = picked[first : first + tail].astype(jnp.bfloat16)
-            high = (picked[first + tail : first + SLOT] + late[face * rest : (face + 1) * rest]).astype(jnp.bfloat16)
-            trace_ref[face, chunk, :tail, :] = low
-            trace_ref[face, chunk, tail:, :] = high
+            trace_ref[face, chunk, :tail, :] = main[first : first + tail].astype(jnp.bfloat16)
+            both = main[first + tail : first + SLOT] + late[face * rest : (face + 1) * rest]
+            trace_ref[face, chunk, tail:, :] = both.astype(jnp.bfloat16)
     for axis, which in enumerate(BOTH[::-1]):
         flip = odd(which)
         low, high = (trace_ref[2 * axis + side, 0, :, :width] for side in range(2))
@@ -81,23 +97,28 @@
         head_refs[2 * axis + 1][...] = jnp.where(flip, high, low)
 
 
+def late_rows(unknowns):
+    rows = np.stack([face_rows(face) for face in range(6)])
+    return int(np.nonzero((rows >= min(unknowns, WIDE)).any(axis=0))[0][0]) // 16 * 16
+
+
 def all_traces(flow_state, head_count):
     unknowns, count = flow_state.shape
-    picks = picker(range(6), unknowns)
     early = min(unknowns, WIDE)
-    rows = np.concatenate([face_rows(face) for face in range(6)]).reshape(6, -1)
-    tail = int(np.nonzero((rows >= early).any(axis=0))[0][0]) // 16 * 16
-    late = picks.reshape(6, SLOT, unknowns)[:, tail:, early:].reshape(-1, unknowns - early)
+    shapes = [(6, count // WIDE, SLOT, WIDE)] + [(SLOT, head_count)] * 4
     return pl.pallas_call(
         trace_kernel,
-        in_specs=[VMEM] * 3,
+        in_specs=[VMEM],
         out_specs=[VMEM] * 5,
-        out_shape=[jax.ShapeDtypeStruct((6, count // WIDE, SLOT, WIDE), jnp.bfloat16)]
-        + [jax.ShapeDtypeStruct((SLOT, head_count), jnp.bfloat16)] * 4,
+        out_shape=[jax.ShapeDtypeStruct(shape, jnp.bfloat16) for shape in shapes],
+        scratch_shapes=[
+            pltpu.VMEM((6 * SLOT, early), jnp.bfloat16),
+            pltpu.VMEM((6 * (SLOT - late_rows(unknowns)), unknowns - early), jnp.bfloat16),
+        ],
         compiler_params=pltpu.CompilerParams(vmem_limit_bytes=24 << 20),
         cost_estimate=pl.CostEstimate(flops=1 << 30, bytes_accessed=4 << 20, transcendentals=0),
         name="all_traces",
-    )(flow_state, picks[:, :early], late)
+    )(flow_state)
 
 
 def chosen(index, rows):
@@ -160,7 +181,7 @@
 
 
 def flow_kernel(
-    state_ref, nbr_ref, trace_ref, local_ref, partner0, other0, partner1, other1, weights_ref, flux_mat_ref,
+    start, state_ref, nbr_ref, trace_ref, local_ref, partner0, other0, partner1, other1, weights_ref, flux_mat_ref,
     out_ref, remote_ref,
 ):
     unknowns, count = state_ref.shape
@@ -170,38 +191,46 @@
         remote_ref[2 * axis] = jnp.where(flip, partner[...], other[...])
         remote_ref[2 * axis + 1] = jnp.where(flip, other[...], partner[...])
 
-    def some(step, carry):
-        here = pl.ds(pl.multiple_of(step * WIDE, WIDE), WIDE)
-        fluxes = []
-        for face in range(6):
-            found = local_ref[face, :, here]
-            if face < 4:
-                index = nbr_ref[face : face + 1, here] - count
-                found += dot(remote_ref[face], chosen(index, remote_ref.shape[2])).astype(jnp.bfloat16)
-            sides = jnp.concatenate([trace_ref[face, step], found], axis=0)
-            fluxes.append(dot(flux_mat_ref[face], sides).astype(jnp.bfloat16))
-        own = state_ref[:, here]
-        own_padded = jnp.concatenate([own, jnp.zeros((first - unknowns, WIDE), jnp.bfloat16)], axis=0)
+    def some(pair, carry):
+        places = [pair * 2 + k for k in range(2)]
+        wheres = [pl.ds(pl.multiple_of((start + p) * WIDE, WIDE), WIDE) for p in places]
+        found = {}
+        for k, here in enumerate(wheres):
+            for face in range(6):
+                found[k, face] = local_ref[face, :, here]
+                if face < 4:
+                    index = nbr_ref[face : face + 1, here] - count
+                    found[k, face] += dot(remote_ref[face], chosen(index, remote_ref.shape[2])).astype(jnp.bfloat16)
+        fluxes = {}
+        for k, p in enumerate(places):
+            for face in range(6):
+                sides = jnp.concatenate([trace_ref[face, start + p], found[k, face]], axis=0)
+                fluxes[k, face] = dot(flux_mat_ref[face], sides).astype(jnp.bfloat16)
         gap = jnp.zeros((second - first - SLOT, WIDE), jnp.bfloat16)
-        for direction in range(4):
-            if direction < 3:
-                operand = jnp.concatenate([own_padded, fluxes[2 * direction], gap, fluxes[2 * direction + 1]], axis=0)
-                out_ref[direction, :, here] = dot(weights_ref[direction], operand)
-            else:
-                out_ref[direction, :, here] = dot(weights_ref[direction, :, :unknowns], own)
+        for k, p in enumerate(places):
+            there = pl.ds(pl.multiple_of(p * WIDE, WIDE), WIDE)
+            own = state_ref[:, wheres[k]]
+            own_padded = jnp.concatenate([own, jnp.zeros((first - unknowns, WIDE), jnp.bfloat16)], axis=0)
+            for direction in range(4):
+                if direction < 3:
+                    operand = [own_padded, fluxes[k, 2 * direction], gap, fluxes[k, 2 * direction + 1]]
+                    out_ref[direction, :, there] = dot(weights_ref[direction], jnp.concatenate(operand, axis=0))
+                else:
+                    out_ref[direction, :, there] = dot(weights_ref[direction, :, :unknowns], own)
         return carry
 
-    lax.fori_loop(0, count // WIDE, some, 0)
-
-
-def flow_parts(flow_state, face_nbr, traces, local, remotes, weights, flux_mat):
-    unknowns, count = flow_state.shape
+    for pair in range(out_ref.shape[2] // WIDE // 2):
+        some(pair, 0)
+
+
+def flow_parts(start, steps, flow_state, face_nbr, traces, local, remotes, weights, flux_mat):
+    unknowns = flow_state.shape[0]
     args = (flow_state, face_nbr, traces, local, *remotes, weights, flux_mat)
     return pl.pallas_call(
-        flow_kernel,
+        functools.partial(flow_kernel, start),
         in_specs=[VMEM] * len(args),
         out_specs=VMEM,
-        out_shape=jax.ShapeDtypeStruct((4, unknowns, count), jnp.float32),
+        out_shape=jax.ShapeDtypeStruct((4, unknowns, steps * WIDE), jnp.float32),
         scratch_shapes=[pltpu.VMEM((4, *remotes[0].shape), jnp.bfloat16)],
         compiler_params=pltpu.CompilerParams(vmem_limit_bytes=32 << 20),
         cost_estimate=pl.CostEstimate(flops=3 << 30, bytes_accessed=4 << 20, transcendentals=0),
@@ -216,13 +245,14 @@
 
 
 def wall_kernel(
-    masks, rows, own_rows,
-    near_ref, far_ref, base_ref, follow_ref, anchor_ref, parts_ref, residual_ref, disp_ref,
+    masks, kind_bits, rows, own_rows,
+    near_ref, far_ref, base_ref, follow_ref, anchor_ref, parts0_ref, parts1_ref, residual_ref, disp_ref,
     disp, resid, applied, search, image, diag,
 ):
     comps = 3
     tiles = rows // TILE
     me = lax.axis_index(BOTH)
+    flip = kind(me, kind_bits) == 1
 
     def strided(block):
         first = block * TILE
@@ -234,7 +264,7 @@
         ref, at = (near_ref, pair) if pair < half // 2 else (far_ref, pair - half // 2)
         both = ref[2 * at * each : 2 * (at + 1) * each, :].astype(jnp.float32)
         for slot in range(2):
-            device = jnp.bitwise_xor(me, masks[2 * pair + slot])
+            device = jnp.bitwise_xor(me, jnp.where(flip, masks[1][2 * pair + slot], masks[0][2 * pair + slot]))
             upper, lower, stiff = (both[slot * each + k * comps * own_rows :][: comps * own_rows] for k in range(3))
             load = upper + lower
             for block in range(own_rows // TILE):
@@ -386,28 +416,33 @@
             out.append(sums[c] + jnp.sum(found, axis=0))
         return tuple(out)
 
-    sums = lax.fori_loop(0, rows // some_rows, look, (jnp.zeros((TILE, count), jnp.float32),) * comps)
+    sums = (jnp.zeros((TILE, count), jnp.float32),) * comps
+    sums = lax.fori_loop(0, rows // some_rows, look, sums, unroll=rows // some_rows <= 4)
     follow = follow_ref[...]
     geometry = [
         base_ref[c : c + 1, :] * jnp.exp(follow * jnp.sum(sums[c], axis=0, keepdims=True)) for c in range(comps)
     ]
     geometry.append(base_ref[comps : comps + 1, :])
     unknowns = residual_ref.shape[0]
-    for first in range(0, unknowns, 16):
-        some = slice(first, min(first + 16, unknowns))
-        value = geometry[0] * parts_ref[0, some, :]
-        for direction in range(1, 4):
-            value += geometry[direction] * parts_ref[direction, some, :]
-        residual_ref[some, :] = value.astype(jnp.bfloat16)
-
-
-def wall_and_residual(near, far, masks, base_geometry, anchor_weight, wall_anchor, parts, own_rows):
-    rows = own_rows * len(masks)
-    _, unknowns, count = parts.shape
+    begin = 0
+    for parts_ref in (parts0_ref, parts1_ref):
+        cols = slice(begin, begin + parts_ref.shape[2])
+        begin = cols.stop
+        for first in range(0, unknowns, 16):
+            some = slice(first, min(first + 16, unknowns))
+            value = geometry[0][:, cols] * parts_ref[0, some, :]
+            for direction in range(1, 4):
+                value += geometry[direction][:, cols] * parts_ref[direction, some, :]
+            residual_ref[some, cols] = value.astype(jnp.bfloat16)
+
+
+def wall_and_residual(near, far, masks, kind_bits, base_geometry, anchor_weight, wall_anchor, parts, own_rows):
+    rows = own_rows * len(masks[0])
+    unknowns, count = parts[0].shape[1], anchor_weight.shape[0]
     field = pltpu.VMEM((3, rows, 128), jnp.float32)
     return pl.pallas_call(
-        functools.partial(wall_kernel, masks, rows, own_rows),
-        in_specs=[VMEM] * 6,
+        functools.partial(wall_kernel, masks, kind_bits, rows, own_rows),
+        in_specs=[VMEM] * 7,
         out_specs=[VMEM] * 2,
         out_shape=[
             jax.ShapeDtypeStruct((unknowns, count), jnp.bfloat16),
@@ -424,7 +459,7 @@
         compiler_params=pltpu.CompilerParams(vmem_limit_bytes=(16 << 20) + 16 * rows * 3 * 128 * 4),
         cost_estimate=pl.CostEstimate(flops=4 << 30, bytes_accessed=8 << 20, transcendentals=0),
         name="wall_and_residual",
-    )(near, far, base_geometry, anchor_weight[None, :], wall_anchor[None, :], parts)
+    )(near, far, base_geometry, anchor_weight[None, :], wall_anchor[None, :], *parts)
 
 
 def paired(x, axis, offset):
@@ -434,60 +469,74 @@
 
 
 def gather_stages(mesh):
-    def bits(axis):
-        assert mesh.shape[axis] & (mesh.shape[axis] - 1) == 0
-        return [(axis, 1 << b) for b in reversed(range(mesh.shape[axis].bit_length() - 1))]
-
-    return bits("dom") + bits("sec")
+    n_sec, n_dom = mesh.shape["sec"], mesh.shape["dom"]
+    assert n_sec & (n_sec - 1) == 0 and n_dom & (n_dom - 1) == 0 and n_sec > 1
+    bits = [1 << b for b in range((n_sec * n_dom).bit_length() - 1)]
+    inner, outer = bits[: n_dom.bit_length() - 1], bits[n_dom.bit_length() :]
+    order = inner[::-1] + outer[::-1]
+    first = [bit ^ n_dom for bit in order]
+    second = first[:-2] + first[-2:][::-1]
+    return (first + [n_dom], second + [n_dom]), order[-2:] + [n_dom]
+
+
+def kind(device, bits):
+    return sum(device // bit % 2 for bit in bits) % 2
 
 
 def on_device(
-    stages, n_dom,
+    stages, kind_bits,
     flow_state, base_geometry, anchor_weight, wall_anchor, face_nbr, volume_ops, lift_ops, face_jac, wall_load, wall_stiff,
 ):
     own_rows, width = wall_load.shape[1:]
-    upper = lax.reduce_precision(wall_load, 8, 7)
-    wall = jnp.concatenate([upper, wall_load - upper, wall_stiff], axis=0).astype(jnp.bfloat16)
-    wall = wall.reshape(9 * own_rows, width)
-    masks = [0]
-    for axis, bit in stages:
-        masks += [m ^ (bit * n_dom if axis == "sec" else bit) for m in masks]
+    wall = jnp.concatenate([wall_load, wall_load, wall_stiff], axis=0).reshape(9 * own_rows, width)
+    third = lax.broadcasted_iota(jnp.int32, wall.shape, 0) // (3 * own_rows)
+    wall = jnp.where(third == 1, wall - lax.reduce_precision(wall, 8, 7), wall).astype(jnp.bfloat16)
+    masks = []
+    for bits in stages:
+        masks.append([0])
+        for bit in bits[:-1]:
+            masks[-1] += [m ^ bit for m in masks[-1]]
+    masks = [ours + [m ^ stages[0][-1] for m in theirs] for ours, theirs in (masks, masks[::-1])]
+    devices = lax.axis_size(BOTH)
 
     def sent(wall, position):
-        axis, bit = stages[position]
-        return lax.ppermute(wall, axis, [(i, i ^ bit) for i in range(lax.axis_size(axis))])
+        pairs = [(i, i ^ stages[kind(i, kind_bits)][position]) for i in range(devices)]
+        return lax.ppermute(wall, BOTH, pairs)
 
     barrier = lax.optimization_barrier
     far = sent(wall, 0)
     head_count = flow_state.shape[1] // 8
     traces, *heads = all_traces(flow_state, head_count)
-    far, traces, heads = barrier((far, traces, heads))
+    far, heads = barrier((far, heads))
     wall = jnp.concatenate([wall, far], axis=0)
     far = sent(wall, 1)
     remotes = [None] * 4
     remotes[2] = paired(heads[2], "sec", 0)
-    remotes[1] = paired(heads[1], "dom", 1)
-    far, heads, remotes[2], volume_ops, lift_ops, face_jac = barrier((far, heads, remotes[2], volume_ops, lift_ops, face_jac))
+    remotes[0] = paired(heads[0], "dom", 0)
+    far, heads = barrier((far, heads))
     wall = jnp.concatenate([wall, far], axis=0)
     far = sent(wall, 2)
-    remotes[0] = paired(heads[0], "dom", 0)
+    remotes[1] = paired(heads[1], "dom", 1)
     remotes[3] = paired(heads[3], "sec", 1)
+    far, traces, volume_ops, face_jac, remotes[0], remotes[2] = barrier((far, traces, volume_ops, face_jac, remotes[0], remotes[2]))
+    wall = jnp.concatenate([wall, far], axis=0)
     jac = face_jac.transpose(2, 0, 1, 3).reshape(NV, 12 * NV)
+    far = sent(wall, 3)
     local, weights, flux_mat = local_traces(traces, face_nbr, volume_ops, lift_ops, jac)
-    far, remotes, local = barrier((far, remotes, local))
-    wall = jnp.concatenate([wall, far], axis=0)
-    far = sent(wall, 3)
-    parts = flow_parts(flow_state, face_nbr, traces, local, remotes, weights, flux_mat)
-    far, parts = barrier((far, parts))
-    for position in range(4, len(stages)):
+    chunks = traces.shape[1]
+    halves = []
+    halves.append(flow_parts(0, chunks // 2, flow_state, face_nbr, traces, local, remotes, weights, flux_mat))
+    far, local, halves = barrier((far, local, halves))
+    for position in range(4, len(stages[0])):
         wall = jnp.concatenate([wall, far], axis=0)
         far = sent(wall, position)
-    return wall_and_residual(wall, far, masks, base_geometry, anchor_weight, wall_anchor, parts, own_rows)
+    halves.append(flow_parts(chunks // 2, chunks // 2, flow_state, face_nbr, traces, local, remotes, weights, flux_mat))
+    return wall_and_residual(wall, far, masks, kind_bits, base_geometry, anchor_weight, wall_anchor, halves, own_rows)
 
 
 def solution(mesh):
     return jax.shard_map(
-        functools.partial(on_device, gather_stages(mesh), mesh.shape["dom"]),
+        functools.partial(on_device, *gather_stages(mesh)),
         mesh=mesh,
         in_specs=(
             P(None, BOTH),

time: 33.2 us -> 30 us (0.904)
  starting transfers between devices: 11.7 us -> 15.8 us
  waiting for transfers between devices: 4.53 us -> 0.43 us
  local copies, waits for them, and re-layouts: 3.23 us -> 1.54 us
  Pallas kernels: 11.1 us -> 10.1 us
  other arithmetic: 1.45 us -> 0.92 us
    ppermute x4, starting transfers between devices: 2.99 us -> 6.61 us  [paired(): return lax.ppermute(x, axis, pairs + [pair[::-1] for pair in pairs])]
    ppermute x5, waiting for transfers between devices: 3.49 us -> 0.42 us  [sent(): return lax.ppermute(wall, BOTH, pairs)]
    unnamed x31 -> x27, local copies, waits for them, and re-layouts: 2.85 us -> 1.15 us
    another operation x2 -> x0, other arithmetic: 1.42 us -> none
    pallas_call x3 -> x4, Pallas kernels: 9.23 us -> 8.18 us  [the longest x1 5.43 us: wall_and_residual(): pl.pallas_call(functools.partial(wall_kernel, masks, kind_bits, rows, own...]
    ppermute x4, waiting for transfers between devices: 1.04 us -> 0.01 us  [paired(): return lax.ppermute(x, axis, pairs + [pair[::-1] for pair in pairs])]
    unnamed x1, other arithmetic: 0.01 us -> 0.88 us
    ppermute x5, starting transfers between devices: 8.72 us -> 9.23 us  [sent(): return lax.ppermute(wall, BOTH, pairs)]
  transfers between devices with their start and end apart: 9 -> 9, of which waited for: 5 -> 2; matrix products, arithmetic and copies ran while one was open for 1% -> 1% of each run, Pallas kernels for 17% -> 16%
where the time goes in v3:
time: 30 us; the launch traced here: 29.7 us
  starting transfers between devices  15.8 us (53%)
  Pallas kernels  10.1 us (34%)
  local copies, waits for them, and re-layouts  1.54 us (5%)
  other arithmetic  0.92 us (3%)
  between operations  0.89 us (3%)
  waiting for transfers between devices  0.43 us (1%)
    ppermute x5, starting transfers between devices, sent(): return lax.ppermute(wall, BOTH, pairs)  9.23 us
    ppermute x4, starting transfers between devices, paired(): return lax.ppermute(x, axis, pairs + [pair[::-1] for pair in pairs])  6.61 us
    pallas_call x1, Pallas kernels, wall_and_residual(): pl.pallas_call(functools.partial(wall_kernel, masks, kind_bits, rows, own...  5.43 us
    pallas_call x2, Pallas kernels, flow_parts(): pl.pallas_call(functools.partial(flow_kernel, start), in_specs=[VMEM] * l...  2.17 us
    pallas_call x1, Pallas kernels, local_traces(): pl.pallas_call(local_kernel, in_specs=[VMEM] * len(args), out_specs=[VMEM...  1.92 us
    unnamed x27, local copies, waits for them, and re-layouts  1.15 us
    unnamed x1, other arithmetic  0.88 us
  transfers between devices with their start and end apart: 9, of which 2 were waited for; matrix products, arithmetic and copies ran while one was open for 1% of the time, Pallas kernels for 16%

profile of v3, /device:TPU:0, one launch (start us, length us, event | category | flops | bytes accessed | tf_op | source)
XLA Modules:
  0.0 29.7 jit_solution(13484979626639916806)
XLA Ops:
  0.7 0.9 %constant_dynamic-update-slice_fusion.4 = (bf16[1152,128]{1,0:T(8,128)(2,1)S(1)}, bf16[72,128]{1,0:T(8,128)(2,1)S(1)}) fusion(f32[3,8,128]{2,1,0:T(8,128)} %param.22, f32[3,8,128]{2,1,0:T(8,128)} %param.21, s32[72]{0:T(128)S(1)} %get-tuple-element.54, s32[72]{0:T(128)S(1)} %get-tuple-element.55, pred[72]{0:T(512)(128)(4,1)S(1)} %compare_and_fusion), kind=kLoop, calls=%fused_computation.11 | loop fusion | flops 73727 | bytes 62088
  1.5 3.5 %collective-permute-start = (bf16[72,128]{1,0:T(8,128)(2,1)S(1)}, bf16[72,128]{1,0:T(8,128)(2,1)S(1)}, u32[]{:S(2)}, u32[]{:S(2)}) collective-permute-start(bf16[72,128]{1,0:T(8,128)(2,1)S(1)} %get-tuple-element.53), channel_id=1, source_target_pairs={{0,12},{1,13},{2,14},{3,15},{4,8},{5,9},{6,10},{7,11},{8,4},{9,5},... | collective-permute-start | bytes 55304 | tf_op jit(solution)/shard_map/ppermute | solution.py:504
  5.1 1.1 %copy-done = bf16[270,1024]{1,0:T(8,128)(2,1)S(1)} copy-done((bf16[270,1024]{1,0:T(8,128)(2,1)S(1)}, bf16[270,1024]{1,0:T(8,128)(2,1)}, u32[]{:S(2)}) %copy-start) | copy-done | bytes 552984
  6.1 0.6 %all_traces.1 = (bf16[6,4,96,256]{3,2,1,0:T(8,128)(2,1)S(1)}, bf16[96,128]{1,0:T(8,128)(2,1)S(1)}, bf16[96,128]{1,0:T(8,128)(2,1)S(1)}, bf16[96,128]{1,0:T(8,128)(2,1)S(1)}, bf16[96,128]{1,0:T(8,128)(2,1)S(1)}) custom-call(bf16[270,1024]{1,0:T(8,128)(2,1)S(1)} %copy-done), custom_call_target="tpu_custom_call" | custom-call | flops 1073741824 | bytes 4194304 | tf_op jit(solution)/shard_map/all_traces/pallas_call | solution.py:109
  6.7 0.0 copy-start.2
  6.7 0.0 copy-start.7
  6.8 0.0 copy-start.8
  6.8 0.0 copy-start.9
  6.8 1.9 %collective-permute-start.1 = (bf16[144,128]{1,0:T(8,128)(2,1)S(1)}, bf16[144,128]{1,0:T(8,128)(2,1)S(1)}, u32[]{:S(2)}, u32[]{:S(2)}) collective-permute-start(bf16[144,128]{1,0:T(8,128)(2,1)S(1)} %pad_maximum_fusion.2), channel_id=1, source_target_pairs={{0,10},{1,11},{2,8},{3,9},{4,14},{5,15},{6,12},{7,13},{8,2},{9,3},... | collective-permute-start | bytes 110600 | tf_op jit(solution)/shard_map/ppermute | solution.py:504
  8.8 1.5 %collective-permute-start.3 = (bf16[96,128]{1,0:T(8,128)(2,1)S(1)}, bf16[96,128]{1,0:T(8,128)(2,1)S(1)}, u32[]{:S(2)}, u32[]{:S(2)}) collective-permute-start(bf16[96,128]{1,0:T(8,128)(2,1)S(1)} %get-tuple-element.32), channel_id=1, source_target_pairs={{0,1},{2,3},{4,5},{6,7},{1,0},{3,2},{5,4},{7,6},{8,9},{10,11},{12,... | collective-permute-start | bytes 73736 | tf_op jit(solution)/shard_map/ppermute | solution.py:468
  10.3 0.1 collective-permute-done.1
  10.4 1.7 %collective-permute-start.2 = (bf16[288,128]{1,0:T(8,128)(2,1)S(1)}, bf16[288,128]{1,0:T(8,128)(2,1)S(1)}, u32[]{:S(2)}, u32[]{:S(2)}) collective-permute-start(bf16[288,128]{1,0:T(8,128)(2,1)S(1)} %pad_maximum_fusion.1), channel_id=1, source_target_pairs={{0,9},{1,25},{2,11},{3,27},{4,13},{5,29},{6,15},{7,31},{8,16},{9,0... | collective-permute-start | bytes 221192 | tf_op jit(solution)/shard_map/ppermute | solution.py:504
  12.1 5.1 %collective-permute-start.6 = (bf16[96,128]{1,0:T(8,128)(2,1)S(1)}, bf16[96,128]{1,0:T(8,128)(2,1)S(1)}, u32[]{:S(2)}, u32[]{:S(2)}) collective-permute-start(bf16[96,128]{1,0:T(8,128)(2,1)S(1)} %get-tuple-element.44), channel_id=1, source_target_pairs={{1,2},{3,4},{5,6},{7,0},{2,1},{4,3},{6,5},{0,7},{9,10},{11,12},{13... | collective-permute-start | bytes 73736 | tf_op jit(solution)/shard_map/ppermute | solution.py:468
  17.2 0.2 copy.17
  17.4 0.1 reshape.11.jac_ref
  17.5 1.8 %collective-permute-start.5 = (bf16[576,128]{1,0:T(8,128)(2,1)S(1)}, bf16[576,128]{1,0:T(8,128)(2,1)S(1)}, u32[]{:S(2)}, u32[]{:S(2)}) collective-permute-start(bf16[576,128]{1,0:T(8,128)(2,1)S(1)} %pad_maximum_fusion), channel_id=1, source_target_pairs={{0,24},{1,8},{2,26},{3,10},{4,28},{5,12},{6,30},{7,14},{8,1},{9,17... | collective-permute-start | bytes 442376 | tf_op jit(solution)/shard_map/ppermute | solution.py:504
  19.3 0.1 copy.18.volume_ref
  19.5 1.9 %local_traces.1 = (bf16[6,96,1024]{2,1,0:T(8,128)(2,1)S(1)}, bf16[4,270,480]{2,1,0:T(8,128)(2,1)S(1)}, bf16[6,96,192]{2,1,0:T(8,128)(2,1)S(1)}) custom-call(bf16[6,4,96,256]{3,2,1,0:T(8,128)(2,1)S(1)} %get-tuple-element.39.trace_ref, s32[6,1024]{1,0:T(8,128)S(1)} %copy-done.3, bf16[4,270,270]{2,1,0:T(8,128)(2,1)S(1)} %copy.18.volume_ref, ...), custom_call_target="tpu_custom_call" | custom-call | flops 2147483648 | bytes 4194304 | tf_op jit(solution)/shard_map/local_traces/pallas_call | solution.py:168
  21.4 1.1 %flow_parts.2.parts0_ref = f32[4,270,512]{2,1,0:T(8,128)S(1)} custom-call(bf16[270,1024]{1,0:T(8,128)(2,1)S(1)} %copy-done.1, s32[6,1024]{1,0:T(8,128)S(1)} %copy-done.3, bf16[6,4,96,256]{3,2,1,0:T(8,128)(2,1)S(1)} %get-tuple-element.39.trace_ref, bf16[6,96,1024]{2,1,0:T(8,128)(2,1)S(1)} %get-tuple-element.51.local_ref, ...), custom_call_target="tpu_custom_call" | custom-call | flops 3221225472 | bytes 4194304 | tf_op jit(solution)/shard_map/flow_parts/pallas_call | solution.py:229
  22.6 0.0 copy-start.5
  22.6 0.3 collective-permute-start.8
  22.9 1.1 %flow_parts.3.parts1_ref = f32[4,270,512]{2,1,0:T(8,128)S(1)} custom-call(bf16[270,1024]{1,0:T(8,128)(2,1)S(1)} %copy-done.1, s32[6,1024]{1,0:T(8,128)S(1)} %copy-done.3, bf16[6,4,96,256]{3,2,1,0:T(8,128)(2,1)S(1)} %get-tuple-element.39.trace_ref, bf16[6,96,1024]{2,1,0:T(8,128)(2,1)S(1)} %get-tuple-element.51.local_ref, ...), custom_call_target="tpu_custom_call" | custom-call | flops 3221225472 | bytes 4194304 | tf_op jit(solution)/shard_map/flow_parts/pallas_call | solution.py:229
  24.0 0.3 collective-permute-done.8.far_ref
  24.3 5.4 %wall_and_residual.1 = (bf16[270,1024]{1,0:T(8,128)(2,1)}, f32[3,8,128]{2,1,0:T(8,128)}) custom-call(bf16[1152,128]{1,0:T(8,128)(2,1)S(1)} %constant_dynamic-update-slice_fusion.near_ref, bf16[1152,128]{1,0:T(8,128)(2,1)S(1)} %collective-permute-done.8.far_ref, f32[4,1024]{1,0:T(4,128)S(1)} %copy-done.4, f32[1,1024]{1,0:T(1,128)S(1)} %bitcast.8, ...), custom_call_target="tpu_custom_call" | custom-call | flops 4294967296 | bytes 8388608 | tf_op jit(solution)/shard_map/wall_and_residual/pallas_call | solution.py:443
  (36 shorter events, 0.2 us)
Async XLA Ops:
  1.5 5.2 %collective-permute-start = (bf16[72,128]{1,0:T(8,128)(2,1)S(1)}, bf16[72,128]{1,0:T(8,128)(2,1)S(1)}, u32[]{:S(2)}, u32[]{:S(2)}) collective-permute-start(bf16[72,128]{1,0:T(8,128)(2,1)S(1)} %get-tuple-element.53), channel_id=1, source_target_pairs={{0,12},{1,13},{2,14},{3,15},{4,8},{5,9},{6,10},{7,11},{8,4},{9,5},... | collective-permute-start | bytes 55304 | tf_op jit(solution)/shard_map/ppermute | solution.py:504
  5.1 1.1 %copy-start = (bf16[270,1024]{1,0:T(8,128)(2,1)S(1)}, bf16[270,1024]{1,0:T(8,128)(2,1)}, u32[]{:S(2)}) copy-start(bf16[270,1024]{1,0:T(8,128)(2,1)} %state_ref.5) | copy-start | bytes 1658884
  6.1 11.1 %copy-start.11 = (bf16[6,2,5,5]{0,1,3,2:T(2,128)(2,1)S(1)}, bf16[6,2,5,5]{0,1,3,2:T(2,128)(2,1)}, u32[]{:S(2)}) copy-start(bf16[6,2,5,5]{0,1,3,2:T(2,128)(2,1)} %param.20) | copy-start | bytes 1804
  6.1 13.2 %copy-start.10 = (bf16[4,270,270]{2,0,1:T(4,128)(2,1)S(1)}, bf16[4,270,270]{2,0,1:T(4,128)(2,1)}, u32[]{:S(2)}) copy-start(bf16[4,270,270]{2,0,1:T(4,128)(2,1)} %param.18) | copy-start | bytes 1749604
  6.7 12.7 %copy-start.2 = (bf16[6,270,90]{2,1,0:T(8,128)(2,1)S(1)}, bf16[6,270,90]{2,1,0:T(8,128)(2,1)}, u32[]{:S(2)}) copy-start(bf16[6,270,90]{2,1,0:T(8,128)(2,1)} %lift_ref.1) | copy-start | bytes 874804
  6.7 12.7 %copy-start.3 = (s32[6,1024]{1,0:T(8,128)S(1)}, s32[6,1024]{1,0:T(8,128)}, u32[]{:S(2)}) copy-start(s32[6,1024]{1,0:T(8,128)} %nbr_ref.5) | copy-start | bytes 73732
  6.7 12.7 %copy-start.7 = (bf16[60,1152]{1,0:T(8,128)(2,1)S(1)}, bf16[60,1152]{1,0:T(8,128)(2,1)}, u32[]{:S(2)}) copy-start(bf16[60,1152]{1,0:T(8,128)(2,1)} %constant.19.clone.right_ref) | copy-start | bytes 414724
  6.8 12.7 %copy-start.8 = (f32[96,192]{1,0:T(8,128)S(1)}, f32[96,192]{1,0:T(8,128)}, u32[]{:S(2)}) copy-start(f32[96,192]{1,0:T(8,128)} %constant.20.clone.same_ref) | copy-start | bytes 221188
  6.8 12.7 %copy-start.9 = (bf16[96,5]{1,0:T(8,128)(2,1)S(1)}, bf16[96,5]{1,0:T(8,128)(2,1)}, u32[]{:S(2)}) copy-start(bf16[96,5]{1,0:T(8,128)(2,1)} %constant.18.clone.left_ref) | copy-start | bytes 2884
  6.8 3.6 %collective-permute-start.1 = (bf16[144,128]{1,0:T(8,128)(2,1)S(1)}, bf16[144,128]{1,0:T(8,128)(2,1)S(1)}, u32[]{:S(2)}, u32[]{:S(2)}) collective-permute-start(bf16[144,128]{1,0:T(8,128)(2,1)S(1)} %pad_maximum_fusion.2), channel_id=1, source_target_pairs={{0,10},{1,11},{2,8},{3,9},{4,14},{5,15},{6,12},{7,13},{8,2},{9,3},... | collective-permute-start | bytes 110600 | tf_op jit(solution)/shard_map/ppermute | solution.py:504
  8.8 8.4 %collective-permute-start.3 = (bf16[96,128]{1,0:T(8,128)(2,1)S(1)}, bf16[96,128]{1,0:T(8,128)(2,1)S(1)}, u32[]{:S(2)}, u32[]{:S(2)}) collective-permute-start(bf16[96,128]{1,0:T(8,128)(2,1)S(1)} %get-tuple-element.32), channel_id=1, source_target_pairs={{0,1},{2,3},{4,5},{6,7},{1,0},{3,2},{5,4},{7,6},{8,9},{10,11},{12,... | collective-permute-start | bytes 73736 | tf_op jit(solution)/shard_map/ppermute | solution.py:468
  10.3 6.9 %collective-permute-start.4 = (bf16[96,128]{1,0:T(8,128)(2,1)S(1)}, bf16[96,128]{1,0:T(8,128)(2,1)S(1)}, u32[]{:S(2)}, u32[]{:S(2)}) collective-permute-start(bf16[96,128]{1,0:T(8,128)(2,1)S(1)} %get-tuple-element.34), channel_id=1, source_target_pairs={{0,8},{16,24},{8,0},{24,16},{1,9},{17,25},{9,1},{25,17},{2,10},{18... | collective-permute-start | bytes 73736 | tf_op jit(solution)/shard_map/ppermute | solution.py:468
  10.4 6.8 %collective-permute-start.2 = (bf16[288,128]{1,0:T(8,128)(2,1)S(1)}, bf16[288,128]{1,0:T(8,128)(2,1)S(1)}, u32[]{:S(2)}, u32[]{:S(2)}) collective-permute-start(bf16[288,128]{1,0:T(8,128)(2,1)S(1)} %pad_maximum_fusion.1), channel_id=1, source_target_pairs={{0,9},{1,25},{2,11},{3,27},{4,13},{5,29},{6,15},{7,31},{8,16},{9,0... | collective-permute-start | bytes 221192 | tf_op jit(solution)/shard_map/ppermute | solution.py:504
  12.1 9.3 %collective-permute-start.6 = (bf16[96,128]{1,0:T(8,128)(2,1)S(1)}, bf16[96,128]{1,0:T(8,128)(2,1)S(1)}, u32[]{:S(2)}, u32[]{:S(2)}) collective-permute-start(bf16[96,128]{1,0:T(8,128)(2,1)S(1)} %get-tuple-element.44), channel_id=1, source_target_pairs={{1,2},{3,4},{5,6},{7,0},{2,1},{4,3},{6,5},{0,7},{9,10},{11,12},{13... | collective-permute-start | bytes 73736 | tf_op jit(solution)/shard_map/ppermute | solution.py:468
  17.2 4.2 %collective-permute-start.7 = (bf16[96,128]{1,0:T(8,128)(2,1)S(1)}, bf16[96,128]{1,0:T(8,128)(2,1)S(1)}, u32[]{:S(2)}, u32[]{:S(2)}) collective-permute-start(bf16[96,128]{1,0:T(8,128)(2,1)S(1)} %get-tuple-element.46), channel_id=1, source_target_pairs={{8,16},{24,0},{16,8},{0,24},{9,17},{25,1},{17,9},{1,25},{10,18},{2... | collective-permute-start | bytes 73736 | tf_op jit(solution)/shard_map/ppermute | solution.py:468
  17.5 5.0 %collective-permute-start.5 = (bf16[576,128]{1,0:T(8,128)(2,1)S(1)}, bf16[576,128]{1,0:T(8,128)(2,1)S(1)}, u32[]{:S(2)}, u32[]{:S(2)}) collective-permute-start(bf16[576,128]{1,0:T(8,128)(2,1)S(1)} %pad_maximum_fusion), channel_id=1, source_target_pairs={{0,24},{1,8},{2,26},{3,10},{4,28},{5,12},{6,30},{7,14},{8,1},{9,17... | collective-permute-start | bytes 442376 | tf_op jit(solution)/shard_map/ppermute | solution.py:504
  19.5 2.0 %copy-start.1 = (bf16[270,1024]{1,0:T(8,128)(2,1)S(1)}, bf16[270,1024]{1,0:T(8,128)(2,1)}, u32[]{:S(2)}) copy-start(bf16[270,1024]{1,0:T(8,128)(2,1)} %state_ref.5) | copy-start | bytes 1658884
  22.6 1.7 %copy-start.4 = (f32[4,1024]{1,0:T(4,128)S(1)}, f32[4,1024]{1,0:T(4,128)}, u32[]{:S(2)}) copy-start(f32[4,1024]{1,0:T(4,128)} %base_ref.1) | copy-start | bytes 49156
  22.6 1.7 %copy-start.5 = (f32[1024]{0:T(1024)S(1)}, f32[1024]{0:T(1024)}, u32[]{:S(2)}) copy-start(f32[1024]{0:T(1024)} %param.15) | copy-start | bytes 12292
  22.6 1.7 %copy-start.6 = (s32[1024]{0:T(1024)S(1)}, s32[1024]{0:T(1024)}, u32[]{:S(2)}) copy-start(s32[1024]{0:T(1024)} %param.16) | copy-start | bytes 12292
  22.6 1.6 %collective-permute-start.8 = (bf16[1152,128]{1,0:T(8,128)(2,1)S(1)}, bf16[1152,128]{1,0:T(8,128)(2,1)S(1)}, u32[]{:S(2)}, u32[]{:S(2)}) collective-permute-start(bf16[1152,128]{1,0:T(8,128)(2,1)S(1)} %constant_dynamic-update-slice_fusion.near_ref), channel_id=1, source_target_pairs={{0,8},{1,9},{2,10},{3,11},{4,12},{5,13},{6,14},{7,15},{8,0},{9,1},... | collective-permute-start | bytes 884744 | tf_op jit(solution)/shard_map/ppermute | solution.py:504

commit v4 on v3

--- a/solution.py
+++ b/solution.py
@@ -180,60 +180,61 @@
     )(*args)
 
 
-def flow_kernel(
-    start, state_ref, nbr_ref, trace_ref, local_ref, partner0, other0, partner1, other1, weights_ref, flux_mat_ref,
-    out_ref, remote_ref,
-):
+def flow_kernel(directions, state_ref, nbr_ref, trace_ref, local_ref, weights_ref, flux_mat_ref, *refs):
     unknowns, count = state_ref.shape
     first, second, height = operand_places(unknowns)
-    for axis, (partner, other, which) in enumerate(((partner0, other0, "dom"), (partner1, other1, "sec"))):
-        flip = odd(which)
-        remote_ref[2 * axis] = jnp.where(flip, partner[...], other[...])
-        remote_ref[2 * axis + 1] = jnp.where(flip, other[...], partner[...])
-
-    def some(pair, carry):
-        places = [pair * 2 + k for k in range(2)]
-        wheres = [pl.ds(pl.multiple_of((start + p) * WIDE, WIDE), WIDE) for p in places]
+    out_ref = refs[0]
+    if len(refs) > 1:
+        out_ref, remote_ref = refs[4:]
+        for axis, which in enumerate(BOTH[::-1]):
+            flip = odd(which)
+            partner, other = refs[2 * axis][...], refs[2 * axis + 1][...]
+            remote_ref[2 * axis] = jnp.where(flip, partner, other)
+            remote_ref[2 * axis + 1] = jnp.where(flip, other, partner)
+    faces = [2 * direction + side for direction in directions if direction < 3 for side in range(2)]
+
+    def some(places):
+        wheres = [slice(p * WIDE, (p + 1) * WIDE) for p in places]
         found = {}
-        for k, here in enumerate(wheres):
-            for face in range(6):
-                found[k, face] = local_ref[face, :, here]
+        for here in wheres:
+            for face in faces:
+                found[here.start, face] = local_ref[face, :, here]
                 if face < 4:
                     index = nbr_ref[face : face + 1, here] - count
-                    found[k, face] += dot(remote_ref[face], chosen(index, remote_ref.shape[2])).astype(jnp.bfloat16)
+                    remote = dot(remote_ref[face], chosen(index, remote_ref.shape[2]))
+                    found[here.start, face] += remote.astype(jnp.bfloat16)
         fluxes = {}
-        for k, p in enumerate(places):
-            for face in range(6):
-                sides = jnp.concatenate([trace_ref[face, start + p], found[k, face]], axis=0)
-                fluxes[k, face] = dot(flux_mat_ref[face], sides).astype(jnp.bfloat16)
+        for p, here in zip(places, wheres):
+            for face in faces:
+                sides = jnp.concatenate([trace_ref[face, p], found[here.start, face]], axis=0)
+                fluxes[p, face] = dot(flux_mat_ref[face], sides).astype(jnp.bfloat16)
         gap = jnp.zeros((second - first - SLOT, WIDE), jnp.bfloat16)
-        for k, p in enumerate(places):
-            there = pl.ds(pl.multiple_of(p * WIDE, WIDE), WIDE)
-            own = state_ref[:, wheres[k]]
+        for p, here in zip(places, wheres):
+            own = state_ref[:, here]
             own_padded = jnp.concatenate([own, jnp.zeros((first - unknowns, WIDE), jnp.bfloat16)], axis=0)
-            for direction in range(4):
+            for place, direction in enumerate(directions):
                 if direction < 3:
-                    operand = [own_padded, fluxes[k, 2 * direction], gap, fluxes[k, 2 * direction + 1]]
-                    out_ref[direction, :, there] = dot(weights_ref[direction], jnp.concatenate(operand, axis=0))
+                    operand = [own_padded, fluxes[p, 2 * direction], gap, fluxes[p, 2 * direction + 1]]
+                    out_ref[place, :, here] = dot(weights_ref[direction], jnp.concatenate(operand, axis=0))
                 else:
-                    out_ref[direction, :, there] = dot(weights_ref[direction, :, :unknowns], own)
-        return carry
-
-    for pair in range(out_ref.shape[2] // WIDE // 2):
-        some(pair, 0)
-
-
-def flow_parts(start, steps, flow_state, face_nbr, traces, local, remotes, weights, flux_mat):
-    unknowns = flow_state.shape[0]
-    args = (flow_state, face_nbr, traces, local, *remotes, weights, flux_mat)
+                    out_ref[place, :, here] = dot(weights_ref[direction, :, :unknowns], own)
+
+    chunks = count // WIDE
+    for start in range(0, chunks, 2):
+        some(range(start, min(start + 2, chunks)))
+
+
+def flow_parts(directions, flow_state, face_nbr, traces, local, weights, flux_mat, *remotes):
+    unknowns, count = flow_state.shape
+    args = (flow_state, face_nbr, traces, local, weights, flux_mat, *remotes)
     return pl.pallas_call(
-        functools.partial(flow_kernel, start),
+        functools.partial(flow_kernel, directions),
         in_specs=[VMEM] * len(args),
         out_specs=VMEM,
-        out_shape=jax.ShapeDtypeStruct((4, unknowns, steps * WIDE), jnp.float32),
-        scratch_shapes=[pltpu.VMEM((4, *remotes[0].shape), jnp.bfloat16)],
+        out_shape=jax.ShapeDtypeStruct((len(directions), unknowns, count), jnp.float32),
+        scratch_shapes=[pltpu.VMEM((4, *remotes[0].shape), jnp.bfloat16)] if remotes else [],
         compiler_params=pltpu.CompilerParams(vmem_limit_bytes=32 << 20),
-        cost_estimate=pl.CostEstimate(flops=3 << 30, bytes_accessed=4 << 20, transcendentals=0),
+        cost_estimate=pl.CostEstimate(flops=2 << 30, bytes_accessed=4 << 20, transcendentals=0),
         name="flow_parts",
     )(*args)
 
@@ -398,17 +399,20 @@
     column = anchor - row * 128
     upper = row // tiles
     place = (row - upper * tiles) * TILE + upper
-    pick = jnp.where(lax.broadcasted_iota(jnp.int32, (128, count), 0) == column, 1.0, 0.0).astype(jnp.bfloat16)
+    some_rows = 128
+    run = lax.shift_right_logical(place, 7)
+    pair = lax.shift_right_logical(run, 1)
+    inner = place - some_rows * run
+    pick = chosen(column + 128 * (run - 2 * pair), 256)
     pick = jnp.concatenate([pick, pick], axis=0)
-    some_rows = 128
     row_of = lax.broadcasted_iota(jnp.int32, (some_rows, count), 0)
 
     def look(chunk, sums):
-        first = pl.multiple_of(chunk * some_rows, some_rows)
-        hit = row_of == place - first
+        hit = row_of == jnp.where(pair == chunk, inner, -1)
         out = []
         for c in range(comps):
-            value = disp[c, pl.ds(first, some_rows), :]
+            values = [disp[c, pl.ds(pl.multiple_of((2 * chunk + k) * some_rows, some_rows), some_rows), :] for k in range(2)]
+            value = jnp.concatenate(values, axis=1)
             coarse = value.astype(jnp.bfloat16)
             fine = (value - coarse.astype(jnp.float32)).astype(jnp.bfloat16)
             found = dot(jnp.concatenate([coarse, fine], axis=1), pick)
@@ -417,23 +421,19 @@
         return tuple(out)
 
     sums = (jnp.zeros((TILE, count), jnp.float32),) * comps
-    sums = lax.fori_loop(0, rows // some_rows, look, sums, unroll=rows // some_rows <= 4)
+    chunks = rows // (2 * some_rows)
+    sums = lax.fori_loop(0, chunks, look, sums, unroll=chunks <= 2)
     follow = follow_ref[...]
     geometry = [
         base_ref[c : c + 1, :] * jnp.exp(follow * jnp.sum(sums[c], axis=0, keepdims=True)) for c in range(comps)
     ]
     geometry.append(base_ref[comps : comps + 1, :])
     unknowns = residual_ref.shape[0]
-    begin = 0
-    for parts_ref in (parts0_ref, parts1_ref):
-        cols = slice(begin, begin + parts_ref.shape[2])
-        begin = cols.stop
-        for first in range(0, unknowns, 16):
-            some = slice(first, min(first + 16, unknowns))
-            value = geometry[0][:, cols] * parts_ref[0, some, :]
-            for direction in range(1, 4):
-                value += geometry[direction][:, cols] * parts_ref[direction, some, :]
-            residual_ref[some, cols] = value.astype(jnp.bfloat16)
+    parts = [(ref, place) for ref in (parts0_ref, parts1_ref) for place in range(ref.shape[0])]
+    for first in range(0, unknowns, 16):
+        some = slice(first, min(first + 16, unknowns))
+        terms = [factor * ref[place, some, :] for factor, (ref, place) in zip(geometry, parts)]
+        residual_ref[some, :] = functools.reduce(jnp.add, terms).astype(jnp.bfloat16)
 
 
 def wall_and_residual(near, far, masks, kind_bits, base_geometry, anchor_weight, wall_anchor, parts, own_rows):
@@ -507,30 +507,30 @@
     far = sent(wall, 0)
     head_count = flow_state.shape[1] // 8
     traces, *heads = all_traces(flow_state, head_count)
+    remotes = [None] * 4
     far, heads = barrier((far, heads))
     wall = jnp.concatenate([wall, far], axis=0)
     far = sent(wall, 1)
-    remotes = [None] * 4
+    remotes[1] = paired(heads[1], "dom", 1)
+    far, heads, face_jac = barrier((far, heads, face_jac))
+    wall = jnp.concatenate([wall, far], axis=0)
+    far = sent(wall, 2)
+    jac = face_jac.transpose(2, 0, 1, 3).reshape(NV, 12 * NV)
     remotes[2] = paired(heads[2], "sec", 0)
     remotes[0] = paired(heads[0], "dom", 0)
-    far, heads = barrier((far, heads))
+    remotes[3] = paired(heads[3], "sec", 1)
+    far, traces, volume_ops, jac, remotes[1] = barrier((far, traces, volume_ops, jac, remotes[1]))
     wall = jnp.concatenate([wall, far], axis=0)
-    far = sent(wall, 2)
-    remotes[1] = paired(heads[1], "dom", 1)
-    remotes[3] = paired(heads[3], "sec", 1)
-    far, traces, volume_ops, face_jac, remotes[0], remotes[2] = barrier((far, traces, volume_ops, face_jac, remotes[0], remotes[2]))
-    wall = jnp.concatenate([wall, far], axis=0)
-    jac = face_jac.transpose(2, 0, 1, 3).reshape(NV, 12 * NV)
     far = sent(wall, 3)
     local, weights, flux_mat = local_traces(traces, face_nbr, volume_ops, lift_ops, jac)
-    chunks = traces.shape[1]
-    halves = []
-    halves.append(flow_parts(0, chunks // 2, flow_state, face_nbr, traces, local, remotes, weights, flux_mat))
-    far, local, halves = barrier((far, local, halves))
+    common = (flow_state, face_nbr, traces, local, weights, flux_mat)
+    inner = flow_parts((2, 3), *common)
+    far, inner, remotes[0], remotes[2], remotes[3] = barrier((far, inner, remotes[0], remotes[2], remotes[3]))
     for position in range(4, len(stages[0])):
         wall = jnp.concatenate([wall, far], axis=0)
         far = sent(wall, position)
-    halves.append(flow_parts(chunks // 2, chunks // 2, flow_state, face_nbr, traces, local, remotes, weights, flux_mat))
+    outer = flow_parts((0, 1), *common, *remotes)
+    halves = (outer, inner)
     return wall_and_residual(wall, far, masks, kind_bits, base_geometry, anchor_weight, wall_anchor, halves, own_rows)
 
 

time: 30 us -> 28.1 us (0.937)
  starting transfers between devices: 15.8 us -> 13.8 us
    ppermute x5, starting transfers between devices: 9.23 us -> 7.04 us  [sent(): return lax.ppermute(wall, BOTH, pairs)]
  transfers between devices with their start and end apart: 9 -> 9, of which waited for: 2 -> 3; matrix products, arithmetic and copies ran while one was open for 1% -> 2% of each run, Pallas kernels for 16% -> 17%
where the time goes in v4:
time: 28.1 us; the launch traced here: 27.8 us
  starting transfers between devices  13.8 us (49%)
  Pallas kernels  10.1 us (36%)
  local copies, waits for them, and re-layouts  1.54 us (5%)
  other arithmetic  0.92 us (3%)
  between operations  0.88 us (3%)
  waiting for transfers between devices  0.62 us (2%)
    ppermute x5, starting transfers between devices, sent(): return lax.ppermute(wall, BOTH, pairs)  7.04 us
    ppermute x4, starting transfers between devices, paired(): return lax.ppermute(x, axis, pairs + [pair[::-1] for pair in pairs])  6.71 us
    pallas_call x1, Pallas kernels, wall_and_residual(): pl.pallas_call(functools.partial(wall_kernel, masks, kind_bits, rows, own...  5.37 us
    pallas_call x2, Pallas kernels, flow_parts(): pl.pallas_call(functools.partial(flow_kernel, directions), in_specs=[VMEM...  2.25 us
    pallas_call x1, Pallas kernels, local_traces(): pl.pallas_call(local_kernel, in_specs=[VMEM] * len(args), out_specs=[VMEM...  1.91 us
    unnamed x27, local copies, waits for them, and re-layouts  1.15 us
    unnamed x1, other arithmetic  0.88 us
    ppermute x5, waiting for transfers between devices, sent(): return lax.ppermute(wall, BOTH, pairs)  0.61 us
  transfers between devices with their start and end apart: 9, of which 3 were waited for; matrix products, arithmetic and copies ran while one was open for 2% of the time, Pallas kernels for 17%

profile of v4, /device:TPU:0, one launch (start us, length us, event | category | flops | bytes accessed | tf_op | source)
XLA Modules:
  0.0 27.8 jit_solution(9523219424087037536)
XLA Ops:
  0.7 0.9 %constant_dynamic-update-slice_fusion.4 = (bf16[1152,128]{1,0:T(8,128)(2,1)S(1)}, bf16[72,128]{1,0:T(8,128)(2,1)S(1)}) fusion(f32[3,8,128]{2,1,0:T(8,128)} %param.22, f32[3,8,128]{2,1,0:T(8,128)} %param.21, s32[72]{0:T(128)S(1)} %get-tuple-element.60, s32[72]{0:T(128)S(1)} %get-tuple-element.61, pred[72]{0:T(512)(128)(4,1)S(1)} %compare_and_fusion), kind=kLoop, calls=%fused_computation.11 | loop fusion | flops 73727 | bytes 62088
  1.5 3.5 %collective-permute-start = (bf16[72,128]{1,0:T(8,128)(2,1)S(1)}, bf16[72,128]{1,0:T(8,128)(2,1)S(1)}, u32[]{:S(2)}, u32[]{:S(2)}) collective-permute-start(bf16[72,128]{1,0:T(8,128)(2,1)S(1)} %get-tuple-element.59), channel_id=1, source_target_pairs={{0,12},{1,13},{2,14},{3,15},{4,8},{5,9},{6,10},{7,11},{8,4},{9,5},... | collective-permute-start | bytes 55304 | tf_op jit(solution)/shard_map/ppermute | solution.py:504
  5.1 1.1 %copy-done = bf16[270,1024]{1,0:T(8,128)(2,1)S(1)} copy-done((bf16[270,1024]{1,0:T(8,128)(2,1)S(1)}, bf16[270,1024]{1,0:T(8,128)(2,1)}, u32[]{:S(2)}) %copy-start) | copy-done | bytes 552984
  6.1 0.6 %all_traces.1 = (bf16[6,4,96,256]{3,2,1,0:T(8,128)(2,1)S(1)}, bf16[96,128]{1,0:T(8,128)(2,1)S(1)}, bf16[96,128]{1,0:T(8,128)(2,1)S(1)}, bf16[96,128]{1,0:T(8,128)(2,1)S(1)}, bf16[96,128]{1,0:T(8,128)(2,1)S(1)}) custom-call(bf16[270,1024]{1,0:T(8,128)(2,1)S(1)} %copy-done), custom_call_target="tpu_custom_call" | custom-call | flops 1073741824 | bytes 4194304 | tf_op jit(solution)/shard_map/all_traces/pallas_call | solution.py:109
  6.8 0.0 copy-start.7
  6.8 0.0 copy-start.8
  6.8 1.9 %collective-permute-start.1 = (bf16[144,128]{1,0:T(8,128)(2,1)S(1)}, bf16[144,128]{1,0:T(8,128)(2,1)S(1)}, u32[]{:S(2)}, u32[]{:S(2)}) collective-permute-start(bf16[144,128]{1,0:T(8,128)(2,1)S(1)} %pad_maximum_fusion.2), channel_id=1, source_target_pairs={{0,10},{1,11},{2,8},{3,9},{4,14},{5,15},{6,12},{7,13},{8,2},{9,3},... | collective-permute-start | bytes 110600 | tf_op jit(solution)/shard_map/ppermute | solution.py:504
  8.8 3.5 %collective-permute-start.3 = (bf16[96,128]{1,0:T(8,128)(2,1)S(1)}, bf16[96,128]{1,0:T(8,128)(2,1)S(1)}, u32[]{:S(2)}, u32[]{:S(2)}) collective-permute-start(bf16[96,128]{1,0:T(8,128)(2,1)S(1)} %get-tuple-element.36), channel_id=1, source_target_pairs={{1,2},{3,4},{5,6},{7,0},{2,1},{4,3},{6,5},{0,7},{9,10},{11,12},{13... | collective-permute-start | bytes 73736 | tf_op jit(solution)/shard_map/ppermute | solution.py:468
  12.2 0.1 collective-permute-start.2
  12.4 0.2 copy.17
  12.5 0.1 reshape.11.jac_ref
  12.6 1.3 %collective-permute-start.5 = (bf16[96,128]{1,0:T(8,128)(2,1)S(1)}, bf16[96,128]{1,0:T(8,128)(2,1)S(1)}, u32[]{:S(2)}, u32[]{:S(2)}) collective-permute-start(bf16[96,128]{1,0:T(8,128)(2,1)S(1)} %get-tuple-element.49), channel_id=1, source_target_pairs={{0,1},{2,3},{4,5},{6,7},{1,0},{3,2},{5,4},{7,6},{8,9},{10,11},{12,... | collective-permute-start | bytes 73736 | tf_op jit(solution)/shard_map/ppermute | solution.py:468
  13.9 0.6 %collective-permute-start.6 = (bf16[96,128]{1,0:T(8,128)(2,1)S(1)}, bf16[96,128]{1,0:T(8,128)(2,1)S(1)}, u32[]{:S(2)}, u32[]{:S(2)}) collective-permute-start(bf16[96,128]{1,0:T(8,128)(2,1)S(1)} %get-tuple-element.50), channel_id=1, source_target_pairs={{0,8},{16,24},{8,0},{24,16},{1,9},{17,25},{9,1},{25,17},{2,10},{18... | collective-permute-start | bytes 73736 | tf_op jit(solution)/shard_map/ppermute | solution.py:468
  14.5 1.3 %collective-permute-start.7 = (bf16[96,128]{1,0:T(8,128)(2,1)S(1)}, bf16[96,128]{1,0:T(8,128)(2,1)S(1)}, u32[]{:S(2)}, u32[]{:S(2)}) collective-permute-start(bf16[96,128]{1,0:T(8,128)(2,1)S(1)} %get-tuple-element.51), channel_id=1, source_target_pairs={{8,16},{24,0},{16,8},{0,24},{9,17},{25,1},{17,9},{1,25},{10,18},{2... | collective-permute-start | bytes 73736 | tf_op jit(solution)/shard_map/ppermute | solution.py:468
  15.9 0.2 collective-permute-done.2
  16.1 1.3 %collective-permute-start.4 = (bf16[576,128]{1,0:T(8,128)(2,1)S(1)}, bf16[576,128]{1,0:T(8,128)(2,1)S(1)}, u32[]{:S(2)}, u32[]{:S(2)}) collective-permute-start(bf16[576,128]{1,0:T(8,128)(2,1)S(1)} %pad_maximum_fusion), channel_id=1, source_target_pairs={{0,24},{1,8},{2,26},{3,10},{4,28},{5,12},{6,30},{7,14},{8,1},{9,17... | collective-permute-start | bytes 442376 | tf_op jit(solution)/shard_map/ppermute | solution.py:504
  17.4 0.1 copy.18.volume_ref
  17.6 1.9 %local_traces.1 = (bf16[6,96,1024]{2,1,0:T(8,128)(2,1)S(1)}, bf16[4,270,480]{2,1,0:T(8,128)(2,1)S(1)}, bf16[6,96,192]{2,1,0:T(8,128)(2,1)S(1)}) custom-call(bf16[6,4,96,256]{3,2,1,0:T(8,128)(2,1)S(1)} %get-tuple-element.43.trace_ref, s32[6,1024]{1,0:T(8,128)S(1)} %copy-done.3, bf16[4,270,270]{2,1,0:T(8,128)(2,1)S(1)} %copy.18.volume_ref, ...), custom_call_target="tpu_custom_call" | custom-call | flops 2147483648 | bytes 4194304 | tf_op jit(solution)/shard_map/local_traces/pallas_call | solution.py:168
  19.5 0.9 %flow_parts.2.parts1_ref = f32[2,270,1024]{2,1,0:T(8,128)S(1)} custom-call(bf16[270,1024]{1,0:T(8,128)(2,1)S(1)} %copy-done.1, s32[6,1024]{1,0:T(8,128)S(1)} %copy-done.3, bf16[6,4,96,256]{3,2,1,0:T(8,128)(2,1)S(1)} %get-tuple-element.43.trace_ref, bf16[6,96,1024]{2,1,0:T(8,128)(2,1)S(1)} %get-tuple-element.46.local_ref, ...), custom_call_target="tpu_custom_call" | custom-call | flops 2147483648 | bytes 4194304 | tf_op jit(solution)/shard_map/flow_parts/pallas_call | solution.py:230
  20.5 0.2 collective-permute-done.4
  20.8 0.2 collective-permute-start.8
  21.0 1.3 %flow_parts.3.parts0_ref = f32[2,270,1024]{2,1,0:T(8,128)S(1)} custom-call(bf16[270,1024]{1,0:T(8,128)(2,1)S(1)} %copy-done.1, s32[6,1024]{1,0:T(8,128)S(1)} %copy-done.3, bf16[6,4,96,256]{3,2,1,0:T(8,128)(2,1)S(1)} %get-tuple-element.43.trace_ref, bf16[6,96,1024]{2,1,0:T(8,128)(2,1)S(1)} %get-tuple-element.46.local_ref, ...), custom_call_target="tpu_custom_call" | custom-call | flops 2147483648 | bytes 4194304 | tf_op jit(solution)/shard_map/flow_parts/pallas_call | solution.py:230
  22.3 0.1 collective-permute-done.8.far_ref
  22.5 5.4 %wall_and_residual.1 = (bf16[270,1024]{1,0:T(8,128)(2,1)}, f32[3,8,128]{2,1,0:T(8,128)}) custom-call(bf16[1152,128]{1,0:T(8,128)(2,1)S(1)} %constant_dynamic-update-slice_fusion.near_ref, bf16[1152,128]{1,0:T(8,128)(2,1)S(1)} %collective-permute-done.8.far_ref, f32[4,1024]{1,0:T(4,128)S(1)} %copy-done.4, f32[1,1024]{1,0:T(1,128)S(1)} %bitcast.8, ...), custom_call_target="tpu_custom_call" | custom-call | flops 4294967296 | bytes 8388608 | tf_op jit(solution)/shard_map/wall_and_residual/pallas_call | solution.py:443
  (36 shorter events, 0.2 us)
Async XLA Ops:
  1.5 5.2 %collective-permute-start = (bf16[72,128]{1,0:T(8,128)(2,1)S(1)}, bf16[72,128]{1,0:T(8,128)(2,1)S(1)}, u32[]{:S(2)}, u32[]{:S(2)}) collective-permute-start(bf16[72,128]{1,0:T(8,128)(2,1)S(1)} %get-tuple-element.59), channel_id=1, source_target_pairs={{0,12},{1,13},{2,14},{3,15},{4,8},{5,9},{6,10},{7,11},{8,4},{9,5},... | collective-permute-start | bytes 55304 | tf_op jit(solution)/shard_map/ppermute | solution.py:504
  5.1 1.1 %copy-start = (bf16[270,1024]{1,0:T(8,128)(2,1)S(1)}, bf16[270,1024]{1,0:T(8,128)(2,1)}, u32[]{:S(2)}) copy-start(bf16[270,1024]{1,0:T(8,128)(2,1)} %state_ref.5) | copy-start | bytes 1658884
  6.1 6.2 %copy-start.11 = (bf16[6,2,5,5]{0,1,3,2:T(2,128)(2,1)S(1)}, bf16[6,2,5,5]{0,1,3,2:T(2,128)(2,1)}, u32[]{:S(2)}) copy-start(bf16[6,2,5,5]{0,1,3,2:T(2,128)(2,1)} %param.20) | copy-start | bytes 1804
  6.1 11.3 %copy-start.10 = (bf16[4,270,270]{2,0,1:T(4,128)(2,1)S(1)}, bf16[4,270,270]{2,0,1:T(4,128)(2,1)}, u32[]{:S(2)}) copy-start(bf16[4,270,270]{2,0,1:T(4,128)(2,1)} %param.18) | copy-start | bytes 1749604
  6.7 10.8 %copy-start.2 = (bf16[6,270,90]{2,1,0:T(8,128)(2,1)S(1)}, bf16[6,270,90]{2,1,0:T(8,128)(2,1)}, u32[]{:S(2)}) copy-start(bf16[6,270,90]{2,1,0:T(8,128)(2,1)} %lift_ref.1) | copy-start | bytes 874804
  6.7 10.8 %copy-start.3 = (s32[6,1024]{1,0:T(8,128)S(1)}, s32[6,1024]{1,0:T(8,128)}, u32[]{:S(2)}) copy-start(s32[6,1024]{1,0:T(8,128)} %nbr_ref.5) | copy-start | bytes 73732
  6.8 10.8 %copy-start.7 = (bf16[60,1152]{1,0:T(8,128)(2,1)S(1)}, bf16[60,1152]{1,0:T(8,128)(2,1)}, u32[]{:S(2)}) copy-start(bf16[60,1152]{1,0:T(8,128)(2,1)} %constant.19.clone.right_ref) | copy-start | bytes 414724
  6.8 10.8 %copy-start.8 = (f32[96,192]{1,0:T(8,128)S(1)}, f32[96,192]{1,0:T(8,128)}, u32[]{:S(2)}) copy-start(f32[96,192]{1,0:T(8,128)} %constant.20.clone.same_ref) | copy-start | bytes 221188
  6.8 10.8 %copy-start.9 = (bf16[96,5]{1,0:T(8,128)(2,1)S(1)}, bf16[96,5]{1,0:T(8,128)(2,1)}, u32[]{:S(2)}) copy-start(bf16[96,5]{1,0:T(8,128)(2,1)} %constant.18.clone.left_ref) | copy-start | bytes 2884
  6.8 5.4 %collective-permute-start.1 = (bf16[144,128]{1,0:T(8,128)(2,1)S(1)}, bf16[144,128]{1,0:T(8,128)(2,1)S(1)}, u32[]{:S(2)}, u32[]{:S(2)}) collective-permute-start(bf16[144,128]{1,0:T(8,128)(2,1)S(1)} %pad_maximum_fusion.2), channel_id=1, source_target_pairs={{0,10},{1,11},{2,8},{3,9},{4,14},{5,15},{6,12},{7,13},{8,2},{9,3},... | collective-permute-start | bytes 110600 | tf_op jit(solution)/shard_map/ppermute | solution.py:504
  8.8 7.1 %collective-permute-start.3 = (bf16[96,128]{1,0:T(8,128)(2,1)S(1)}, bf16[96,128]{1,0:T(8,128)(2,1)S(1)}, u32[]{:S(2)}, u32[]{:S(2)}) collective-permute-start(bf16[96,128]{1,0:T(8,128)(2,1)S(1)} %get-tuple-element.36), channel_id=1, source_target_pairs={{1,2},{3,4},{5,6},{7,0},{2,1},{4,3},{6,5},{0,7},{9,10},{11,12},{13... | collective-permute-start | bytes 73736 | tf_op jit(solution)/shard_map/ppermute | solution.py:468
  12.2 3.8 %collective-permute-start.2 = (bf16[288,128]{1,0:T(8,128)(2,1)S(1)}, bf16[288,128]{1,0:T(8,128)(2,1)S(1)}, u32[]{:S(2)}, u32[]{:S(2)}) collective-permute-start(bf16[288,128]{1,0:T(8,128)(2,1)S(1)} %pad_maximum_fusion.1), channel_id=1, source_target_pairs={{0,9},{1,25},{2,11},{3,27},{4,13},{5,29},{6,15},{7,31},{8,16},{9,0... | collective-permute-start | bytes 221192 | tf_op jit(solution)/shard_map/ppermute | solution.py:504
  12.6 7.8 %collective-permute-start.5 = (bf16[96,128]{1,0:T(8,128)(2,1)S(1)}, bf16[96,128]{1,0:T(8,128)(2,1)S(1)}, u32[]{:S(2)}, u32[]{:S(2)}) collective-permute-start(bf16[96,128]{1,0:T(8,128)(2,1)S(1)} %get-tuple-element.49), channel_id=1, source_target_pairs={{0,1},{2,3},{4,5},{6,7},{1,0},{3,2},{5,4},{7,6},{8,9},{10,11},{12,... | collective-permute-start | bytes 73736 | tf_op jit(solution)/shard_map/ppermute | solution.py:468
  13.9 6.6 %collective-permute-start.6 = (bf16[96,128]{1,0:T(8,128)(2,1)S(1)}, bf16[96,128]{1,0:T(8,128)(2,1)S(1)}, u32[]{:S(2)}, u32[]{:S(2)}) collective-permute-start(bf16[96,128]{1,0:T(8,128)(2,1)S(1)} %get-tuple-element.50), channel_id=1, source_target_pairs={{0,8},{16,24},{8,0},{24,16},{1,9},{17,25},{9,1},{25,17},{2,10},{18... | collective-permute-start | bytes 73736 | tf_op jit(solution)/shard_map/ppermute | solution.py:468
  14.5 6.0 %collective-permute-start.7 = (bf16[96,128]{1,0:T(8,128)(2,1)S(1)}, bf16[96,128]{1,0:T(8,128)(2,1)S(1)}, u32[]{:S(2)}, u32[]{:S(2)}) collective-permute-start(bf16[96,128]{1,0:T(8,128)(2,1)S(1)} %get-tuple-element.51), channel_id=1, source_target_pairs={{8,16},{24,0},{16,8},{0,24},{9,17},{25,1},{17,9},{1,25},{10,18},{2... | collective-permute-start | bytes 73736 | tf_op jit(solution)/shard_map/ppermute | solution.py:468
  16.1 4.6 %collective-permute-start.4 = (bf16[576,128]{1,0:T(8,128)(2,1)S(1)}, bf16[576,128]{1,0:T(8,128)(2,1)S(1)}, u32[]{:S(2)}, u32[]{:S(2)}) collective-permute-start(bf16[576,128]{1,0:T(8,128)(2,1)S(1)} %pad_maximum_fusion), channel_id=1, source_target_pairs={{0,24},{1,8},{2,26},{3,10},{4,28},{5,12},{6,30},{7,14},{8,1},{9,17... | collective-permute-start | bytes 442376 | tf_op jit(solution)/shard_map/ppermute | solution.py:504
  17.6 1.9 %copy-start.1 = (bf16[270,1024]{1,0:T(8,128)(2,1)S(1)}, bf16[270,1024]{1,0:T(8,128)(2,1)}, u32[]{:S(2)}) copy-start(bf16[270,1024]{1,0:T(8,128)(2,1)} %state_ref.5) | copy-start | bytes 1658884
  20.8 1.7 %copy-start.4 = (f32[4,1024]{1,0:T(4,128)S(1)}, f32[4,1024]{1,0:T(4,128)}, u32[]{:S(2)}) copy-start(f32[4,1024]{1,0:T(4,128)} %base_ref.1) | copy-start | bytes 49156
  20.8 1.7 %copy-start.5 = (f32[1024]{0:T(1024)S(1)}, f32[1024]{0:T(1024)}, u32[]{:S(2)}) copy-start(f32[1024]{0:T(1024)} %param.15) | copy-start | bytes 12292
  20.8 1.7 %copy-start.6 = (s32[1024]{0:T(1024)S(1)}, s32[1024]{0:T(1024)}, u32[]{:S(2)}) copy-start(s32[1024]{0:T(1024)} %param.16) | copy-start | bytes 12292
  20.8 1.6 %collective-permute-start.8 = (bf16[1152,128]{1,0:T(8,128)(2,1)S(1)}, bf16[1152,128]{1,0:T(8,128)(2,1)S(1)}, u32[]{:S(2)}, u32[]{:S(2)}) collective-permute-start(bf16[1152,128]{1,0:T(8,128)(2,1)S(1)} %constant_dynamic-update-slice_fusion.near_ref), channel_id=1, source_target_pairs={{0,8},{1,9},{2,10},{3,11},{4,12},{5,13},{6,14},{7,15},{8,0},{9,1},... | collective-permute-start | bytes 884744 | tf_op jit(solution)/shard_map/ppermute | solution.py:504

commit v5 on v4

--- a/solution.py
+++ b/solution.py
@@ -474,6 +474,7 @@
     bits = [1 << b for b in range((n_sec * n_dom).bit_length() - 1)]
     inner, outer = bits[: n_dom.bit_length() - 1], bits[n_dom.bit_length() :]
     order = inner[::-1] + outer[::-1]
+    order[:2] = order[1::-1]
     first = [bit ^ n_dom for bit in order]
     second = first[:-2] + first[-2:][::-1]
     return (first + [n_dom], second + [n_dom]), order[-2:] + [n_dom]

time: 28.1 us -> 27.5 us (0.979)
  starting transfers between devices: 13.8 us -> 12.9 us
    ppermute x4, starting transfers between devices: 6.71 us -> 4.91 us  [paired(): return lax.ppermute(x, axis, pairs + [pair[::-1] for pair in pairs])]
    ppermute x5, starting transfers between devices: 7.04 us -> 7.98 us  [sent(): return lax.ppermute(wall, BOTH, pairs)]
    ppermute x4, waiting for transfers between devices: 0.01 us -> 0.5 us  [paired(): return lax.ppermute(x, axis, pairs + [pair[::-1] for pair in pairs])]
  transfers between devices with their start and end apart: 9 -> 9, of which waited for: 3 -> 4; matrix products, arithmetic and copies ran while one was open for 2% -> 2% of each run, Pallas kernels for 17% -> 17%
where the time goes in v5:
time: 27.5 us; the launch traced here: 27.2 us
  starting transfers between devices  12.9 us (47%)
  Pallas kernels  10.1 us (37%)
  local copies, waits for them, and re-layouts  1.54 us (6%)
  other arithmetic  0.92 us (3%)
  between operations  0.86 us (3%)
  waiting for transfers between devices  0.85 us (3%)
    ppermute x5, starting transfers between devices, sent(): return lax.ppermute(wall, BOTH, pairs)  7.98 us
    pallas_call x1, Pallas kernels, wall_and_residual(): pl.pallas_call(functools.partial(wall_kernel, masks, kind_bits, rows, own...  5.37 us
    ppermute x4, starting transfers between devices, paired(): return lax.ppermute(x, axis, pairs + [pair[::-1] for pair in pairs])  4.91 us
    pallas_call x2, Pallas kernels, flow_parts(): pl.pallas_call(functools.partial(flow_kernel, directions), in_specs=[VMEM...  2.25 us
    pallas_call x1, Pallas kernels, local_traces(): pl.pallas_call(local_kernel, in_specs=[VMEM] * len(args), out_specs=[VMEM...  1.91 us
    unnamed x27, local copies, waits for them, and re-layouts  1.15 us
    unnamed x1, other arithmetic  0.88 us
    pallas_call x1, Pallas kernels, all_traces(): pl.pallas_call(trace_kernel, in_specs=[VMEM], out_specs=[VMEM] * 5, out_s...  0.58 us
  transfers between devices with their start and end apart: 9, of which 4 were waited for; matrix products, arithmetic and copies ran while one was open for 2% of the time, Pallas kernels for 17%

profile of v5, /device:TPU:0, one launch (start us, length us, event | category | flops | bytes accessed | tf_op | source)
XLA Modules:
  0.0 27.2 jit_solution(1314049710045510322)
XLA Ops:
  0.7 0.9 %constant_dynamic-update-slice_fusion.4 = (bf16[1152,128]{1,0:T(8,128)(2,1)S(1)}, bf16[72,128]{1,0:T(8,128)(2,1)S(1)}) fusion(f32[3,8,128]{2,1,0:T(8,128)} %param.22, f32[3,8,128]{2,1,0:T(8,128)} %param.21, s32[72]{0:T(128)S(1)} %get-tuple-element.60, s32[72]{0:T(128)S(1)} %get-tuple-element.61, pred[72]{0:T(512)(128)(4,1)S(1)} %compare_and_fusion), kind=kLoop, calls=%fused_computation.11 | loop fusion | flops 73727 | bytes 62088
  1.5 2.5 %collective-permute-start = (bf16[72,128]{1,0:T(8,128)(2,1)S(1)}, bf16[72,128]{1,0:T(8,128)(2,1)S(1)}, u32[]{:S(2)}, u32[]{:S(2)}) collective-permute-start(bf16[72,128]{1,0:T(8,128)(2,1)S(1)} %get-tuple-element.59), channel_id=1, source_target_pairs={{0,10},{1,11},{2,8},{3,9},{4,14},{5,15},{6,12},{7,13},{8,2},{9,3},... | collective-permute-start | bytes 55304 | tf_op jit(solution)/shard_map/ppermute | solution.py:505
  4.1 1.1 %copy-done = bf16[270,1024]{1,0:T(8,128)(2,1)S(1)} copy-done((bf16[270,1024]{1,0:T(8,128)(2,1)S(1)}, bf16[270,1024]{1,0:T(8,128)(2,1)}, u32[]{:S(2)}) %copy-start) | copy-done | bytes 552984
  5.1 0.6 %all_traces.1 = (bf16[6,4,96,256]{3,2,1,0:T(8,128)(2,1)S(1)}, bf16[96,128]{1,0:T(8,128)(2,1)S(1)}, bf16[96,128]{1,0:T(8,128)(2,1)S(1)}, bf16[96,128]{1,0:T(8,128)(2,1)S(1)}, bf16[96,128]{1,0:T(8,128)(2,1)S(1)}) custom-call(bf16[270,1024]{1,0:T(8,128)(2,1)S(1)} %copy-done), custom_call_target="tpu_custom_call" | custom-call | flops 1073741824 | bytes 4194304 | tf_op jit(solution)/shard_map/all_traces/pallas_call | solution.py:109
  5.7 0.0 copy-start.7
  5.8 0.0 copy-start.8
  5.8 2.9 %collective-permute-start.1 = (bf16[144,128]{1,0:T(8,128)(2,1)S(1)}, bf16[144,128]{1,0:T(8,128)(2,1)S(1)}, u32[]{:S(2)}, u32[]{:S(2)}) collective-permute-start(bf16[144,128]{1,0:T(8,128)(2,1)S(1)} %pad_maximum_fusion.2), channel_id=1, source_target_pairs={{0,12},{1,13},{2,14},{3,15},{4,8},{5,9},{6,10},{7,11},{8,4},{9,5},... | collective-permute-start | bytes 110600 | tf_op jit(solution)/shard_map/ppermute | solution.py:505
  8.8 2.3 %collective-permute-start.3 = (bf16[96,128]{1,0:T(8,128)(2,1)S(1)}, bf16[96,128]{1,0:T(8,128)(2,1)S(1)}, u32[]{:S(2)}, u32[]{:S(2)}) collective-permute-start(bf16[96,128]{1,0:T(8,128)(2,1)S(1)} %get-tuple-element.36), channel_id=1, source_target_pairs={{1,2},{3,4},{5,6},{7,0},{2,1},{4,3},{6,5},{0,7},{9,10},{11,12},{13... | collective-permute-start | bytes 73736 | tf_op jit(solution)/shard_map/ppermute | solution.py:468
  11.1 0.9 %collective-permute-start.2 = (bf16[288,128]{1,0:T(8,128)(2,1)S(1)}, bf16[288,128]{1,0:T(8,128)(2,1)S(1)}, u32[]{:S(2)}, u32[]{:S(2)}) collective-permute-start(bf16[288,128]{1,0:T(8,128)(2,1)S(1)} %pad_maximum_fusion.1), channel_id=1, source_target_pairs={{0,9},{1,25},{2,11},{3,27},{4,13},{5,29},{6,15},{7,31},{8,16},{9,0... | collective-permute-start | bytes 221192 | tf_op jit(solution)/shard_map/ppermute | solution.py:505
  11.9 0.2 copy.17
  12.1 0.1 reshape.11.jac_ref
  12.2 1.6 %collective-permute-start.5 = (bf16[96,128]{1,0:T(8,128)(2,1)S(1)}, bf16[96,128]{1,0:T(8,128)(2,1)S(1)}, u32[]{:S(2)}, u32[]{:S(2)}) collective-permute-start(bf16[96,128]{1,0:T(8,128)(2,1)S(1)} %get-tuple-element.49), channel_id=1, source_target_pairs={{0,1},{2,3},{4,5},{6,7},{1,0},{3,2},{5,4},{7,6},{8,9},{10,11},{12,... | collective-permute-start | bytes 73736 | tf_op jit(solution)/shard_map/ppermute | solution.py:468
  13.8 1.0 %collective-permute-start.7 = (bf16[96,128]{1,0:T(8,128)(2,1)S(1)}, bf16[96,128]{1,0:T(8,128)(2,1)S(1)}, u32[]{:S(2)}, u32[]{:S(2)}) collective-permute-start(bf16[96,128]{1,0:T(8,128)(2,1)S(1)} %get-tuple-element.51), channel_id=1, source_target_pairs={{8,16},{24,0},{16,8},{0,24},{9,17},{25,1},{17,9},{1,25},{10,18},{2... | collective-permute-start | bytes 73736 | tf_op jit(solution)/shard_map/ppermute | solution.py:468
  14.8 0.5 %collective-permute-done.3.refs_1_ = bf16[96,128]{1,0:T(8,128)(2,1)S(1)} collective-permute-done((bf16[96,128]{1,0:T(8,128)(2,1)S(1)}, bf16[96,128]{1,0:T(8,128)(2,1)S(1)}, u32[]{:S(2)}, u32[]{:S(2)}) %collective-permute-start.3) | collective-permute-done | bytes 24608 | tf_op jit(solution)/shard_map/ppermute | solution.py:468
  15.3 0.1 collective-permute-done.2
  15.5 1.5 %collective-permute-start.4 = (bf16[576,128]{1,0:T(8,128)(2,1)S(1)}, bf16[576,128]{1,0:T(8,128)(2,1)S(1)}, u32[]{:S(2)}, u32[]{:S(2)}) collective-permute-start(bf16[576,128]{1,0:T(8,128)(2,1)S(1)} %pad_maximum_fusion), channel_id=1, source_target_pairs={{0,24},{1,8},{2,26},{3,10},{4,28},{5,12},{6,30},{7,14},{8,1},{9,17... | collective-permute-start | bytes 442376 | tf_op jit(solution)/shard_map/ppermute | solution.py:505
  16.9 0.1 copy.18.volume_ref
  17.1 1.9 %local_traces.1 = (bf16[6,96,1024]{2,1,0:T(8,128)(2,1)S(1)}, bf16[4,270,480]{2,1,0:T(8,128)(2,1)S(1)}, bf16[6,96,192]{2,1,0:T(8,128)(2,1)S(1)}) custom-call(bf16[6,4,96,256]{3,2,1,0:T(8,128)(2,1)S(1)} %get-tuple-element.43.trace_ref, s32[6,1024]{1,0:T(8,128)S(1)} %copy-done.3, bf16[4,270,270]{2,1,0:T(8,128)(2,1)S(1)} %copy.18.volume_ref, ...), custom_call_target="tpu_custom_call" | custom-call | flops 2147483648 | bytes 4194304 | tf_op jit(solution)/shard_map/local_traces/pallas_call | solution.py:168
  19.0 0.9 %flow_parts.2.parts1_ref = f32[2,270,1024]{2,1,0:T(8,128)S(1)} custom-call(bf16[270,1024]{1,0:T(8,128)(2,1)S(1)} %copy-done.1, s32[6,1024]{1,0:T(8,128)S(1)} %copy-done.3, bf16[6,4,96,256]{3,2,1,0:T(8,128)(2,1)S(1)} %get-tuple-element.43.trace_ref, bf16[6,96,1024]{2,1,0:T(8,128)(2,1)S(1)} %get-tuple-element.46.local_ref, ...), custom_call_target="tpu_custom_call" | custom-call | flops 2147483648 | bytes 4194304 | tf_op jit(solution)/shard_map/flow_parts/pallas_call | solution.py:230
  20.0 0.1 collective-permute-done.4
  20.2 0.2 collective-permute-start.8
  20.3 1.3 %flow_parts.3.parts0_ref = f32[2,270,1024]{2,1,0:T(8,128)S(1)} custom-call(bf16[270,1024]{1,0:T(8,128)(2,1)S(1)} %copy-done.1, s32[6,1024]{1,0:T(8,128)S(1)} %copy-done.3, bf16[6,4,96,256]{3,2,1,0:T(8,128)(2,1)S(1)} %get-tuple-element.43.trace_ref, bf16[6,96,1024]{2,1,0:T(8,128)(2,1)S(1)} %get-tuple-element.46.local_ref, ...), custom_call_target="tpu_custom_call" | custom-call | flops 2147483648 | bytes 4194304 | tf_op jit(solution)/shard_map/flow_parts/pallas_call | solution.py:230
  21.7 0.1 collective-permute-done.8.far_ref
  21.8 5.4 %wall_and_residual.1 = (bf16[270,1024]{1,0:T(8,128)(2,1)}, f32[3,8,128]{2,1,0:T(8,128)}) custom-call(bf16[1152,128]{1,0:T(8,128)(2,1)S(1)} %constant_dynamic-update-slice_fusion.near_ref, bf16[1152,128]{1,0:T(8,128)(2,1)S(1)} %collective-permute-done.8.far_ref, f32[4,1024]{1,0:T(4,128)S(1)} %copy-done.4, f32[1,1024]{1,0:T(1,128)S(1)} %bitcast.8, ...), custom_call_target="tpu_custom_call" | custom-call | flops 4294967296 | bytes 8388608 | tf_op jit(solution)/shard_map/wall_and_residual/pallas_call | solution.py:443
  (36 shorter events, 0.2 us)
Async XLA Ops:
  1.5 4.2 %collective-permute-start = (bf16[72,128]{1,0:T(8,128)(2,1)S(1)}, bf16[72,128]{1,0:T(8,128)(2,1)S(1)}, u32[]{:S(2)}, u32[]{:S(2)}) collective-permute-start(bf16[72,128]{1,0:T(8,128)(2,1)S(1)} %get-tuple-element.59), channel_id=1, source_target_pairs={{0,10},{1,11},{2,8},{3,9},{4,14},{5,15},{6,12},{7,13},{8,2},{9,3},... | collective-permute-start | bytes 55304 | tf_op jit(solution)/shard_map/ppermute | solution.py:505
  4.1 1.1 %copy-start = (bf16[270,1024]{1,0:T(8,128)(2,1)S(1)}, bf16[270,1024]{1,0:T(8,128)(2,1)}, u32[]{:S(2)}) copy-start(bf16[270,1024]{1,0:T(8,128)(2,1)} %state_ref.5) | copy-start | bytes 1658884
  5.1 6.8 %copy-start.11 = (bf16[6,2,5,5]{0,1,3,2:T(2,128)(2,1)S(1)}, bf16[6,2,5,5]{0,1,3,2:T(2,128)(2,1)}, u32[]{:S(2)}) copy-start(bf16[6,2,5,5]{0,1,3,2:T(2,128)(2,1)} %param.20) | copy-start | bytes 1804
  5.1 11.8 %copy-start.10 = (bf16[4,270,270]{2,0,1:T(4,128)(2,1)S(1)}, bf16[4,270,270]{2,0,1:T(4,128)(2,1)}, u32[]{:S(2)}) copy-start(bf16[4,270,270]{2,0,1:T(4,128)(2,1)} %param.18) | copy-start | bytes 1749604
  5.7 11.3 %copy-start.2 = (bf16[6,270,90]{2,1,0:T(8,128)(2,1)S(1)}, bf16[6,270,90]{2,1,0:T(8,128)(2,1)}, u32[]{:S(2)}) copy-start(bf16[6,270,90]{2,1,0:T(8,128)(2,1)} %lift_ref.1) | copy-start | bytes 874804
  5.7 11.3 %copy-start.3 = (s32[6,1024]{1,0:T(8,128)S(1)}, s32[6,1024]{1,0:T(8,128)}, u32[]{:S(2)}) copy-start(s32[6,1024]{1,0:T(8,128)} %nbr_ref.5) | copy-start | bytes 73732
  5.7 11.3 %copy-start.7 = (bf16[60,1152]{1,0:T(8,128)(2,1)S(1)}, bf16[60,1152]{1,0:T(8,128)(2,1)}, u32[]{:S(2)}) copy-start(bf16[60,1152]{1,0:T(8,128)(2,1)} %constant.19.clone.right_ref) | copy-start | bytes 414724
  5.8 11.3 %copy-start.8 = (f32[96,192]{1,0:T(8,128)S(1)}, f32[96,192]{1,0:T(8,128)}, u32[]{:S(2)}) copy-start(f32[96,192]{1,0:T(8,128)} %constant.20.clone.same_ref) | copy-start | bytes 221188
  5.8 11.3 %copy-start.9 = (bf16[96,5]{1,0:T(8,128)(2,1)S(1)}, bf16[96,5]{1,0:T(8,128)(2,1)}, u32[]{:S(2)}) copy-start(bf16[96,5]{1,0:T(8,128)(2,1)} %constant.18.clone.left_ref) | copy-start | bytes 2884
  5.8 5.3 %collective-permute-start.1 = (bf16[144,128]{1,0:T(8,128)(2,1)S(1)}, bf16[144,128]{1,0:T(8,128)(2,1)S(1)}, u32[]{:S(2)}, u32[]{:S(2)}) collective-permute-start(bf16[144,128]{1,0:T(8,128)(2,1)S(1)} %pad_maximum_fusion.2), channel_id=1, source_target_pairs={{0,12},{1,13},{2,14},{3,15},{4,8},{5,9},{6,10},{7,11},{8,4},{9,5},... | collective-permute-start | bytes 110600 | tf_op jit(solution)/shard_map/ppermute | solution.py:505
  8.8 6.6 %collective-permute-start.3 = (bf16[96,128]{1,0:T(8,128)(2,1)S(1)}, bf16[96,128]{1,0:T(8,128)(2,1)S(1)}, u32[]{:S(2)}, u32[]{:S(2)}) collective-permute-start(bf16[96,128]{1,0:T(8,128)(2,1)S(1)} %get-tuple-element.36), channel_id=1, source_target_pairs={{1,2},{3,4},{5,6},{7,0},{2,1},{4,3},{6,5},{0,7},{9,10},{11,12},{13... | collective-permute-start | bytes 73736 | tf_op jit(solution)/shard_map/ppermute | solution.py:468
  11.1 4.4 %collective-permute-start.2 = (bf16[288,128]{1,0:T(8,128)(2,1)S(1)}, bf16[288,128]{1,0:T(8,128)(2,1)S(1)}, u32[]{:S(2)}, u32[]{:S(2)}) collective-permute-start(bf16[288,128]{1,0:T(8,128)(2,1)S(1)} %pad_maximum_fusion.1), channel_id=1, source_target_pairs={{0,9},{1,25},{2,11},{3,27},{4,13},{5,29},{6,15},{7,31},{8,16},{9,0... | collective-permute-start | bytes 221192 | tf_op jit(solution)/shard_map/ppermute | solution.py:505
  12.2 7.8 %collective-permute-start.5 = (bf16[96,128]{1,0:T(8,128)(2,1)S(1)}, bf16[96,128]{1,0:T(8,128)(2,1)S(1)}, u32[]{:S(2)}, u32[]{:S(2)}) collective-permute-start(bf16[96,128]{1,0:T(8,128)(2,1)S(1)} %get-tuple-element.49), channel_id=1, source_target_pairs={{0,1},{2,3},{4,5},{6,7},{1,0},{3,2},{5,4},{7,6},{8,9},{10,11},{12,... | collective-permute-start | bytes 73736 | tf_op jit(solution)/shard_map/ppermute | solution.py:468
  13.8 6.2 %collective-permute-start.6 = (bf16[96,128]{1,0:T(8,128)(2,1)S(1)}, bf16[96,128]{1,0:T(8,128)(2,1)S(1)}, u32[]{:S(2)}, u32[]{:S(2)}) collective-permute-start(bf16[96,128]{1,0:T(8,128)(2,1)S(1)} %get-tuple-element.50), channel_id=1, source_target_pairs={{0,8},{16,24},{8,0},{24,16},{1,9},{17,25},{9,1},{25,17},{2,10},{18... | collective-permute-start | bytes 73736 | tf_op jit(solution)/shard_map/ppermute | solution.py:468
  13.8 6.2 %collective-permute-start.7 = (bf16[96,128]{1,0:T(8,128)(2,1)S(1)}, bf16[96,128]{1,0:T(8,128)(2,1)S(1)}, u32[]{:S(2)}, u32[]{:S(2)}) collective-permute-start(bf16[96,128]{1,0:T(8,128)(2,1)S(1)} %get-tuple-element.51), channel_id=1, source_target_pairs={{8,16},{24,0},{16,8},{0,24},{9,17},{25,1},{17,9},{1,25},{10,18},{2... | collective-permute-start | bytes 73736 | tf_op jit(solution)/shard_map/ppermute | solution.py:468
  15.5 4.6 %collective-permute-start.4 = (bf16[576,128]{1,0:T(8,128)(2,1)S(1)}, bf16[576,128]{1,0:T(8,128)(2,1)S(1)}, u32[]{:S(2)}, u32[]{:S(2)}) collective-permute-start(bf16[576,128]{1,0:T(8,128)(2,1)S(1)} %pad_maximum_fusion), channel_id=1, source_target_pairs={{0,24},{1,8},{2,26},{3,10},{4,28},{5,12},{6,30},{7,14},{8,1},{9,17... | collective-permute-start | bytes 442376 | tf_op jit(solution)/shard_map/ppermute | solution.py:505
  17.1 1.9 %copy-start.1 = (bf16[270,1024]{1,0:T(8,128)(2,1)S(1)}, bf16[270,1024]{1,0:T(8,128)(2,1)}, u32[]{:S(2)}) copy-start(bf16[270,1024]{1,0:T(8,128)(2,1)} %state_ref.5) | copy-start | bytes 1658884
  20.1 1.7 %copy-start.4 = (f32[4,1024]{1,0:T(4,128)S(1)}, f32[4,1024]{1,0:T(4,128)}, u32[]{:S(2)}) copy-start(f32[4,1024]{1,0:T(4,128)} %base_ref.1) | copy-start | bytes 49156
  20.1 1.7 %copy-start.5 = (f32[1024]{0:T(1024)S(1)}, f32[1024]{0:T(1024)}, u32[]{:S(2)}) copy-start(f32[1024]{0:T(1024)} %param.15) | copy-start | bytes 12292
  20.1 1.7 %copy-start.6 = (s32[1024]{0:T(1024)S(1)}, s32[1024]{0:T(1024)}, u32[]{:S(2)}) copy-start(s32[1024]{0:T(1024)} %param.16) | copy-start | bytes 12292
  20.2 1.6 %collective-permute-start.8 = (bf16[1152,128]{1,0:T(8,128)(2,1)S(1)}, bf16[1152,128]{1,0:T(8,128)(2,1)S(1)}, u32[]{:S(2)}, u32[]{:S(2)}) collective-permute-start(bf16[1152,128]{1,0:T(8,128)(2,1)S(1)} %constant_dynamic-update-slice_fusion.near_ref), channel_id=1, source_target_pairs={{0,8},{1,9},{2,10},{3,11},{4,12},{5,13},{6,14},{7,15},{8,0},{9,1},... | collective-permute-start | bytes 884744 | tf_op jit(solution)/shard_map/ppermute | solution.py:505

commit v6 on v5

--- a/solution.py
+++ b/solution.py
@@ -277,7 +277,7 @@
 
     lane = lax.broadcasted_iota(jnp.int32, (TILE, 128), 1)
     sub = lax.broadcasted_iota(jnp.int32, (TILE, 128), 0)
-    group = 32 if tiles % 32 == 0 else 8
+    group = 16
     zero = jnp.zeros((TILE, 128), jnp.float32)
 
     def at(tile):

time: 27.5 us -> 27.5 us (level)
  no operation moved by 1% of the time
where the time goes in v6:
time: 27.5 us; the launch traced here: 27.2 us
  starting transfers between devices  12.9 us (47%)
  Pallas kernels  10.1 us (37%)
  local copies, waits for them, and re-layouts  1.54 us (6%)
  other arithmetic  0.92 us (3%)
  between operations  0.86 us (3%)
  waiting for transfers between devices  0.85 us (3%)
    ppermute x5, starting transfers between devices, sent(): return lax.ppermute(wall, BOTH, pairs)  7.98 us
    pallas_call x1, Pallas kernels, wall_and_residual(): pl.pallas_call(functools.partial(wall_kernel, masks, kind_bits, rows, own...  5.36 us
    ppermute x4, starting transfers between devices, paired(): return lax.ppermute(x, axis, pairs + [pair[::-1] for pair in pairs])  4.91 us
    pallas_call x2, Pallas kernels, flow_parts(): pl.pallas_call(functools.partial(flow_kernel, directions), in_specs=[VMEM...  2.25 us
    pallas_call x1, Pallas kernels, local_traces(): pl.pallas_call(local_kernel, in_specs=[VMEM] * len(args), out_specs=[VMEM...  1.91 us
    unnamed x27, local copies, waits for them, and re-layouts  1.15 us
    unnamed x1, other arithmetic  0.88 us
    pallas_call x1, Pallas kernels, all_traces(): pl.pallas_call(trace_kernel, in_specs=[VMEM], out_specs=[VMEM] * 5, out_s...  0.58 us
  transfers between devices with their start and end apart: 9, of which 4 were waited for; matrix products, arithmetic and copies ran while one was open for 2% of the time, Pallas kernels for 17%

profile of v6, /device:TPU:0, one launch (start us, length us, event | category | flops | bytes accessed | tf_op | source)
XLA Modules:
  0.0 27.2 jit_solution(8044367382604365310)
XLA Ops:
  0.7 0.9 %constant_dynamic-update-slice_fusion.4 = (bf16[1152,128]{1,0:T(8,128)(2,1)S(1)}, bf16[72,128]{1,0:T(8,128)(2,1)S(1)}) fusion(f32[3,8,128]{2,1,0:T(8,128)} %param.22, f32[3,8,128]{2,1,0:T(8,128)} %param.21, s32[72]{0:T(128)S(1)} %get-tuple-element.60, s32[72]{0:T(128)S(1)} %get-tuple-element.61, pred[72]{0:T(512)(128)(4,1)S(1)} %compare_and_fusion), kind=kLoop, calls=%fused_computation.11 | loop fusion | flops 73727 | bytes 62088
  1.5 2.5 %collective-permute-start = (bf16[72,128]{1,0:T(8,128)(2,1)S(1)}, bf16[72,128]{1,0:T(8,128)(2,1)S(1)}, u32[]{:S(2)}, u32[]{:S(2)}) collective-permute-start(bf16[72,128]{1,0:T(8,128)(2,1)S(1)} %get-tuple-element.59), channel_id=1, source_target_pairs={{0,10},{1,11},{2,8},{3,9},{4,14},{5,15},{6,12},{7,13},{8,2},{9,3},... | collective-permute-start | bytes 55304 | tf_op jit(solution)/shard_map/ppermute | solution.py:505
  4.1 1.1 %copy-done = bf16[270,1024]{1,0:T(8,128)(2,1)S(1)} copy-done((bf16[270,1024]{1,0:T(8,128)(2,1)S(1)}, bf16[270,1024]{1,0:T(8,128)(2,1)}, u32[]{:S(2)}) %copy-start) | copy-done | bytes 552984
  5.1 0.6 %all_traces.1 = (bf16[6,4,96,256]{3,2,1,0:T(8,128)(2,1)S(1)}, bf16[96,128]{1,0:T(8,128)(2,1)S(1)}, bf16[96,128]{1,0:T(8,128)(2,1)S(1)}, bf16[96,128]{1,0:T(8,128)(2,1)S(1)}, bf16[96,128]{1,0:T(8,128)(2,1)S(1)}) custom-call(bf16[270,1024]{1,0:T(8,128)(2,1)S(1)} %copy-done), custom_call_target="tpu_custom_call" | custom-call | flops 1073741824 | bytes 4194304 | tf_op jit(solution)/shard_map/all_traces/pallas_call | solution.py:109
  5.8 0.0 copy-start.8
  5.8 0.0 copy-start.9
  5.8 2.9 %collective-permute-start.1 = (bf16[144,128]{1,0:T(8,128)(2,1)S(1)}, bf16[144,128]{1,0:T(8,128)(2,1)S(1)}, u32[]{:S(2)}, u32[]{:S(2)}) collective-permute-start(bf16[144,128]{1,0:T(8,128)(2,1)S(1)} %pad_maximum_fusion.2), channel_id=1, source_target_pairs={{0,12},{1,13},{2,14},{3,15},{4,8},{5,9},{6,10},{7,11},{8,4},{9,5},... | collective-permute-start | bytes 110600 | tf_op jit(solution)/shard_map/ppermute | solution.py:505
  8.8 2.3 %collective-permute-start.3 = (bf16[96,128]{1,0:T(8,128)(2,1)S(1)}, bf16[96,128]{1,0:T(8,128)(2,1)S(1)}, u32[]{:S(2)}, u32[]{:S(2)}) collective-permute-start(bf16[96,128]{1,0:T(8,128)(2,1)S(1)} %get-tuple-element.36), channel_id=1, source_target_pairs={{1,2},{3,4},{5,6},{7,0},{2,1},{4,3},{6,5},{0,7},{9,10},{11,12},{13... | collective-permute-start | bytes 73736 | tf_op jit(solution)/shard_map/ppermute | solution.py:468
  11.1 0.9 %collective-permute-start.2 = (bf16[288,128]{1,0:T(8,128)(2,1)S(1)}, bf16[288,128]{1,0:T(8,128)(2,1)S(1)}, u32[]{:S(2)}, u32[]{:S(2)}) collective-permute-start(bf16[288,128]{1,0:T(8,128)(2,1)S(1)} %pad_maximum_fusion.1), channel_id=1, source_target_pairs={{0,9},{1,25},{2,11},{3,27},{4,13},{5,29},{6,15},{7,31},{8,16},{9,0... | collective-permute-start | bytes 221192 | tf_op jit(solution)/shard_map/ppermute | solution.py:505
  11.9 0.2 copy.17
  12.1 0.1 reshape.11.jac_ref
  12.2 1.6 %collective-permute-start.5 = (bf16[96,128]{1,0:T(8,128)(2,1)S(1)}, bf16[96,128]{1,0:T(8,128)(2,1)S(1)}, u32[]{:S(2)}, u32[]{:S(2)}) collective-permute-start(bf16[96,128]{1,0:T(8,128)(2,1)S(1)} %get-tuple-element.49), channel_id=1, source_target_pairs={{0,1},{2,3},{4,5},{6,7},{1,0},{3,2},{5,4},{7,6},{8,9},{10,11},{12,... | collective-permute-start | bytes 73736 | tf_op jit(solution)/shard_map/ppermute | solution.py:468
  13.8 1.0 %collective-permute-start.7 = (bf16[96,128]{1,0:T(8,128)(2,1)S(1)}, bf16[96,128]{1,0:T(8,128)(2,1)S(1)}, u32[]{:S(2)}, u32[]{:S(2)}) collective-permute-start(bf16[96,128]{1,0:T(8,128)(2,1)S(1)} %get-tuple-element.51), channel_id=1, source_target_pairs={{8,16},{24,0},{16,8},{0,24},{9,17},{25,1},{17,9},{1,25},{10,18},{2... | collective-permute-start | bytes 73736 | tf_op jit(solution)/shard_map/ppermute | solution.py:468
  14.8 0.5 %collective-permute-done.3.refs_1_ = bf16[96,128]{1,0:T(8,128)(2,1)S(1)} collective-permute-done((bf16[96,128]{1,0:T(8,128)(2,1)S(1)}, bf16[96,128]{1,0:T(8,128)(2,1)S(1)}, u32[]{:S(2)}, u32[]{:S(2)}) %collective-permute-start.3) | collective-permute-done | bytes 24608 | tf_op jit(solution)/shard_map/ppermute | solution.py:468
  15.3 0.1 collective-permute-done.2
  15.5 1.5 %collective-permute-start.4 = (bf16[576,128]{1,0:T(8,128)(2,1)S(1)}, bf16[576,128]{1,0:T(8,128)(2,1)S(1)}, u32[]{:S(2)}, u32[]{:S(2)}) collective-permute-start(bf16[576,128]{1,0:T(8,128)(2,1)S(1)} %pad_maximum_fusion), channel_id=1, source_target_pairs={{0,24},{1,8},{2,26},{3,10},{4,28},{5,12},{6,30},{7,14},{8,1},{9,17... | collective-permute-start | bytes 442376 | tf_op jit(solution)/shard_map/ppermute | solution.py:505
  16.9 0.1 copy.18.volume_ref
  17.1 1.9 %local_traces.1 = (bf16[6,96,1024]{2,1,0:T(8,128)(2,1)S(1)}, bf16[4,270,480]{2,1,0:T(8,128)(2,1)S(1)}, bf16[6,96,192]{2,1,0:T(8,128)(2,1)S(1)}) custom-call(bf16[6,4,96,256]{3,2,1,0:T(8,128)(2,1)S(1)} %get-tuple-element.43.trace_ref, s32[6,1024]{1,0:T(8,128)S(1)} %copy-done.3, bf16[4,270,270]{2,1,0:T(8,128)(2,1)S(1)} %copy.18.volume_ref, ...), custom_call_target="tpu_custom_call" | custom-call | flops 2147483648 | bytes 4194304 | tf_op jit(solution)/shard_map/local_traces/pallas_call | solution.py:168
  19.0 0.9 %flow_parts.2.parts1_ref = f32[2,270,1024]{2,1,0:T(8,128)S(1)} custom-call(bf16[270,1024]{1,0:T(8,128)(2,1)S(1)} %copy-done.1, s32[6,1024]{1,0:T(8,128)S(1)} %copy-done.3, bf16[6,4,96,256]{3,2,1,0:T(8,128)(2,1)S(1)} %get-tuple-element.43.trace_ref, bf16[6,96,1024]{2,1,0:T(8,128)(2,1)S(1)} %get-tuple-element.46.local_ref, ...), custom_call_target="tpu_custom_call" | custom-call | flops 2147483648 | bytes 4194304 | tf_op jit(solution)/shard_map/flow_parts/pallas_call | solution.py:230
  20.0 0.1 collective-permute-done.4
  20.2 0.2 collective-permute-start.8
  20.3 1.3 %flow_parts.3.parts0_ref = f32[2,270,1024]{2,1,0:T(8,128)S(1)} custom-call(bf16[270,1024]{1,0:T(8,128)(2,1)S(1)} %copy-done.1, s32[6,1024]{1,0:T(8,128)S(1)} %copy-done.3, bf16[6,4,96,256]{3,2,1,0:T(8,128)(2,1)S(1)} %get-tuple-element.43.trace_ref, bf16[6,96,1024]{2,1,0:T(8,128)(2,1)S(1)} %get-tuple-element.46.local_ref, ...), custom_call_target="tpu_custom_call" | custom-call | flops 2147483648 | bytes 4194304 | tf_op jit(solution)/shard_map/flow_parts/pallas_call | solution.py:230
  21.7 0.1 collective-permute-done.8.far_ref
  21.8 5.4 %wall_and_residual.1 = (bf16[270,1024]{1,0:T(8,128)(2,1)}, f32[3,8,128]{2,1,0:T(8,128)}) custom-call(bf16[1152,128]{1,0:T(8,128)(2,1)S(1)} %constant_dynamic-update-slice_fusion.near_ref, bf16[1152,128]{1,0:T(8,128)(2,1)S(1)} %collective-permute-done.8.far_ref, f32[4,1024]{1,0:T(4,128)S(1)} %copy-done.4, f32[1,1024]{1,0:T(1,128)S(1)} %bitcast.8, ...), custom_call_target="tpu_custom_call" | custom-call | flops 4294967296 | bytes 8388608 | tf_op jit(solution)/shard_map/wall_and_residual/pallas_call | solution.py:443
  (36 shorter events, 0.2 us)
Async XLA Ops:
  1.5 4.2 %collective-permute-start = (bf16[72,128]{1,0:T(8,128)(2,1)S(1)}, bf16[72,128]{1,0:T(8,128)(2,1)S(1)}, u32[]{:S(2)}, u32[]{:S(2)}) collective-permute-start(bf16[72,128]{1,0:T(8,128)(2,1)S(1)} %get-tuple-element.59), channel_id=1, source_target_pairs={{0,10},{1,11},{2,8},{3,9},{4,14},{5,15},{6,12},{7,13},{8,2},{9,3},... | collective-permute-start | bytes 55304 | tf_op jit(solution)/shard_map/ppermute | solution.py:505
  4.1 1.1 %copy-start = (bf16[270,1024]{1,0:T(8,128)(2,1)S(1)}, bf16[270,1024]{1,0:T(8,128)(2,1)}, u32[]{:S(2)}) copy-start(bf16[270,1024]{1,0:T(8,128)(2,1)} %state_ref.5) | copy-start | bytes 1658884
  5.1 6.8 %copy-start.11 = (bf16[6,2,5,5]{0,1,3,2:T(2,128)(2,1)S(1)}, bf16[6,2,5,5]{0,1,3,2:T(2,128)(2,1)}, u32[]{:S(2)}) copy-start(bf16[6,2,5,5]{0,1,3,2:T(2,128)(2,1)} %param.20) | copy-start | bytes 1804
  5.1 11.8 %copy-start.10 = (bf16[4,270,270]{2,0,1:T(4,128)(2,1)S(1)}, bf16[4,270,270]{2,0,1:T(4,128)(2,1)}, u32[]{:S(2)}) copy-start(bf16[4,270,270]{2,0,1:T(4,128)(2,1)} %param.18) | copy-start | bytes 1749604
  5.7 11.3 %copy-start.2 = (bf16[6,270,90]{2,1,0:T(8,128)(2,1)S(1)}, bf16[6,270,90]{2,1,0:T(8,128)(2,1)}, u32[]{:S(2)}) copy-start(bf16[6,270,90]{2,1,0:T(8,128)(2,1)} %lift_ref.1) | copy-start | bytes 874804
  5.7 11.3 %copy-start.3 = (s32[6,1024]{1,0:T(8,128)S(1)}, s32[6,1024]{1,0:T(8,128)}, u32[]{:S(2)}) copy-start(s32[6,1024]{1,0:T(8,128)} %nbr_ref.5) | copy-start | bytes 73732
  5.7 11.3 %copy-start.7 = (bf16[60,1152]{1,0:T(8,128)(2,1)S(1)}, bf16[60,1152]{1,0:T(8,128)(2,1)}, u32[]{:S(2)}) copy-start(bf16[60,1152]{1,0:T(8,128)(2,1)} %constant.19.clone.right_ref) | copy-start | bytes 414724
  5.8 11.3 %copy-start.8 = (f32[96,192]{1,0:T(8,128)S(1)}, f32[96,192]{1,0:T(8,128)}, u32[]{:S(2)}) copy-start(f32[96,192]{1,0:T(8,128)} %constant.20.clone.same_ref) | copy-start | bytes 221188
  5.8 11.3 %copy-start.9 = (bf16[96,5]{1,0:T(8,128)(2,1)S(1)}, bf16[96,5]{1,0:T(8,128)(2,1)}, u32[]{:S(2)}) copy-start(bf16[96,5]{1,0:T(8,128)(2,1)} %constant.18.clone.left_ref) | copy-start | bytes 2884
  5.8 5.3 %collective-permute-start.1 = (bf16[144,128]{1,0:T(8,128)(2,1)S(1)}, bf16[144,128]{1,0:T(8,128)(2,1)S(1)}, u32[]{:S(2)}, u32[]{:S(2)}) collective-permute-start(bf16[144,128]{1,0:T(8,128)(2,1)S(1)} %pad_maximum_fusion.2), channel_id=1, source_target_pairs={{0,12},{1,13},{2,14},{3,15},{4,8},{5,9},{6,10},{7,11},{8,4},{9,5},... | collective-permute-start | bytes 110600 | tf_op jit(solution)/shard_map/ppermute | solution.py:505
  8.8 6.6 %collective-permute-start.3 = (bf16[96,128]{1,0:T(8,128)(2,1)S(1)}, bf16[96,128]{1,0:T(8,128)(2,1)S(1)}, u32[]{:S(2)}, u32[]{:S(2)}) collective-permute-start(bf16[96,128]{1,0:T(8,128)(2,1)S(1)} %get-tuple-element.36), channel_id=1, source_target_pairs={{1,2},{3,4},{5,6},{7,0},{2,1},{4,3},{6,5},{0,7},{9,10},{11,12},{13... | collective-permute-start | bytes 73736 | tf_op jit(solution)/shard_map/ppermute | solution.py:468
  11.1 4.4 %collective-permute-start.2 = (bf16[288,128]{1,0:T(8,128)(2,1)S(1)}, bf16[288,128]{1,0:T(8,128)(2,1)S(1)}, u32[]{:S(2)}, u32[]{:S(2)}) collective-permute-start(bf16[288,128]{1,0:T(8,128)(2,1)S(1)} %pad_maximum_fusion.1), channel_id=1, source_target_pairs={{0,9},{1,25},{2,11},{3,27},{4,13},{5,29},{6,15},{7,31},{8,16},{9,0... | collective-permute-start | bytes 221192 | tf_op jit(solution)/shard_map/ppermute | solution.py:505
  12.2 7.8 %collective-permute-start.5 = (bf16[96,128]{1,0:T(8,128)(2,1)S(1)}, bf16[96,128]{1,0:T(8,128)(2,1)S(1)}, u32[]{:S(2)}, u32[]{:S(2)}) collective-permute-start(bf16[96,128]{1,0:T(8,128)(2,1)S(1)} %get-tuple-element.49), channel_id=1, source_target_pairs={{0,1},{2,3},{4,5},{6,7},{1,0},{3,2},{5,4},{7,6},{8,9},{10,11},{12,... | collective-permute-start | bytes 73736 | tf_op jit(solution)/shard_map/ppermute | solution.py:468
  13.8 6.2 %collective-permute-start.6 = (bf16[96,128]{1,0:T(8,128)(2,1)S(1)}, bf16[96,128]{1,0:T(8,128)(2,1)S(1)}, u32[]{:S(2)}, u32[]{:S(2)}) collective-permute-start(bf16[96,128]{1,0:T(8,128)(2,1)S(1)} %get-tuple-element.50), channel_id=1, source_target_pairs={{0,8},{16,24},{8,0},{24,16},{1,9},{17,25},{9,1},{25,17},{2,10},{18... | collective-permute-start | bytes 73736 | tf_op jit(solution)/shard_map/ppermute | solution.py:468
  13.8 6.2 %collective-permute-start.7 = (bf16[96,128]{1,0:T(8,128)(2,1)S(1)}, bf16[96,128]{1,0:T(8,128)(2,1)S(1)}, u32[]{:S(2)}, u32[]{:S(2)}) collective-permute-start(bf16[96,128]{1,0:T(8,128)(2,1)S(1)} %get-tuple-element.51), channel_id=1, source_target_pairs={{8,16},{24,0},{16,8},{0,24},{9,17},{25,1},{17,9},{1,25},{10,18},{2... | collective-permute-start | bytes 73736 | tf_op jit(solution)/shard_map/ppermute | solution.py:468
  15.5 4.6 %collective-permute-start.4 = (bf16[576,128]{1,0:T(8,128)(2,1)S(1)}, bf16[576,128]{1,0:T(8,128)(2,1)S(1)}, u32[]{:S(2)}, u32[]{:S(2)}) collective-permute-start(bf16[576,128]{1,0:T(8,128)(2,1)S(1)} %pad_maximum_fusion), channel_id=1, source_target_pairs={{0,24},{1,8},{2,26},{3,10},{4,28},{5,12},{6,30},{7,14},{8,1},{9,17... | collective-permute-start | bytes 442376 | tf_op jit(solution)/shard_map/ppermute | solution.py:505
  17.1 1.9 %copy-start.1 = (bf16[270,1024]{1,0:T(8,128)(2,1)S(1)}, bf16[270,1024]{1,0:T(8,128)(2,1)}, u32[]{:S(2)}) copy-start(bf16[270,1024]{1,0:T(8,128)(2,1)} %state_ref.5) | copy-start | bytes 1658884
  20.1 1.7 %copy-start.4 = (f32[4,1024]{1,0:T(4,128)S(1)}, f32[4,1024]{1,0:T(4,128)}, u32[]{:S(2)}) copy-start(f32[4,1024]{1,0:T(4,128)} %base_ref.1) | copy-start | bytes 49156
  20.1 1.7 %copy-start.5 = (f32[1024]{0:T(1024)S(1)}, f32[1024]{0:T(1024)}, u32[]{:S(2)}) copy-start(f32[1024]{0:T(1024)} %param.15) | copy-start | bytes 12292
  20.1 1.7 %copy-start.6 = (s32[1024]{0:T(1024)S(1)}, s32[1024]{0:T(1024)}, u32[]{:S(2)}) copy-start(s32[1024]{0:T(1024)} %param.16) | copy-start | bytes 12292
  20.2 1.6 %collective-permute-start.8 = (bf16[1152,128]{1,0:T(8,128)(2,1)S(1)}, bf16[1152,128]{1,0:T(8,128)(2,1)S(1)}, u32[]{:S(2)}, u32[]{:S(2)}) collective-permute-start(bf16[1152,128]{1,0:T(8,128)(2,1)S(1)} %constant_dynamic-update-slice_fusion.near_ref), channel_id=1, source_target_pairs={{0,8},{1,9},{2,10},{3,11},{4,12},{5,13},{6,14},{7,15},{8,0},{9,1},... | collective-permute-start | bytes 884744 | tf_op jit(solution)/shard_map/ppermute | solution.py:505

commit v7 on v5

--- a/solution.py
+++ b/solution.py
@@ -298,29 +298,29 @@
 
             def some(chunk, carry, c=c):
                 above, value, norm, energy = carry
-                norm, energy = [norm, zero], [energy, zero]
+                norm, energy = [norm, zero, zero, zero], [energy, zero, zero, zero]
                 for k in range(group):
                     tile = chunk * group + k + 1
                     below = renew(c, tile, True)
                     terms = operate(tile - 1, above, value, below)
-                    norm[k % 2] += terms[0]
-                    energy[k % 2] += terms[1]
+                    norm[k % 4] += terms[0]
+                    energy[k % 4] += terms[1]
                     above, value = value, below
-                return above, value, norm[0] + norm[1], energy[0] + energy[1]
+                return above, value, sum(norm[1:], norm[0]), sum(energy[1:], energy[0])
 
             first = value = renew(c, 0, True)
             norm = energy = zero
             if tiles > group:
                 above, value, norm, energy = lax.fori_loop(0, tiles // group - 1, some, (above, value, norm, energy))
-            norm, energy = [norm, zero], [energy, zero]
+            norm, energy = [norm, zero, zero, zero], [energy, zero, zero, zero]
             for tile in range(tiles - group + 1, tiles + 1):
                 if tile < tiles:
                     below = renew(c, tile, True)
                 else:
                     below = jnp.where(sub == TILE - 1, 0.0, pltpu.roll(first, TILE - 1, 0))
                 terms = operate(tile - 1, above, value, below)
-                norm[tile % 2] += terms[0]
-                energy[tile % 2] += terms[1]
+                norm[tile % 4] += terms[0]
+                energy[tile % 4] += terms[1]
                 above, value = value, below
             norms += norm
             energies += energy

time: 27.5 us -> 27.5 us (level)
  no operation moved by 1% of the time
where the time goes in v7:
time: 27.5 us; the launch traced here: 27.2 us
  starting transfers between devices  12.9 us (47%)
  Pallas kernels  10.1 us (37%)
  local copies, waits for them, and re-layouts  1.54 us (6%)
  other arithmetic  0.92 us (3%)
  between operations  0.86 us (3%)
  waiting for transfers between devices  0.85 us (3%)
    ppermute x5, starting transfers between devices, sent(): return lax.ppermute(wall, BOTH, pairs)  7.98 us
    pallas_call x1, Pallas kernels, wall_and_residual(): pl.pallas_call(functools.partial(wall_kernel, masks, kind_bits, rows, own...  5.38 us
    ppermute x4, starting transfers between devices, paired(): return lax.ppermute(x, axis, pairs + [pair[::-1] for pair in pairs])  4.91 us
    pallas_call x2, Pallas kernels, flow_parts(): pl.pallas_call(functools.partial(flow_kernel, directions), in_specs=[VMEM...  2.25 us
    pallas_call x1, Pallas kernels, local_traces(): pl.pallas_call(local_kernel, in_specs=[VMEM] * len(args), out_specs=[VMEM...  1.91 us
    unnamed x27, local copies, waits for them, and re-layouts  1.15 us
    unnamed x1, other arithmetic  0.88 us
    pallas_call x1, Pallas kernels, all_traces(): pl.pallas_call(trace_kernel, in_specs=[VMEM], out_specs=[VMEM] * 5, out_s...  0.58 us
  transfers between devices with their start and end apart: 9, of which 4 were waited for; matrix products, arithmetic and copies ran while one was open for 2% of the time, Pallas kernels for 17%

profile of v7, /device:TPU:0, one launch (start us, length us, event | category | flops | bytes accessed | tf_op | source)
XLA Modules:
  0.0 27.2 jit_solution(12194207332811461700)
XLA Ops:
  0.7 0.9 %constant_dynamic-update-slice_fusion.4 = (bf16[1152,128]{1,0:T(8,128)(2,1)S(1)}, bf16[72,128]{1,0:T(8,128)(2,1)S(1)}) fusion(f32[3,8,128]{2,1,0:T(8,128)} %param.22, f32[3,8,128]{2,1,0:T(8,128)} %param.21, s32[72]{0:T(128)S(1)} %get-tuple-element.60, s32[72]{0:T(128)S(1)} %get-tuple-element.61, pred[72]{0:T(512)(128)(4,1)S(1)} %compare_and_fusion), kind=kLoop, calls=%fused_computation.11 | loop fusion | flops 73727 | bytes 62088
  1.5 2.5 %collective-permute-start = (bf16[72,128]{1,0:T(8,128)(2,1)S(1)}, bf16[72,128]{1,0:T(8,128)(2,1)S(1)}, u32[]{:S(2)}, u32[]{:S(2)}) collective-permute-start(bf16[72,128]{1,0:T(8,128)(2,1)S(1)} %get-tuple-element.59), channel_id=1, source_target_pairs={{0,10},{1,11},{2,8},{3,9},{4,14},{5,15},{6,12},{7,13},{8,2},{9,3},... | collective-permute-start | bytes 55304 | tf_op jit(solution)/shard_map/ppermute | solution.py:505
  4.1 1.1 %copy-done = bf16[270,1024]{1,0:T(8,128)(2,1)S(1)} copy-done((bf16[270,1024]{1,0:T(8,128)(2,1)S(1)}, bf16[270,1024]{1,0:T(8,128)(2,1)}, u32[]{:S(2)}) %copy-start) | copy-done | bytes 552984
  5.1 0.6 %all_traces.1 = (bf16[6,4,96,256]{3,2,1,0:T(8,128)(2,1)S(1)}, bf16[96,128]{1,0:T(8,128)(2,1)S(1)}, bf16[96,128]{1,0:T(8,128)(2,1)S(1)}, bf16[96,128]{1,0:T(8,128)(2,1)S(1)}, bf16[96,128]{1,0:T(8,128)(2,1)S(1)}) custom-call(bf16[270,1024]{1,0:T(8,128)(2,1)S(1)} %copy-done), custom_call_target="tpu_custom_call" | custom-call | flops 1073741824 | bytes 4194304 | tf_op jit(solution)/shard_map/all_traces/pallas_call | solution.py:109
  5.7 0.0 copy-start.7
  5.8 0.0 copy-start.8
  5.8 2.9 %collective-permute-start.1 = (bf16[144,128]{1,0:T(8,128)(2,1)S(1)}, bf16[144,128]{1,0:T(8,128)(2,1)S(1)}, u32[]{:S(2)}, u32[]{:S(2)}) collective-permute-start(bf16[144,128]{1,0:T(8,128)(2,1)S(1)} %pad_maximum_fusion.2), channel_id=1, source_target_pairs={{0,12},{1,13},{2,14},{3,15},{4,8},{5,9},{6,10},{7,11},{8,4},{9,5},... | collective-permute-start | bytes 110600 | tf_op jit(solution)/shard_map/ppermute | solution.py:505
  8.8 2.3 %collective-permute-start.3 = (bf16[96,128]{1,0:T(8,128)(2,1)S(1)}, bf16[96,128]{1,0:T(8,128)(2,1)S(1)}, u32[]{:S(2)}, u32[]{:S(2)}) collective-permute-start(bf16[96,128]{1,0:T(8,128)(2,1)S(1)} %get-tuple-element.36), channel_id=1, source_target_pairs={{1,2},{3,4},{5,6},{7,0},{2,1},{4,3},{6,5},{0,7},{9,10},{11,12},{13... | collective-permute-start | bytes 73736 | tf_op jit(solution)/shard_map/ppermute | solution.py:468
  11.1 0.9 %collective-permute-start.2 = (bf16[288,128]{1,0:T(8,128)(2,1)S(1)}, bf16[288,128]{1,0:T(8,128)(2,1)S(1)}, u32[]{:S(2)}, u32[]{:S(2)}) collective-permute-start(bf16[288,128]{1,0:T(8,128)(2,1)S(1)} %pad_maximum_fusion.1), channel_id=1, source_target_pairs={{0,9},{1,25},{2,11},{3,27},{4,13},{5,29},{6,15},{7,31},{8,16},{9,0... | collective-permute-start | bytes 221192 | tf_op jit(solution)/shard_map/ppermute | solution.py:505
  11.9 0.2 copy.17
  12.1 0.1 reshape.11.jac_ref
  12.2 1.6 %collective-permute-start.5 = (bf16[96,128]{1,0:T(8,128)(2,1)S(1)}, bf16[96,128]{1,0:T(8,128)(2,1)S(1)}, u32[]{:S(2)}, u32[]{:S(2)}) collective-permute-start(bf16[96,128]{1,0:T(8,128)(2,1)S(1)} %get-tuple-element.49), channel_id=1, source_target_pairs={{0,1},{2,3},{4,5},{6,7},{1,0},{3,2},{5,4},{7,6},{8,9},{10,11},{12,... | collective-permute-start | bytes 73736 | tf_op jit(solution)/shard_map/ppermute | solution.py:468
  13.8 1.0 %collective-permute-start.7 = (bf16[96,128]{1,0:T(8,128)(2,1)S(1)}, bf16[96,128]{1,0:T(8,128)(2,1)S(1)}, u32[]{:S(2)}, u32[]{:S(2)}) collective-permute-start(bf16[96,128]{1,0:T(8,128)(2,1)S(1)} %get-tuple-element.51), channel_id=1, source_target_pairs={{8,16},{24,0},{16,8},{0,24},{9,17},{25,1},{17,9},{1,25},{10,18},{2... | collective-permute-start | bytes 73736 | tf_op jit(solution)/shard_map/ppermute | solution.py:468
  14.8 0.5 %collective-permute-done.3.refs_1_ = bf16[96,128]{1,0:T(8,128)(2,1)S(1)} collective-permute-done((bf16[96,128]{1,0:T(8,128)(2,1)S(1)}, bf16[96,128]{1,0:T(8,128)(2,1)S(1)}, u32[]{:S(2)}, u32[]{:S(2)}) %collective-permute-start.3) | collective-permute-done | bytes 24608 | tf_op jit(solution)/shard_map/ppermute | solution.py:468
  15.3 0.1 collective-permute-done.2
  15.5 1.5 %collective-permute-start.4 = (bf16[576,128]{1,0:T(8,128)(2,1)S(1)}, bf16[576,128]{1,0:T(8,128)(2,1)S(1)}, u32[]{:S(2)}, u32[]{:S(2)}) collective-permute-start(bf16[576,128]{1,0:T(8,128)(2,1)S(1)} %pad_maximum_fusion), channel_id=1, source_target_pairs={{0,24},{1,8},{2,26},{3,10},{4,28},{5,12},{6,30},{7,14},{8,1},{9,17... | collective-permute-start | bytes 442376 | tf_op jit(solution)/shard_map/ppermute | solution.py:505
  16.9 0.1 copy.18.volume_ref
  17.1 1.9 %local_traces.1 = (bf16[6,96,1024]{2,1,0:T(8,128)(2,1)S(1)}, bf16[4,270,480]{2,1,0:T(8,128)(2,1)S(1)}, bf16[6,96,192]{2,1,0:T(8,128)(2,1)S(1)}) custom-call(bf16[6,4,96,256]{3,2,1,0:T(8,128)(2,1)S(1)} %get-tuple-element.43.trace_ref, s32[6,1024]{1,0:T(8,128)S(1)} %copy-done.3, bf16[4,270,270]{2,1,0:T(8,128)(2,1)S(1)} %copy.18.volume_ref, ...), custom_call_target="tpu_custom_call" | custom-call | flops 2147483648 | bytes 4194304 | tf_op jit(solution)/shard_map/local_traces/pallas_call | solution.py:168
  19.0 0.9 %flow_parts.2.parts1_ref = f32[2,270,1024]{2,1,0:T(8,128)S(1)} custom-call(bf16[270,1024]{1,0:T(8,128)(2,1)S(1)} %copy-done.1, s32[6,1024]{1,0:T(8,128)S(1)} %copy-done.3, bf16[6,4,96,256]{3,2,1,0:T(8,128)(2,1)S(1)} %get-tuple-element.43.trace_ref, bf16[6,96,1024]{2,1,0:T(8,128)(2,1)S(1)} %get-tuple-element.46.local_ref, ...), custom_call_target="tpu_custom_call" | custom-call | flops 2147483648 | bytes 4194304 | tf_op jit(solution)/shard_map/flow_parts/pallas_call | solution.py:230
  20.0 0.1 collective-permute-done.4
  20.2 0.2 collective-permute-start.8
  20.3 1.3 %flow_parts.3.parts0_ref = f32[2,270,1024]{2,1,0:T(8,128)S(1)} custom-call(bf16[270,1024]{1,0:T(8,128)(2,1)S(1)} %copy-done.1, s32[6,1024]{1,0:T(8,128)S(1)} %copy-done.3, bf16[6,4,96,256]{3,2,1,0:T(8,128)(2,1)S(1)} %get-tuple-element.43.trace_ref, bf16[6,96,1024]{2,1,0:T(8,128)(2,1)S(1)} %get-tuple-element.46.local_ref, ...), custom_call_target="tpu_custom_call" | custom-call | flops 2147483648 | bytes 4194304 | tf_op jit(solution)/shard_map/flow_parts/pallas_call | solution.py:230
  21.7 0.1 collective-permute-done.8.far_ref
  21.8 5.4 %wall_and_residual.1 = (bf16[270,1024]{1,0:T(8,128)(2,1)}, f32[3,8,128]{2,1,0:T(8,128)}) custom-call(bf16[1152,128]{1,0:T(8,128)(2,1)S(1)} %constant_dynamic-update-slice_fusion.near_ref, bf16[1152,128]{1,0:T(8,128)(2,1)S(1)} %collective-permute-done.8.far_ref, f32[4,1024]{1,0:T(4,128)S(1)} %copy-done.4, f32[1,1024]{1,0:T(1,128)S(1)} %bitcast.8, ...), custom_call_target="tpu_custom_call" | custom-call | flops 4294967296 | bytes 8388608 | tf_op jit(solution)/shard_map/wall_and_residual/pallas_call | solution.py:443
  (36 shorter events, 0.2 us)
Async XLA Ops:
  1.5 4.2 %collective-permute-start = (bf16[72,128]{1,0:T(8,128)(2,1)S(1)}, bf16[72,128]{1,0:T(8,128)(2,1)S(1)}, u32[]{:S(2)}, u32[]{:S(2)}) collective-permute-start(bf16[72,128]{1,0:T(8,128)(2,1)S(1)} %get-tuple-element.59), channel_id=1, source_target_pairs={{0,10},{1,11},{2,8},{3,9},{4,14},{5,15},{6,12},{7,13},{8,2},{9,3},... | collective-permute-start | bytes 55304 | tf_op jit(solution)/shard_map/ppermute | solution.py:505
  4.1 1.1 %copy-start = (bf16[270,1024]{1,0:T(8,128)(2,1)S(1)}, bf16[270,1024]{1,0:T(8,128)(2,1)}, u32[]{:S(2)}) copy-start(bf16[270,1024]{1,0:T(8,128)(2,1)} %state_ref.5) | copy-start | bytes 1658884
  5.1 6.8 %copy-start.11 = (bf16[6,2,5,5]{0,1,3,2:T(2,128)(2,1)S(1)}, bf16[6,2,5,5]{0,1,3,2:T(2,128)(2,1)}, u32[]{:S(2)}) copy-start(bf16[6,2,5,5]{0,1,3,2:T(2,128)(2,1)} %param.20) | copy-start | bytes 1804
  5.1 11.8 %copy-start.10 = (bf16[4,270,270]{2,0,1:T(4,128)(2,1)S(1)}, bf16[4,270,270]{2,0,1:T(4,128)(2,1)}, u32[]{:S(2)}) copy-start(bf16[4,270,270]{2,0,1:T(4,128)(2,1)} %param.18) | copy-start | bytes 1749604
  5.7 11.3 %copy-start.2 = (bf16[6,270,90]{2,1,0:T(8,128)(2,1)S(1)}, bf16[6,270,90]{2,1,0:T(8,128)(2,1)}, u32[]{:S(2)}) copy-start(bf16[6,270,90]{2,1,0:T(8,128)(2,1)} %lift_ref.1) | copy-start | bytes 874804
  5.7 11.3 %copy-start.3 = (s32[6,1024]{1,0:T(8,128)S(1)}, s32[6,1024]{1,0:T(8,128)}, u32[]{:S(2)}) copy-start(s32[6,1024]{1,0:T(8,128)} %nbr_ref.5) | copy-start | bytes 73732
  5.7 11.3 %copy-start.7 = (bf16[60,1152]{1,0:T(8,128)(2,1)S(1)}, bf16[60,1152]{1,0:T(8,128)(2,1)}, u32[]{:S(2)}) copy-start(bf16[60,1152]{1,0:T(8,128)(2,1)} %constant.19.clone.right_ref) | copy-start | bytes 414724
  5.8 11.3 %copy-start.8 = (f32[96,192]{1,0:T(8,128)S(1)}, f32[96,192]{1,0:T(8,128)}, u32[]{:S(2)}) copy-start(f32[96,192]{1,0:T(8,128)} %constant.20.clone.same_ref) | copy-start | bytes 221188
  5.8 11.3 %copy-start.9 = (bf16[96,5]{1,0:T(8,128)(2,1)S(1)}, bf16[96,5]{1,0:T(8,128)(2,1)}, u32[]{:S(2)}) copy-start(bf16[96,5]{1,0:T(8,128)(2,1)} %constant.18.clone.left_ref) | copy-start | bytes 2884
  5.8 5.3 %collective-permute-start.1 = (bf16[144,128]{1,0:T(8,128)(2,1)S(1)}, bf16[144,128]{1,0:T(8,128)(2,1)S(1)}, u32[]{:S(2)}, u32[]{:S(2)}) collective-permute-start(bf16[144,128]{1,0:T(8,128)(2,1)S(1)} %pad_maximum_fusion.2), channel_id=1, source_target_pairs={{0,12},{1,13},{2,14},{3,15},{4,8},{5,9},{6,10},{7,11},{8,4},{9,5},... | collective-permute-start | bytes 110600 | tf_op jit(solution)/shard_map/ppermute | solution.py:505
  8.8 6.6 %collective-permute-start.3 = (bf16[96,128]{1,0:T(8,128)(2,1)S(1)}, bf16[96,128]{1,0:T(8,128)(2,1)S(1)}, u32[]{:S(2)}, u32[]{:S(2)}) collective-permute-start(bf16[96,128]{1,0:T(8,128)(2,1)S(1)} %get-tuple-element.36), channel_id=1, source_target_pairs={{1,2},{3,4},{5,6},{7,0},{2,1},{4,3},{6,5},{0,7},{9,10},{11,12},{13... | collective-permute-start | bytes 73736 | tf_op jit(solution)/shard_map/ppermute | solution.py:468
  11.1 4.4 %collective-permute-start.2 = (bf16[288,128]{1,0:T(8,128)(2,1)S(1)}, bf16[288,128]{1,0:T(8,128)(2,1)S(1)}, u32[]{:S(2)}, u32[]{:S(2)}) collective-permute-start(bf16[288,128]{1,0:T(8,128)(2,1)S(1)} %pad_maximum_fusion.1), channel_id=1, source_target_pairs={{0,9},{1,25},{2,11},{3,27},{4,13},{5,29},{6,15},{7,31},{8,16},{9,0... | collective-permute-start | bytes 221192 | tf_op jit(solution)/shard_map/ppermute | solution.py:505
  12.2 7.8 %collective-permute-start.5 = (bf16[96,128]{1,0:T(8,128)(2,1)S(1)}, bf16[96,128]{1,0:T(8,128)(2,1)S(1)}, u32[]{:S(2)}, u32[]{:S(2)}) collective-permute-start(bf16[96,128]{1,0:T(8,128)(2,1)S(1)} %get-tuple-element.49), channel_id=1, source_target_pairs={{0,1},{2,3},{4,5},{6,7},{1,0},{3,2},{5,4},{7,6},{8,9},{10,11},{12,... | collective-permute-start | bytes 73736 | tf_op jit(solution)/shard_map/ppermute | solution.py:468
  13.8 6.2 %collective-permute-start.6 = (bf16[96,128]{1,0:T(8,128)(2,1)S(1)}, bf16[96,128]{1,0:T(8,128)(2,1)S(1)}, u32[]{:S(2)}, u32[]{:S(2)}) collective-permute-start(bf16[96,128]{1,0:T(8,128)(2,1)S(1)} %get-tuple-element.50), channel_id=1, source_target_pairs={{0,8},{16,24},{8,0},{24,16},{1,9},{17,25},{9,1},{25,17},{2,10},{18... | collective-permute-start | bytes 73736 | tf_op jit(solution)/shard_map/ppermute | solution.py:468
  13.8 6.2 %collective-permute-start.7 = (bf16[96,128]{1,0:T(8,128)(2,1)S(1)}, bf16[96,128]{1,0:T(8,128)(2,1)S(1)}, u32[]{:S(2)}, u32[]{:S(2)}) collective-permute-start(bf16[96,128]{1,0:T(8,128)(2,1)S(1)} %get-tuple-element.51), channel_id=1, source_target_pairs={{8,16},{24,0},{16,8},{0,24},{9,17},{25,1},{17,9},{1,25},{10,18},{2... | collective-permute-start | bytes 73736 | tf_op jit(solution)/shard_map/ppermute | solution.py:468
  15.5 4.6 %collective-permute-start.4 = (bf16[576,128]{1,0:T(8,128)(2,1)S(1)}, bf16[576,128]{1,0:T(8,128)(2,1)S(1)}, u32[]{:S(2)}, u32[]{:S(2)}) collective-permute-start(bf16[576,128]{1,0:T(8,128)(2,1)S(1)} %pad_maximum_fusion), channel_id=1, source_target_pairs={{0,24},{1,8},{2,26},{3,10},{4,28},{5,12},{6,30},{7,14},{8,1},{9,17... | collective-permute-start | bytes 442376 | tf_op jit(solution)/shard_map/ppermute | solution.py:505
  17.1 1.9 %copy-start.1 = (bf16[270,1024]{1,0:T(8,128)(2,1)S(1)}, bf16[270,1024]{1,0:T(8,128)(2,1)}, u32[]{:S(2)}) copy-start(bf16[270,1024]{1,0:T(8,128)(2,1)} %state_ref.5) | copy-start | bytes 1658884
  20.1 1.7 %copy-start.4 = (f32[4,1024]{1,0:T(4,128)S(1)}, f32[4,1024]{1,0:T(4,128)}, u32[]{:S(2)}) copy-start(f32[4,1024]{1,0:T(4,128)} %base_ref.1) | copy-start | bytes 49156
  20.1 1.7 %copy-start.5 = (f32[1024]{0:T(1024)S(1)}, f32[1024]{0:T(1024)}, u32[]{:S(2)}) copy-start(f32[1024]{0:T(1024)} %param.15) | copy-start | bytes 12292
  20.1 1.7 %copy-start.6 = (s32[1024]{0:T(1024)S(1)}, s32[1024]{0:T(1024)}, u32[]{:S(2)}) copy-start(s32[1024]{0:T(1024)} %param.16) | copy-start | bytes 12292
  20.2 1.6 %collective-permute-start.8 = (bf16[1152,128]{1,0:T(8,128)(2,1)S(1)}, bf16[1152,128]{1,0:T(8,128)(2,1)S(1)}, u32[]{:S(2)}, u32[]{:S(2)}) collective-permute-start(bf16[1152,128]{1,0:T(8,128)(2,1)S(1)} %constant_dynamic-update-slice_fusion.near_ref), channel_id=1, source_target_pairs={{0,8},{1,9},{2,10},{3,11},{4,12},{5,13},{6,14},{7,15},{8,0},{9,1},... | collective-permute-start | bytes 884744 | tf_op jit(solution)/shard_map/ppermute | solution.py:505
